TPU v7x, 32 devices: a whole 2x2x4 slice. The times are simulated.
32 devices in a mesh: image: 4 (over y, x), token: 8 (over z, core).
Axes of the slice: x: 2, y: 2, z: 4, core: 2. Of those that a mesh axis runs over, the one named last changes fastest.
Arguments:
- hidden: bfloat16 [2, 4, 1024, 3072], P(None, 'image', 'token'), may hold values from -6 to 6
- key_cache: bfloat16 [2, 4, 1024, 1536], P(None, 'image', 'token')
- value_cache: bfloat16 [2, 4, 1024, 1536], P(None, 'image', 'token'), may hold values from -6 to 6
- cached_out: bfloat16 [4, 1024, 1536], P('image', 'token'), may hold values from -6 to 6
- w_query: bfloat16 [3072, 1536], P('image'), may hold values from -0.109375 to 0.109375
- guide: float32 [4], P('image'), may hold values from 1.5 to 4
- masked_tiles: int32 [4, 2], P('image'), may hold values from 0 to 7, as said below
- mask_count: int32 [4], P('image'), may hold values from 1 to 2, as said below
Outputs:
- edited: bfloat16 [4, 1024, 1536], P('image', 'token')
Inputs may be any that keep to these rules, and one draw needn't show every extreme that they name: `masked_tiles`: in each image the first mask_count entries are distinct tiles; later entries are tiles too. `mask_count`: some image of every draw has exactly 2 masked tiles.
All inputs are finite; a program needn't handle non-finite values.
Results may differ from a plain program's by a relative error of at most 0.011.
The roundings to bfloat16 on the way count: a program that leaves them out, or rounds other values in their place, can miss the bound.
Values may be sent and summed in bfloat16 or wider, within the bound.
No kernel may reach another device: no remote copies, remote signals or barrier semaphores. Data moves between devices by JAX's collectives and lax.ppermute only.
A program may use at most 128 MiB of HBM per device.

v0:
```python
import math

import jax
import jax.numpy as jnp
from jax import lax
from jax.sharding import PartitionSpec as P

HD = 128
TILE = 128


def spread(array, axis, root):
    mine = lax.axis_index(axis) == root
    return lax.psum(jnp.where(mine, array, jnp.zeros_like(array)), axis)


def body(hidden, key_cache, value_cache, cached_out, w_query, guide, masked_tiles, mask_count):
    position = lax.axis_index("token")
    images = hidden.shape[1]
    tok_dev = hidden.shape[2]
    model_width = hidden.shape[3]
    inner_width = key_cache.shape[3]
    head_count = inner_width // HD
    per_dev = tok_dev // TILE
    slot_most = masked_tiles.shape[1]
    slot_total = images * slot_most
    scale_for_scores = 1.0 / math.sqrt(HD)
    flattened = hidden.reshape(2 * images * tok_dev, model_width)
    query_sum = jnp.dot(
        flattened,
        lax.all_gather(w_query, "image", axis=0, tiled=True),
        preferred_element_type=jnp.float32,
    )
    own_query = query_sum.astype(jnp.bfloat16).reshape(2, images, per_dev, TILE, inner_width)
    slot_tile = masked_tiles.reshape(slot_total)
    slot_image = jnp.arange(slot_total, dtype=jnp.int32) // slot_most
    slot_owner = slot_tile // per_dev
    slot_local = slot_tile % per_dev

    def send_one(slot_index, gathered):
        picked = own_query[:, slot_image[slot_index], slot_local[slot_index]]
        arrived = spread(picked, "token", slot_owner[slot_index])
        return lax.dynamic_update_index_in_dim(gathered, arrived, slot_index, 1)

    queries = lax.fori_loop(
        0, slot_total, send_one, jnp.zeros((2, slot_total, TILE, inner_width), jnp.bfloat16)
    )
    query_heads = queries.reshape(2, images, slot_most, TILE, head_count, HD)
    key_block = key_cache.reshape(2, images, tok_dev, head_count, HD)
    value_block = value_cache.reshape(2, images, tok_dev, head_count, HD)
    logit_scores = (
        jnp.einsum(
            "bimrhd,bikhd->bimhrk", query_heads, key_block, preferred_element_type=jnp.float32
        )
        * scale_for_scores
    )
    local_max = jnp.max(logit_scores, axis=-1)
    row_max = lax.pmax(local_max.astype(jnp.bfloat16), "token").astype(local_max.dtype)
    exp_scores = jnp.exp(logit_scores - row_max[..., None])
    row_total = lax.psum(jnp.sum(exp_scores, axis=-1).astype(jnp.bfloat16), "token").astype(
        jnp.float32
    )
    softmax_weights = (exp_scores / row_total[..., None]).astype(jnp.bfloat16)
    attended = jnp.einsum(
        "bimhrk,bikhd->bimrhd", softmax_weights, value_block, preferred_element_type=jnp.float32
    )
    attended = attended.reshape(2, images, slot_most, TILE, inner_width)
    guide_scale = guide[:, None, None, None]
    guided_part = attended[1] + guide_scale * (attended[0] - attended[1])
    guided_part = guided_part.reshape(slot_total * TILE, inner_width)
    summed_rows = lax.psum(guided_part, "token")
    result = summed_rows.astype(jnp.bfloat16)
    result = result.reshape(images, slot_most, TILE, inner_width)
    tile_ids = position * per_dev + jnp.arange(per_dev, dtype=jnp.int32)
    in_use = jnp.arange(slot_most, dtype=jnp.int32)[None, :] < mask_count[:, None]
    matched = (masked_tiles[:, None, :] == tile_ids[None, :, None]) & in_use[:, None, :]
    chosen = jnp.einsum(
        "iuj,ijrc->iurc", matched.astype(jnp.bfloat16), result, preferred_element_type=jnp.float32
    )
    pasted_mask = jnp.any(matched, axis=-1)[:, :, None, None]
    previous = cached_out.reshape(images, per_dev, TILE, inner_width)
    edited = jnp.where(pasted_mask, chosen.astype(jnp.bfloat16), previous)
    return edited.reshape(images, tok_dev, inner_width)


def solution(mesh):
    return jax.shard_map(
        body,
        mesh=mesh,
        in_specs=(
            P(None, "image", "token", None),
            P(None, "image", "token", None),
            P(None, "image", "token", None),
            P("image", "token", None),
            P("image", None),
            P("image"),
            P("image", None),
            P("image"),
        ),
        out_specs=P("image", "token", None),
        check_vma=False,
    )
```

profile of v0, /device:TPU:0, one launch (start us, length us, event | category | flops | bytes accessed | tf_op | source)
XLA Modules:
  0.0 380.4 jit_solution(3122968004342945191)
XLA Ops:
  6.5 0.0 copy-start
  6.5 0.0 copy-start.1
  6.5 0.0 copy-start.2
  6.5 0.0 all-gather.2.cloned.1.call-start
  6.5 0.7 all-gather.2.cloned.1.call-update
  8.6 0.0 copy-done.1
  8.6 0.0 copy-start.5
  8.6 1.2 copy.14
  9.8 0.0 copy-done.2
  9.8 1.2 copy.17
  10.9 0.0 copy-done.5
  10.9 0.7 fusion.14
  11.6 96.6 %all-gather.2.cloned.1.call-done = bf16[3072,1536]{1,0:T(8,128)(2,1)} async-done(((bf16[768,1536]{1,0:T(8,128)(2,1)}), bf16[3072,1536]{1,0:T(8,128)(2,1)}) %all-gather.2.cloned.1.call-update) | async-done | bytes 9437200 | tf_op jit(solution)/shard_map/all_gather | solution.py:31
  108.3 0.0 copy-done
  108.3 6.3 %convolution_convert_fusion = bf16[256,1536]{1,0:T(8,128)(2,1)S(1)} fusion(bf16[256,3072]{1,0:T(8,128)(2,1)S(1)} %bitcast.89, bf16[3072,1536]{1,0:T(8,128)(2,1)} %all-gather.2.cloned.1.call-done), kind=kOutput, calls=%fused_computation.6 | convolution fusion | flops 2416312320 | bytes 11796480 | tf_op jit(solution)/shard_map/dot_general | solution.py:29
  114.6 125.3 %while.13 = (s32[]{:T(128)}, bf16[2,2,128,1536]{2,3,1,0:T(8,128)(2,1)}, s32[2]{0:T(128)S(1)}, bf16[2,1,1,128,1536]{4,3,0,2,1:T(8,128)(2,1)S(1)}, s32[]{:T(128)}, /*index=5*/u32[]{:T(128)}) while((s32[]{:T(128)}, bf16[2,2,128,1536]{2,3,1,0:T(8,128)(2,1)}, s32[2]{0:T(128)S(1)}, bf16[2,1,1,128,1536]{4,3,0,2,1:T(8,128)(2,1)S(1)}, s32[]{:T(128)}, ...), condition=%wide.region_3.4_spmd, body=%wide.region_1.3_spmd.sunk | while | flops 786437 | bytes 9437347 | solution.py:45
  114.6 0.0 all-reduce.3.cloned.1.call-start
  114.6 0.6 dynamic_slice.17
  115.9 1.0 select_bitcast_fusion.2
  116.8 0.0 all-reduce.3.cloned.1.call-update
  116.8 58.4 %all-reduce.3.cloned.1.call-done = bf16[2,1,128,1536]{3,2,1,0:T(8,128)(2,1)} async-done(((bf16[2,1,128,1536]{3,2,1,0:T(8,128)(2,1)}), bf16[2,1,128,1536]{3,2,1,0:T(8,128)(2,1)}) %all-reduce.3.cloned.1.call-update) | async-done | bytes 786448 | tf_op jit(solution)/shard_map/while/body/eval_jaxpr/psum | solution.py:14
  175.2 1.5 copy.49
  176.7 0.9 constant_dynamic-update-slice_fusion.2
  177.7 0.0 all-reduce.3.cloned.1.call-start
  177.7 0.6 dynamic_slice.17
  178.9 1.0 select_bitcast_fusion.2
  179.9 0.0 all-reduce.3.cloned.1.call-update
  179.9 57.5 %all-reduce.3.cloned.1.call-done = bf16[2,1,128,1536]{3,2,1,0:T(8,128)(2,1)} async-done(((bf16[2,1,128,1536]{3,2,1,0:T(8,128)(2,1)}), bf16[2,1,128,1536]{3,2,1,0:T(8,128)(2,1)}) %all-reduce.3.cloned.1.call-update) | async-done | bytes 786448 | tf_op jit(solution)/shard_map/while/body/eval_jaxpr/psum | solution.py:14
  237.4 1.5 copy.49
  238.9 1.0 constant_dynamic-update-slice_fusion.2
  239.9 3.9 %bitcast_reduce_fusion = (bf16[2,2,12,128]{3,1,2,0:T(2,128)(2,1)S(1)}, f32[2,12,2,128,128]{3,4,2,1,0:T(8,128)}) fusion(bf16[2,128,12,128,1]{1,3,4,2,0:T(8,128)(2,1)} %bitcast.93, bf16[2,2,128,12,128]{2,4,3,1,0:T(8,128)(2,1)} %bitcast.94), kind=kOutput, calls=%fused_computation.3 | convolution fusion | flops 202893312 | bytes 5517312 | tf_op jit(solution)/shard_map/bimrhd,bikhd->bimhrk/dot_general | solution.py:52
  243.8 25.9 %pmax.7 = bf16[2,2,12,128]{3,1,2,0:T(2,128)(2,1)S(1)} all-reduce(bf16[2,2,12,128]{3,1,2,0:T(2,128)(2,1)S(1)} %get-tuple-element.117), channel_id=1, replica_groups=mesh['image'=4,'token'=8] {'token'}, use_global_device_ids=true, to_apply=%region_5.6 | all-reduce | flops 6144 | bytes 24576 | tf_op jit(solution)/shard_map/pmax | solution.py:58
  269.7 0.0 copy-start.3
  269.7 2.6 fusion.1
  272.4 25.9 %psum.25 = bf16[2,2,12,128]{3,1,2,0:T(2,128)(2,1)S(1)} all-reduce(bf16[2,2,12,128]{3,1,2,0:T(2,128)(2,1)S(1)} %fusion.1), channel_id=1, replica_groups=mesh['image'=4,'token'=8] {'token'}, use_global_device_ids=true, to_apply=%region_7.8 | all-reduce | flops 6144 | bytes 24576 | tf_op jit(solution)/shard_map/psum | solution.py:60
  298.3 0.0 copy-done.3
  298.3 2.8 convolution_bitcast_fusion
  301.1 2.0 fusion.15
  303.1 2.6 copy.20
  305.7 3.7 copy.21
  309.4 2.8 fusion.3
  312.1 58.2 %all-reduce.4 = bf16[256,1536]{0,1:T(8,128)(2,1)S(1)} all-reduce(f32[256,1536]{0,1:T(8,128)} %fusion.3), channel_id=1, replica_groups=mesh['image'=4,'token'=8] {'token'}, use_global_device_ids=true, to_apply=%region_8.9 | all-reduce | flops 393216 | bytes 2359296 | tf_op jit(solution)/shard_map/psum | solution.py:71
  370.3 0.2 reshape.138
  370.5 0.9 copy.26
  371.4 0.0 copy-start.4
  371.4 1.0 fusion.11
  372.4 0.0 copy-done.4
  372.4 1.5 fusion.10
  (3 shorter events, 0.0 us)
Async XLA Ops:
  6.5 101.7 %copy-start = (bf16[2,1,128,3072]{3,2,1,0:T(8,128)(2,1)S(1)}, bf16[2,1,128,3072]{3,2,1,0:T(8,128)(2,1)}, u32[]{:S(2)}) copy-start(bf16[2,1,128,3072]{3,2,1,0:T(8,128)(2,1)} %param.10) | copy-start | bytes 4718596
  6.5 2.0 copy-start.1
  6.5 3.2 copy-start.2
  6.5 101.7 %all-gather.2.cloned.1.call-start = ((), (), s32[]{:S(2)}) async-start(), calls=%async_computation | async-start | bytes 11796480 | tf_op jit(solution)/shard_map/all_gather | solution.py:31
  8.6 2.4 copy-start.5
  114.6 60.7 %all-reduce.3.cloned.1.call-start = ((), (), s32[]{:S(2)}) async-start(), calls=%async_computation.1 | async-start | bytes 1572864 | tf_op jit(solution)/shard_map/while/body/eval_jaxpr/psum | solution.py:14
  177.7 59.7 %all-reduce.3.cloned.1.call-start = ((), (), s32[]{:S(2)}) async-start(), calls=%async_computation.1 | async-start | bytes 1572864 | tf_op jit(solution)/shard_map/while/body/eval_jaxpr/psum | solution.py:14
  269.7 28.6 %copy-start.3 = (bf16[2,1,128,1536]{2,3,0,1:T(8,128)(2,1)S(1)}, bf16[2,1,128,1536]{2,3,0,1:T(8,128)(2,1)}, u32[]{:S(2)}) copy-start(bf16[2,1,128,1536]{2,3,0,1:T(8,128)(2,1)} %copy.17) | copy-start | bytes 2359300
  371.4 1.0 copy-start.4
Sparse Core Ops, SparseCore 0:
  9.2 99.0 all-gather.1
  117.8 57.4 all-reduce.2
  180.8 56.4 all-reduce.2
where the time goes:
time: 381 us; the launch traced here: 380 us
  waiting for transfers between devices  213 us (56%)
  blocking collectives  110 us (29%)
  local copies, waits for them, and re-layouts  17.9 us (5%)
  between operations  14.5 us (4%)
  matrix products  13.9 us (4%)
  other arithmetic  9.51 us (2%)
    psum x2, waiting for transfers between devices, spread(): return lax.psum(jnp.where(mine, array, jnp.zeros_like(array)), axis)  116 us
    all_gather x1, waiting for transfers between devices, body(): lax.all_gather(w_query, 'image', axis=0, tiled=True)  96.6 us
    psum x1, blocking collectives, body(): summed_rows = lax.psum(guided_part, 'token')  58.2 us
    pmax x1, blocking collectives, body(): lax.pmax(local_max.astype(jnp.bfloat16), 'token').astype(local_max.dtype)  25.9 us
    psum x1, blocking collectives, body(): lax.psum(jnp.sum(exp_scores, axis=-1).astype(jnp.bfloat16), 'token')  25.9 us
    slice x3, local copies, waits for them, and re-layouts, body(): guided_part = attended[1] + guide_scale * (attended[0] - attended[1])  8.3 us
  transfers between devices with their start and end apart: 3, of which 3 were waited for; matrix products, arithmetic and copies ran while one was open for 1% of the time, Pallas kernels for 0%

commit v1 on v0

v1 whole, which is shorter than its diff:
```python
import math

import jax
import jax.numpy as jnp
from jax import lax
from jax.experimental import pallas as pl
from jax.experimental.pallas import tpu as pltpu
from jax.sharding import PartitionSpec as P

HD = 128
TILE = 128
GROUPS = 4
BF = jnp.bfloat16
F32 = jnp.float32
VMEM_LIMIT = 48 * 1024 * 1024

SMEM_SPEC = pl.BlockSpec(memory_space=pltpu.SMEM)
VMEM_SPEC = pl.BlockSpec(memory_space=pltpu.VMEM)


def call(kernel, out_shape, scalars, arrays, flops, moved, scratch=(), exps=0):
    many = isinstance(out_shape, (list, tuple))
    return pl.pallas_call(
        kernel,
        out_shape=out_shape,
        in_specs=[SMEM_SPEC] + [VMEM_SPEC] * len(arrays),
        out_specs=[VMEM_SPEC] * len(out_shape) if many else VMEM_SPEC,
        scratch_shapes=list(scratch),
        compiler_params=pltpu.CompilerParams(vmem_limit_bytes=VMEM_LIMIT),
        cost_estimate=pl.CostEstimate(flops=flops, bytes_accessed=moved, transcendentals=exps),
    )(scalars, *arrays)


def pack_weights(core, w_query, parts):
    rows, columns = w_query.shape
    half = columns // 2
    width = 2 * HD

    def kernel(core_ref, w_ref, *out_refs):
        for k, out in enumerate(out_refs):
            for hi in range(2):
                at = pl.multiple_of(core_ref[0] * half + (hi * parts + k) * HD, HD)
                out[:, hi * HD : (hi + 1) * HD] = w_ref[:, pl.ds(at, HD)]

    return call(
        kernel,
        [jax.ShapeDtypeStruct((rows, width), BF)] * parts,
        core,
        [w_query],
        0,
        2 * rows * columns * 3,
    )


def pack_keys(z_pos, key_block, value_block):
    branches, tokens, columns = key_block.shape
    width = columns // GROUPS

    def kernel(z_ref, k_ref, v_ref, *out_refs):
        for m, out in enumerate(out_refs):
            at = pl.multiple_of((z_ref[0] ^ m) * width, HD)
            out[0] = k_ref[:, :, pl.ds(at, width)]
            out[1] = v_ref[:, :, pl.ds(at, width)]

    return call(
        kernel,
        [jax.ShapeDtypeStruct((2, branches, tokens, width), BF)] * GROUPS,
        z_pos,
        [key_block, value_block],
        0,
        2 * 4 * branches * tokens * columns,
    )


def project(scalars, own, other, pieces):
    branches, rows, depth = own.shape
    chunk = pieces[0].shape[0]
    width = pieces[0].shape[1]

    def kernel(s_ref, own_ref, other_ref, *refs):
        w_refs, out_refs, held = refs[:5], refs[5:9], refs[9]
        image = s_ref[0]
        for slot in range(2):

            def part(h_ref):
                total = jnp.zeros((branches * rows, width), F32)
                for m, first, w_ref in ((0, 0, w_refs[0]), (1, 0, w_refs[1]), (2, 0, w_refs[2]), (3, 0, w_refs[3]), (3, 1, w_refs[4])):
                    size = w_ref.shape[0]
                    at = pl.multiple_of((image ^ m) * chunk + first * (chunk // 2), HD)
                    x = h_ref[:, :, pl.ds(at, size)].reshape(branches * rows, size)
                    total = total + jnp.dot(x, w_ref[...], preferred_element_type=F32)
                total = total.astype(BF)
                for hi in range(2):
                    held[hi * 2 + slot] = total[:, hi * HD : (hi + 1) * HD]

            @pl.when(s_ref[2 + slot] == 1)
            def _():
                part(own_ref)

            @pl.when(s_ref[2 + slot] != 1)
            def _():
                part(other_ref)

        for r, out in enumerate(out_refs):
            out[...] = held[(s_ref[1] + r) % 4]

    return call(
        kernel,
        [jax.ShapeDtypeStruct((branches * rows, HD), BF)] * 4,
        scalars,
        [own, other, *pieces],
        2 * 2 * branches * rows * depth * width,
        2 * (2 * branches * rows * depth + depth * width),
        [pltpu.VMEM((4, branches * rows, HD), BF)],
    )


def attend(scalars, guide, queries, caches, part):
    rows = queries[0].shape[0] // 2
    scale = 1.0 / math.sqrt(HD)
    count = len(queries)
    here = slice(part * HD, (part + 1) * HD)
    keys_all = sum(c.shape[0] * c.shape[3] for c in caches)

    def kernel(s_ref, g_ref, *refs):
        q_refs, c_refs, out, held = refs[:count], refs[count:-2], refs[-2], refs[-1]
        for r in range(count):

            @pl.when(s_ref[0] == r)
            def _():
                held[...] = q_refs[r][...]

        attended = []
        for b in range(2):
            q = held[b * rows : (b + 1) * rows]
            scores = []
            for c_ref in c_refs:
                for n in range(c_ref.shape[0]):
                    scores.append(
                        lax.dot_general(
                            q, c_ref[n, 0, b, :, here], (((1,), (1,)), ((), ())), preferred_element_type=F32
                        )
                        * scale
                    )
            top = jnp.max(scores[0], axis=-1, keepdims=True)
            for s in scores[1:]:
                top = jnp.maximum(top, jnp.max(s, axis=-1, keepdims=True))
            exps = [jnp.exp(s - top) for s in scores]
            total = jnp.sum(exps[0], axis=-1, keepdims=True)
            for e in exps[1:]:
                total = total + jnp.sum(e, axis=-1, keepdims=True)
            over = 1.0 / total
            result = jnp.zeros((rows, HD), F32)
            at = 0
            for c_ref in c_refs:
                for n in range(c_ref.shape[0]):
                    w = (exps[at] * over).astype(BF)
                    result = result + jnp.dot(w, c_ref[n, 1, b, :, here], preferred_element_type=F32)
                    at += 1
            attended.append(result)
        guided = attended[1] + g_ref[0] * (attended[0] - attended[1])
        out[...] = guided.astype(BF)

    def smem_kernel(s_ref, g_ref, *refs):
        kernel(s_ref, g_ref, *refs)

    return pl.pallas_call(
        smem_kernel,
        out_shape=jax.ShapeDtypeStruct((rows, HD), BF),
        in_specs=[SMEM_SPEC, SMEM_SPEC] + [VMEM_SPEC] * (count + len(caches)),
        out_specs=VMEM_SPEC,
        scratch_shapes=[pltpu.VMEM((2 * rows, HD), BF)],
        compiler_params=pltpu.CompilerParams(vmem_limit_bytes=VMEM_LIMIT),
        cost_estimate=pl.CostEstimate(
            flops=8 * rows * keys_all * HD,
            bytes_accessed=keys_all * 3 * HD * 8,
            transcendentals=2 * rows * keys_all,
        ),
    )(scalars, guide, *queries, *caches)


def paste(scalars, previous, mine, others, parts):
    rows, columns = previous.shape
    flat = [piece for part in mine for piece in part]
    rest = [piece for other in others for piece in other]

    def kernel(s_ref, prev_ref, *refs):
        out = refs[-1]
        out[...] = prev_ref[...]

        def put(k, m, piece):
            at = pl.multiple_of(((s_ref[0] ^ m) * parts + k) * HD, HD)
            out[:, pl.ds(at, HD)] = piece

        @pl.when(s_ref[1] == 1)
        def _():
            for k in range(parts):
                for m in range(GROUPS):
                    put(k, m, refs[k * GROUPS + m][...])

        for n in range(len(others)):

            @pl.when(s_ref[2 + n] == 1)
            def _():
                for k in range(parts):
                    for m in range(GROUPS):
                        put(k, m, refs[parts * GROUPS + n * parts + k][m])

    return call(
        kernel,
        jax.ShapeDtypeStruct((rows, columns), BF),
        scalars,
        [previous, *flat, *rest],
        0,
        2 * rows * columns * 4,
    )


def body(hidden, key_cache, value_cache, cached_out, w_query, guide, masked_tiles, mask_count):
    images = lax.axis_size("image")
    tokens = lax.axis_size("token")
    inner = key_cache.shape[3]
    heads = inner // HD
    parts = heads // GROUPS
    slots = masked_tiles.shape[1]
    layers = tokens // (2 * GROUPS)
    assert images == 4 and hidden.shape[1] == 1 and hidden.shape[2] == TILE
    assert tokens == layers * 2 * GROUPS and slots == 2 * layers and heads == parts * GROUPS

    image = lax.axis_index("image")
    token = lax.axis_index("token")
    core = token % 2
    chip = token // 2
    z = chip // layers
    layer = chip % layers
    tiles = masked_tiles[0]

    def over_image(x, m):
        return lax.ppermute(x, "image", [(i, i ^ m) for i in range(images)])

    def over_z(x, m):
        span = 2 * layers
        return lax.ppermute(x, "token", [(t, ((t // span) ^ m) * span + t % span) for t in range(tokens)])

    def over_core(x):
        return lax.ppermute(x, "token", [(t, t ^ 1) for t in range(tokens)])

    def to_targets(x, r):
        pairs = []
        for t in range(tokens):
            c, at, s = t % 2, (t // 2) % layers, t // 2 // layers
            goal = (s + r) % 4
            pairs.append((t, ((2 * c + goal // 2) * layers + at) * 2 + goal % 2))
        return lax.ppermute(x, "token", pairs)

    layer_groups = [
        [(s * layers + at) * 2 + c for at in range(layers)] for s in range(GROUPS) for c in range(2)
    ]
    group_groups = [list(range(s * layers * 2, (s + 1) * layers * 2)) for s in range(GROUPS)]

    packed = pack_weights(core[None], w_query, parts)
    half = w_query.shape[0] // 2
    weights = []
    for own in packed:
        by_x = over_image(own, 1)
        by_y = over_image(own, 2)
        far_first = over_image(by_x[:half], 2)
        far_last = over_image(by_y[half:], 1)
        weights.append([own, by_x, by_y, far_first, far_last])

    own_hidden = hidden[:, 0]
    other_hidden = over_core(own_hidden)

    blocks = pack_keys(z[None], key_cache[:, 0], value_cache[:, 0])
    arrived = [blocks[0]] + [over_z(blocks[m], m) for m in range(1, GROUPS)]
    gathered = jnp.concatenate(arrived, axis=2)
    if layers == 1:
        caches = [gathered[None], over_core(gathered)[None]]
    else:
        caches = [lax.all_gather(gathered, "token", axis_index_groups=group_groups)]

    my_slot = layer * 2 + core
    my_tile = tiles[my_slot]
    target = 2 * (z % 2) + core
    owner_z = my_tile // 2 // layers
    choice = (target - owner_z) % 4

    mine, others = [], []
    for k in range(parts):
        arrived_queries = None
        for at in range(layers):
            pair = tiles[2 * at : 2 * at + 2]
            is_own = (pair % 2 == core).astype(jnp.int32)
            scalars = jnp.concatenate([jnp.stack([image, z]).astype(jnp.int32), is_own])
            sent = project(scalars, own_hidden, other_hidden, weights[k])
            came = [to_targets(x, r) for r, x in enumerate(sent)]
            if layers > 1:
                holds = (tiles[2 * at + core] // 2) % layers == layer
                came = [
                    lax.psum(jnp.where(holds, x, jnp.zeros_like(x)), "token", axis_index_groups=layer_groups)
                    for x in came
                ]
            if arrived_queries is None:
                arrived_queries = came
            else:
                arrived_queries = [
                    jnp.where(layer == at, new, old) for new, old in zip(came, arrived_queries)
                ]
        guided = attend(choice[None], guide, arrived_queries, caches, k)
        pieces = [guided] + [over_z(guided, m) for m in range(1, GROUPS)]
        mine.append(pieces)
        stacked = jnp.stack(pieces)
        if layers == 1:
            others.append([over_core(stacked)])
        else:
            everyone = lax.all_gather(stacked, "token", axis_index_groups=group_groups)
            others.append([everyone[n] for n in range(slots)])

    in_use = jnp.arange(slots, dtype=jnp.int32) < mask_count[0]
    hit = ((tiles == token) & in_use).astype(jnp.int32)
    if layers == 1:
        flags = jnp.stack([z, hit[core], hit[1 - core]]).astype(jnp.int32)
    else:
        flags = jnp.concatenate([jnp.stack([z, hit[my_slot]]).astype(jnp.int32), hit])
    by_other = [[others[k][n] for k in range(parts)] for n in range(len(others[0]))]
    edited = paste(flags, cached_out[0], mine, by_other, parts)
    return edited[None]


def solution(mesh):
    return jax.shard_map(
        body,
        mesh=mesh,
        in_specs=(
            P(None, "image", "token", None),
            P(None, "image", "token", None),
            P(None, "image", "token", None),
            P("image", "token", None),
            P("image", None),
            P("image"),
            P("image", None),
            P("image"),
        ),
        out_specs=P("image", "token", None),
        check_vma=False,
    )
```

time: 381 us -> 169 us (0.44)
  waiting for transfers between devices: 213 us -> 48.8 us
  blocking collectives: 110 us -> 0 us
  starting transfers between devices: 0.05 us -> 70.6 us
  Pallas kernels: 0 us -> 19.1 us
  matrix products: 13.9 us -> 0 us
  between operations: 14.5 us -> 4.68 us
  other arithmetic: 9.51 us -> 1.41 us
  local copies, waits for them, and re-layouts: 17.9 us -> 23.7 us
    psum x2 -> x0, waiting for transfers between devices: 116 us -> none  [spread(): return lax.psum(jnp.where(mine, array, jnp.zeros_like(array)), axis)]
    all_gather x1 -> x0, waiting for transfers between devices: 96.6 us -> none  [body(): lax.all_gather(w_query, 'image', axis=0, tiled=True)]
    psum x2 -> x0, blocking collectives: 84.1 us -> none  [the longest x1 58.2 us: body(): summed_rows = lax.psum(guided_part, 'token')]
    ppermute x0 -> x41, starting transfers between devices: none -> 70.6 us  [the longest x12 35.5 us: to_targets(): return lax.ppermute(x, 'token', pairs)]
    ppermute x0 -> x41, waiting for transfers between devices: none -> 48.8 us  [the longest x12 31.3 us: over_z(): lax.ppermute(x, 'token', [(t, (t // span ^ m) * span + t % span) for t in...]
    pmax x1 -> x0, blocking collectives: 25.9 us -> none  [body(): lax.pmax(local_max.astype(jnp.bfloat16), 'token').astype(local_max.dtype)]
    pallas_call x0 -> x9, Pallas kernels: none -> 19.1 us  [the longest x6 11.6 us: call(): pl.pallas_call(kernel, out_shape=out_shape, in_specs=[SMEM_SPEC] + [VMEM_...]
    unnamed x14 -> x79, local copies, waits for them, and re-layouts: 2.38 us -> 19.3 us
  transfers between devices with their start and end apart: 3 -> 41, of which waited for: 3 -> 9; matrix products, arithmetic and copies ran while one was open for 1% -> 4% of each run, Pallas kernels for 0% -> 10%
where the time goes in v1:
time: 169 us; the launch traced here: 168 us
  starting transfers between devices  70.6 us (42%)
  waiting for transfers between devices  48.8 us (29%)
  local copies, waits for them, and re-layouts  23.7 us (14%)
  Pallas kernels  19.1 us (11%)
  between operations  4.68 us (3%)
    ppermute x12, starting transfers between devices, to_targets(): return lax.ppermute(x, 'token', pairs)  35.5 us
    ppermute x12, waiting for transfers between devices, over_z(): lax.ppermute(x, 'token', [(t, (t // span ^ m) * span + t % span) for t in...  31.3 us
    unnamed x79, local copies, waits for them, and re-layouts  19.3 us
    ppermute x12, starting transfers between devices, over_z(): lax.ppermute(x, 'token', [(t, (t // span ^ m) * span + t % span) for t in...  19.1 us
    ppermute x12, waiting for transfers between devices, over_image(): return lax.ppermute(x, 'image', [(i, i ^ m) for i in range(images)])  17.4 us
    ppermute x12, starting transfers between devices, over_image(): return lax.ppermute(x, 'image', [(i, i ^ m) for i in range(images)])  15.5 us
    pallas_call x6, Pallas kernels, call(): pl.pallas_call(kernel, out_shape=out_shape, in_specs=[SMEM_SPEC] + [VMEM_...  11.6 us
    pallas_call x3, Pallas kernels, attend(): pl.pallas_call(smem_kernel, out_shape=jax.ShapeDtypeStruct((rows, HD), BF...  7.46 us
  transfers between devices with their start and end apart: 41, of which 9 were waited for; matrix products, arithmetic and copies ran while one was open for 4% of the time, Pallas kernels for 10%

profile of v1, /device:TPU:0, one launch (start us, length us, event | category | flops | bytes accessed | tf_op | source)
XLA Modules:
  0.0 168.3 jit_solution(16518901196875564501)
XLA Ops:
  0.0 1.3 copy-done.10
  1.3 1.1 copy-done.11
  2.5 3.1 %collective-permute-start.9 = (bf16[2,2,128,384]{3,2,1,0:T(8,128)(2,1)S(1)}, bf16[2,2,128,384]{3,2,1,0:T(8,128)(2,1)S(1)}, u32[]{:S(2)}, u32[]{:S(2)}) collective-permute-start(bf16[2,2,128,384]{3,2,1,0:T(8,128)(2,1)S(1)} %get-tuple-element.30), channel_id=1, source_target_pairs={{0,2},{1,3},{2,0},{3,1},{4,6},{5,7},{6,4},{7,5},{8,10},{9,11},{10,... | collective-permute-start | bytes 1179656 | tf_op jit(solution)/shard_map/ppermute | solution.py:243
  5.6 2.6 %collective-permute-start.10 = (bf16[2,2,128,384]{3,2,1,0:T(8,128)(2,1)S(1)}, bf16[2,2,128,384]{3,2,1,0:T(8,128)(2,1)S(1)}, u32[]{:S(2)}, u32[]{:S(2)}) collective-permute-start(bf16[2,2,128,384]{3,2,1,0:T(8,128)(2,1)S(1)} %get-tuple-element.31), channel_id=1, source_target_pairs={{0,4},{1,5},{2,6},{3,7},{4,0},{5,1},{6,2},{7,3},{8,12},{9,13},{10,... | collective-permute-start | bytes 1179656 | tf_op jit(solution)/shard_map/ppermute | solution.py:243
  8.3 14.1 %collective-permute-done.9 = bf16[2,2,128,384]{3,2,1,0:T(8,128)(2,1)S(1)} collective-permute-done((bf16[2,2,128,384]{3,2,1,0:T(8,128)(2,1)S(1)}, bf16[2,2,128,384]{3,2,1,0:T(8,128)(2,1)S(1)}, u32[]{:S(2)}, u32[]{:S(2)}) %collective-permute-start.9) | collective-permute-done | bytes 393248 | tf_op jit(solution)/shard_map/ppermute | solution.py:243
  22.5 13.0 %collective-permute-done.10 = bf16[2,2,128,384]{3,2,1,0:T(8,128)(2,1)S(1)} collective-permute-done((bf16[2,2,128,384]{3,2,1,0:T(8,128)(2,1)S(1)}, bf16[2,2,128,384]{3,2,1,0:T(8,128)(2,1)S(1)}, u32[]{:S(2)}, u32[]{:S(2)}) %collective-permute-start.10) | collective-permute-done | bytes 393248 | tf_op jit(solution)/shard_map/ppermute | solution.py:243
  35.7 1.7 copy-done.1
  37.5 1.6 collective-permute-start.1
  39.1 1.5 collective-permute-start.2
  40.6 0.7 copy-done.16
  41.9 7.6 %collective-permute-done.1.refs_1_ = bf16[768,256]{1,0:T(8,128)(2,1)S(1)} collective-permute-done((bf16[768,256]{1,0:T(8,128)(2,1)S(1)}, bf16[768,256]{1,0:T(8,128)(2,1)S(1)}, u32[]{:S(2)}, u32[]{:S(2)}) %collective-permute-start.1) | collective-permute-done | bytes 393248 | tf_op jit(solution)/shard_map/ppermute | solution.py:239
  49.5 1.5 collective-permute-start.17
  51.0 0.8 copy-done.14
  51.8 1.5 collective-permute-start.27
  53.3 4.7 %collective-permute-done.16.refs_1_ = bf16[768,256]{1,0:T(8,128)(2,1)S(1)} collective-permute-done((bf16[768,256]{1,0:T(8,128)(2,1)S(1)}, bf16[768,256]{1,0:T(8,128)(2,1)S(1)}, u32[]{:S(2)}, u32[]{:S(2)}) %collective-permute-start.16) | collective-permute-done | bytes 393248 | tf_op jit(solution)/shard_map/ppermute | solution.py:239
  57.9 1.5 collective-permute-start.28
  59.5 0.8 copy-done.12
  60.3 0.7 copy-done.8
  61.5 4.4 %collective-permute-done.27.refs_1_ = bf16[768,256]{1,0:T(8,128)(2,1)S(1)} collective-permute-done((bf16[768,256]{1,0:T(8,128)(2,1)S(1)}, bf16[768,256]{1,0:T(8,128)(2,1)S(1)}, u32[]{:S(2)}, u32[]{:S(2)}) %collective-permute-start.27) | collective-permute-done | bytes 393248 | tf_op jit(solution)/shard_map/ppermute | solution.py:239
  66.0 1.5 collective-permute-start.4
  68.1 0.7 slice.26
  68.8 0.7 slice.27
  69.5 0.7 slice.28
  70.2 1.5 collective-permute-start.18
  71.8 0.7 collective-permute-done.3.refs_3_
  72.5 0.7 copy-done.19
  73.2 2.3 %collective-permute-start.19 = (bf16[384,256]{1,0:T(8,128)(2,1)}, bf16[384,256]{1,0:T(8,128)(2,1)}, u32[]{:S(2)}, u32[]{:S(2)}) collective-permute-start(bf16[384,256]{1,0:T(8,128)(2,1)} %slice.27), channel_id=1, source_target_pairs={{0,8},{8,0},{16,24},{24,16},{1,9},{9,1},{17,25},{25,17},{2,10},{10... | collective-permute-start | bytes 589832 | tf_op jit(solution)/shard_map/ppermute | solution.py:239
  75.5 0.7 copy-done.21
  76.1 1.5 collective-permute-start.29
  77.7 0.9 slice.29
  78.8 1.0 copy-done.7
  79.8 1.0 copy-done.9
  80.8 1.0 copy-done.17
  81.8 0.9 copy-done.20
  82.7 0.9 copy-done.22
  83.6 2.8 %shard_map.83 = (bf16[256,128]{1,0:T(8,128)(2,1)S(1)}, bf16[256,128]{1,0:T(8,128)(2,1)S(1)}, bf16[256,128]{1,0:T(8,128)(2,1)S(1)}, bf16[256,128]{1,0:T(8,128)(2,1)S(1)}) custom-call(s32[4]{0:T(128)S(1)} %pad_add_fusion.1.s_ref, bf16[2,128,3072]{2,1,0:T(8,128)(2,1)S(1)} %bitcast.33, bf16[2,128,3072]{2,1,0:T(8,128)(2,1)} %collective-permute-done.other_ref, ...), custom_call_target="tpu_custom_call" | custom-call | flops 805306368 | bytes 4718592 | tf_op jit(solution)/shard_map/pallas_call | solution.py:23
  86.5 0.7 collective-permute-start.5
  87.2 11.8 %collective-permute-start.6 = (bf16[256,128]{1,0:T(8,128)(2,1)S(1)}, bf16[256,128]{1,0:T(8,128)(2,1)S(1)}, u32[]{:S(2)}, u32[]{:S(2)}) collective-permute-start(bf16[256,128]{1,0:T(8,128)(2,1)S(1)} %get-tuple-element.26), channel_id=1, source_target_pairs={{0,1},{1,5},{2,2},{3,6},{4,3},{5,7},{6,0},{7,4},{8,9},{9,13},{10,1... | collective-permute-start | bytes 196616 | tf_op jit(solution)/shard_map/ppermute | solution.py:254
  99.1 3.5 %shard_map.86 = (bf16[256,128]{1,0:T(8,128)(2,1)S(1)}, bf16[256,128]{1,0:T(8,128)(2,1)S(1)}, bf16[256,128]{1,0:T(8,128)(2,1)S(1)}, bf16[256,128]{1,0:T(8,128)(2,1)}) custom-call(s32[4]{0:T(128)S(1)} %pad_add_fusion.1.s_ref, bf16[2,128,3072]{2,1,0:T(8,128)(2,1)S(1)} %bitcast.34, bf16[2,128,3072]{2,1,0:T(8,128)(2,1)} %collective-permute-done.other_ref, ...), custom_call_target="tpu_custom_call" | custom-call | flops 805306368 | bytes 4718592 | tf_op jit(solution)/shard_map/pallas_call | solution.py:23
  102.6 3.6 %collective-permute-start.8 = (bf16[256,128]{1,0:T(8,128)(2,1)S(1)}, bf16[256,128]{1,0:T(8,128)(2,1)S(1)}, u32[]{:S(2)}, u32[]{:S(2)}) collective-permute-start(bf16[256,128]{1,0:T(8,128)(2,1)S(1)} %get-tuple-element.28), channel_id=1, source_target_pairs={{0,3},{1,7},{2,0},{3,4},{4,1},{5,5},{6,2},{7,6},{8,11},{9,15},{10,... | collective-permute-start | bytes 196616 | tf_op jit(solution)/shard_map/ppermute | solution.py:254
  106.2 0.7 collective-permute-start.20
  106.9 4.4 %collective-permute-start.21 = (bf16[256,128]{1,0:T(8,128)(2,1)S(1)}, bf16[256,128]{1,0:T(8,128)(2,1)S(1)}, u32[]{:S(2)}, u32[]{:S(2)}) collective-permute-start(bf16[256,128]{1,0:T(8,128)(2,1)S(1)} %get-tuple-element.35), channel_id=1, source_target_pairs={{0,1},{1,5},{2,2},{3,6},{4,3},{5,7},{6,0},{7,4},{8,9},{9,13},{10,1... | collective-permute-start | bytes 196616 | tf_op jit(solution)/shard_map/ppermute | solution.py:254
  111.4 3.6 %shard_map.88 = (bf16[256,128]{1,0:T(8,128)(2,1)}, bf16[256,128]{1,0:T(8,128)(2,1)}, bf16[256,128]{1,0:T(8,128)(2,1)}, bf16[256,128]{1,0:T(8,128)(2,1)}) custom-call(s32[4]{0:T(128)S(1)} %pad_add_fusion.1.s_ref, bf16[2,128,3072]{2,1,0:T(8,128)(2,1)S(1)} %bitcast.35, bf16[2,128,3072]{2,1,0:T(8,128)(2,1)} %collective-permute-done.other_ref, ...), custom_call_target="tpu_custom_call" | custom-call | flops 805306368 | bytes 4718592 | tf_op jit(solution)/shard_map/pallas_call | solution.py:23
  115.7 4.7 %collective-permute-start.23 = (bf16[256,128]{1,0:T(8,128)(2,1)}, bf16[256,128]{1,0:T(8,128)(2,1)S(1)}, u32[]{:S(2)}, u32[]{:S(2)}) collective-permute-start(bf16[256,128]{1,0:T(8,128)(2,1)} %get-tuple-element.37), channel_id=1, source_target_pairs={{0,3},{1,7},{2,0},{3,4},{4,1},{5,5},{6,2},{7,6},{8,11},{9,15},{10,... | collective-permute-start | bytes 196616 | tf_op jit(solution)/shard_map/ppermute | solution.py:254
  121.0 1.5 collective-permute-start.31
  123.1 4.8 %collective-permute-start.32 = (bf16[256,128]{1,0:T(8,128)(2,1)}, bf16[256,128]{1,0:T(8,128)(2,1)S(1)}, u32[]{:S(2)}, u32[]{:S(2)}) collective-permute-start(bf16[256,128]{1,0:T(8,128)(2,1)} %get-tuple-element.40), channel_id=1, source_target_pairs={{0,1},{1,5},{2,2},{3,6},{4,3},{5,7},{6,0},{7,4},{8,9},{9,13},{10,1... | collective-permute-start | bytes 196616 | tf_op jit(solution)/shard_map/ppermute | solution.py:254
  128.5 3.3 %collective-permute-start.34 = (bf16[256,128]{1,0:T(8,128)(2,1)}, bf16[256,128]{1,0:T(8,128)(2,1)S(1)}, u32[]{:S(2)}, u32[]{:S(2)}) collective-permute-start(bf16[256,128]{1,0:T(8,128)(2,1)} %get-tuple-element.42), channel_id=1, source_target_pairs={{0,3},{1,7},{2,0},{3,4},{4,1},{5,5},{6,2},{7,6},{8,11},{9,15},{10,... | collective-permute-start | bytes 196616 | tf_op jit(solution)/shard_map/ppermute | solution.py:254
  135.9 0.8 copy-done.24
  136.8 0.8 copy-done.26
  137.6 0.8 copy-done.28
  138.5 0.8 copy-done.36
  139.3 2.5 %shard_map.85.refs_0_ = bf16[128,128]{1,0:T(8,128)(2,1)S(1)} custom-call(s32[1]{0:T(128)} %bitcast.5.s_ref, f32[1]{0:T(128)S(6)} %copy.12.g_ref, bf16[256,128]{1,0:T(8,128)(2,1)S(1)} %copy-done.24, bf16[256,128]{1,0:T(8,128)(2,1)S(1)} %copy-done.26, bf16[256,128]{1,0:T(8,128)(2,1)S(1)} %copy-done.28, bf16[256,128]{1,0:T(8,128)(2,1)S(1)} %copy-done.36, ...), custom_call_target="tpu_custom_call" | custom-call | flops 134217728 | bytes 3145728 | tf_op jit(solution)/shard_map/pallas_call | solution.py:167
  141.8 0.7 collective-permute-start.13
  142.6 2.6 %collective-permute-start.14 = (bf16[128,128]{1,0:T(8,128)(2,1)S(1)}, bf16[128,128]{1,0:T(8,128)(2,1)S(1)}, u32[]{:S(2)}, u32[]{:S(2)}) collective-permute-start(bf16[128,128]{1,0:T(8,128)(2,1)S(1)} %shard_map.85.refs_0_), channel_id=1, source_target_pairs={{0,4},{1,5},{2,6},{3,7},{4,0},{5,1},{6,2},{7,3},{8,12},{9,13},{10,... | collective-permute-start | bytes 98312 | tf_op jit(solution)/shard_map/ppermute | solution.py:243
  145.2 1.1 collective-permute-start.15
  146.3 2.5 %shard_map.87.refs_4_ = bf16[128,128]{1,0:T(8,128)(2,1)S(1)} custom-call(s32[1]{0:T(128)} %bitcast.5.s_ref, f32[1]{0:T(128)S(6)} %copy.12.g_ref, bf16[256,128]{1,0:T(8,128)(2,1)S(1)} %copy-done.30, bf16[256,128]{1,0:T(8,128)(2,1)S(1)} %copy-done.32, bf16[256,128]{1,0:T(8,128)(2,1)S(1)} %copy-done.34, bf16[256,128]{1,0:T(8,128)(2,1)S(1)} %collective-permute-done.23.refs_3_, ...), custom_call_target="tpu_custom_call" | custom-call | flops 134217728 | bytes 3145728 | tf_op jit(solution)/shard_map/pallas_call | solution.py:167
  148.9 3.3 %collective-permute-start.25 = (bf16[128,128]{1,0:T(8,128)(2,1)S(1)}, bf16[128,128]{1,0:T(8,128)(2,1)S(1)}, u32[]{:S(2)}, u32[]{:S(2)}) collective-permute-start(bf16[128,128]{1,0:T(8,128)(2,1)S(1)} %shard_map.87.refs_4_), channel_id=1, source_target_pairs={{0,4},{1,5},{2,6},{3,7},{4,0},{5,1},{6,2},{7,3},{8,12},{9,13},{10,... | collective-permute-start | bytes 98312 | tf_op jit(solution)/shard_map/ppermute | solution.py:243
  152.2 2.5 %shard_map.89.refs_8_ = bf16[128,128]{1,0:T(8,128)(2,1)S(1)} custom-call(s32[1]{0:T(128)} %bitcast.5.s_ref, f32[1]{0:T(128)S(6)} %copy.12.g_ref, bf16[256,128]{1,0:T(8,128)(2,1)S(1)} %collective-permute-done.31.refs_0_, bf16[256,128]{1,0:T(8,128)(2,1)S(1)} %collective-permute-done.32.refs_1_, bf16[256,128]{1,0:T(8,128)(2,1)S(1)} %collective-permute-done.33.refs_2_, ...), custom_call_target="tpu_custom_call" | custom-call | flops 134217728 | bytes 3145728 | tf_op jit(solution)/shard_map/pallas_call | solution.py:167
  154.7 1.2 collective-permute-start.26
  155.8 3.3 %collective-permute-start.36 = (bf16[128,128]{1,0:T(8,128)(2,1)S(1)}, bf16[128,128]{1,0:T(8,128)(2,1)S(1)}, u32[]{:S(2)}, u32[]{:S(2)}) collective-permute-start(bf16[128,128]{1,0:T(8,128)(2,1)S(1)} %shard_map.89.refs_8_), channel_id=1, source_target_pairs={{0,4},{1,5},{2,6},{3,7},{4,0},{5,1},{6,2},{7,3},{8,12},{9,13},{10,... | collective-permute-start | bytes 98312 | tf_op jit(solution)/shard_map/ppermute | solution.py:243
  159.2 1.2 collective-permute-start.37
  161.0 3.9 %collective-permute-done.37.refs_11_ = bf16[128,128]{1,0:T(8,128)(2,1)S(1)} collective-permute-done((bf16[128,128]{1,0:T(8,128)(2,1)S(1)}, bf16[128,128]{1,0:T(8,128)(2,1)S(1)}, u32[]{:S(2)}, u32[]{:S(2)}) %collective-permute-start.37) | collective-permute-done | bytes 32800 | tf_op jit(solution)/shard_map/ppermute | solution.py:243
  165.6 1.3 pad_add_fusion.s_ref
  166.9 1.3 shard_map.90
  (121 shorter events, 6.8 us)
Async XLA Ops:
  0.0 8.2 %copy-start = (bf16[2,1,128,3072]{3,2,1,0:T(8,128)(2,1)S(1)}, bf16[2,1,128,3072]{3,2,1,0:T(8,128)(2,1)}, u32[]{:S(2)}) copy-start(bf16[2,1,128,3072]{3,2,1,0:T(8,128)(2,1)} %param.8) | copy-start | bytes 4718596
  0.0 1.3 copy-start.10
  1.3 1.1 copy-start.11
  2.5 19.9 %collective-permute-start.9 = (bf16[2,2,128,384]{3,2,1,0:T(8,128)(2,1)S(1)}, bf16[2,2,128,384]{3,2,1,0:T(8,128)(2,1)S(1)}, u32[]{:S(2)}, u32[]{:S(2)}) collective-permute-start(bf16[2,2,128,384]{3,2,1,0:T(8,128)(2,1)S(1)} %get-tuple-element.30), channel_id=1, source_target_pairs={{0,2},{1,3},{2,0},{3,1},{4,6},{5,7},{6,4},{7,5},{8,10},{9,11},{10,... | collective-permute-start | bytes 1179656 | tf_op jit(solution)/shard_map/ppermute | solution.py:243
  5.6 29.8 %collective-permute-start.10 = (bf16[2,2,128,384]{3,2,1,0:T(8,128)(2,1)S(1)}, bf16[2,2,128,384]{3,2,1,0:T(8,128)(2,1)S(1)}, u32[]{:S(2)}, u32[]{:S(2)}) collective-permute-start(bf16[2,2,128,384]{3,2,1,0:T(8,128)(2,1)S(1)} %get-tuple-element.31), channel_id=1, source_target_pairs={{0,4},{1,5},{2,6},{3,7},{4,0},{5,1},{6,2},{7,3},{8,12},{9,13},{10,... | collective-permute-start | bytes 1179656 | tf_op jit(solution)/shard_map/ppermute | solution.py:243
  8.2 27.3 %collective-permute-start.11 = (bf16[2,2,128,384]{3,2,1,0:T(8,128)(2,1)S(1)}, bf16[2,2,128,384]{3,2,1,0:T(8,128)(2,1)S(1)}, u32[]{:S(2)}, u32[]{:S(2)}) collective-permute-start(bf16[2,2,128,384]{3,2,1,0:T(8,128)(2,1)S(1)} %get-tuple-element.32), channel_id=1, source_target_pairs={{0,6},{1,7},{2,4},{3,5},{4,2},{5,3},{6,0},{7,1},{8,14},{9,15},{10,... | collective-permute-start | bytes 1179656 | tf_op jit(solution)/shard_map/ppermute | solution.py:243
  8.2 70.4 %collective-permute-start = (bf16[2,128,3072]{2,1,0:T(8,128)(2,1)S(1)}, bf16[2,128,3072]{2,1,0:T(8,128)(2,1)}, u32[]{:S(2)}, u32[]{:S(2)}) collective-permute-start(bf16[2,128,3072]{2,1,0:T(8,128)(2,1)S(1)} %bitcast.32), channel_id=1, source_target_pairs={{0,1},{1,0},{2,3},{3,2},{4,5},{5,4},{6,7},{7,6},{8,9},{9,8},{10,11... | collective-permute-start | bytes 4718600 | tf_op jit(solution)/shard_map/ppermute | solution.py:246
  35.6 93.0 %collective-permute-start.12 = (bf16[2,2,512,384]{3,2,1,0:T(8,128)(2,1)S(1)}, bf16[2,2,512,384]{3,2,1,0:T(8,128)(2,1)}, u32[]{:S(2)}, u32[]{:S(2)}) collective-permute-start(bf16[2,2,512,384]{3,2,1,0:T(8,128)(2,1)S(1)} %constant_dynamic-update-slice_fusion), channel_id=1, source_target_pairs={{0,1},{1,0},{2,3},{3,2},{4,5},{5,4},{6,7},{7,6},{8,9},{9,8},{10,11... | collective-permute-start | bytes 4718600 | tf_op jit(solution)/shard_map/ppermute | solution.py:246
  35.7 1.7 copy-start.1
  37.5 40.1 %copy-start.37 = (s32[1,2]{1,0:T(1,128)S(1)}, s32[1,2]{1,0:T(1,128)}, u32[]{:S(2)}) copy-start(s32[1,2]{1,0:T(1,128)} %param.14) | copy-start | bytes 28
  37.5 12.0 %collective-permute-start.1 = (bf16[768,256]{1,0:T(8,128)(2,1)S(1)}, bf16[768,256]{1,0:T(8,128)(2,1)S(1)}, u32[]{:S(2)}, u32[]{:S(2)}) collective-permute-start(bf16[768,256]{1,0:T(8,128)(2,1)S(1)} %get-tuple-element.24.refs_0_), channel_id=1, source_target_pairs={{0,8},{8,0},{16,24},{24,16},{1,9},{9,1},{17,25},{25,17},{2,10},{10... | collective-permute-start | bytes 1179656 | tf_op jit(solution)/shard_map/ppermute | solution.py:239
  39.1 12.7 %collective-permute-start.2 = (bf16[768,256]{1,0:T(8,128)(2,1)S(1)}, bf16[768,256]{1,0:T(8,128)(2,1)S(1)}, u32[]{:S(2)}, u32[]{:S(2)}) collective-permute-start(bf16[768,256]{1,0:T(8,128)(2,1)S(1)} %get-tuple-element.24.refs_0_), channel_id=1, source_target_pairs={{0,16},{8,24},{16,0},{24,8},{1,17},{9,25},{17,1},{25,9},{2,18},{10... | collective-permute-start | bytes 1179656 | tf_op jit(solution)/shard_map/ppermute | solution.py:239
  41.4 16.6 %collective-permute-start.16 = (bf16[768,256]{1,0:T(8,128)(2,1)S(1)}, bf16[768,256]{1,0:T(8,128)(2,1)S(1)}, u32[]{:S(2)}, u32[]{:S(2)}) collective-permute-start(bf16[768,256]{1,0:T(8,128)(2,1)S(1)} %get-tuple-element.33.refs_0_), channel_id=1, source_target_pairs={{0,8},{8,0},{16,24},{24,16},{1,9},{9,1},{17,25},{25,17},{2,10},{10... | collective-permute-start | bytes 1179656 | tf_op jit(solution)/shard_map/ppermute | solution.py:239
  49.5 20.0 %copy-start.6 = (bf16[768,256]{1,0:T(8,128)(2,1)}, bf16[768,256]{1,0:T(8,128)(2,1)S(1)}, u32[]{:S(2)}) copy-start(bf16[768,256]{1,0:T(8,128)(2,1)S(1)} %collective-permute-done.1.refs_1_) | copy-start | bytes 1179652
  49.5 11.5 %collective-permute-start.17 = (bf16[768,256]{1,0:T(8,128)(2,1)S(1)}, bf16[768,256]{1,0:T(8,128)(2,1)S(1)}, u32[]{:S(2)}, u32[]{:S(2)}) collective-permute-start(bf16[768,256]{1,0:T(8,128)(2,1)S(1)} %get-tuple-element.33.refs_0_), channel_id=1, source_target_pairs={{0,16},{8,24},{16,0},{24,8},{1,17},{9,25},{17,1},{25,9},{2,18},{10... | collective-permute-start | bytes 1179656 | tf_op jit(solution)/shard_map/ppermute | solution.py:239
  51.8 14.2 %collective-permute-start.27 = (bf16[768,256]{1,0:T(8,128)(2,1)S(1)}, bf16[768,256]{1,0:T(8,128)(2,1)S(1)}, u32[]{:S(2)}, u32[]{:S(2)}) collective-permute-start(bf16[768,256]{1,0:T(8,128)(2,1)S(1)} %get-tuple-element.38.refs_0_), channel_id=1, source_target_pairs={{0,8},{8,0},{16,24},{24,16},{1,9},{9,1},{17,25},{25,17},{2,10},{10... | collective-permute-start | bytes 1179656 | tf_op jit(solution)/shard_map/ppermute | solution.py:239
  57.9 10.2 %copy-start.2 = (bf16[768,256]{1,0:T(8,128)(2,1)}, bf16[768,256]{1,0:T(8,128)(2,1)S(1)}, u32[]{:S(2)}) copy-start(bf16[768,256]{1,0:T(8,128)(2,1)S(1)} %collective-permute-done.16.refs_1_) | copy-start | bytes 1179652
  57.9 12.3 %collective-permute-start.28 = (bf16[768,256]{1,0:T(8,128)(2,1)S(1)}, bf16[768,256]{1,0:T(8,128)(2,1)}, u32[]{:S(2)}, u32[]{:S(2)}) collective-permute-start(bf16[768,256]{1,0:T(8,128)(2,1)S(1)} %get-tuple-element.38.refs_0_), channel_id=1, source_target_pairs={{0,16},{8,24},{16,0},{24,8},{1,17},{9,25},{17,1},{25,9},{2,18},{10... | collective-permute-start | bytes 1179656 | tf_op jit(solution)/shard_map/ppermute | solution.py:239
  61.0 7.8 %copy-start.4 = (bf16[768,256]{1,0:T(8,128)(2,1)}, bf16[768,256]{1,0:T(8,128)(2,1)S(1)}, u32[]{:S(2)}) copy-start(bf16[768,256]{1,0:T(8,128)(2,1)S(1)} %collective-permute-done.17.refs_2_) | copy-start | bytes 1179652
  61.0 11.5 %collective-permute-start.3 = (bf16[384,256]{1,0:T(8,128)(2,1)S(1)}, bf16[384,256]{1,0:T(8,128)(2,1)S(1)}, u32[]{:S(2)}, u32[]{:S(2)}) collective-permute-start(bf16[384,256]{1,0:T(8,128)(2,1)S(1)} %slice.24), channel_id=1, source_target_pairs={{0,16},{8,24},{16,0},{24,8},{1,17},{9,25},{17,1},{25,9},{2,18},{10... | collective-permute-start | bytes 589832 | tf_op jit(solution)/shard_map/ppermute | solution.py:239
  66.0 9.5 %collective-permute-start.4 = (bf16[384,256]{1,0:T(8,128)(2,1)S(1)}, bf16[384,256]{1,0:T(8,128)(2,1)S(1)}, u32[]{:S(2)}, u32[]{:S(2)}) collective-permute-start(bf16[384,256]{1,0:T(8,128)(2,1)S(1)} %slice.25), channel_id=1, source_target_pairs={{0,8},{8,0},{16,24},{24,16},{1,9},{9,1},{17,25},{25,17},{2,10},{10... | collective-permute-start | bytes 589832 | tf_op jit(solution)/shard_map/ppermute | solution.py:239
  70.2 16.2 %collective-permute-start.18 = (bf16[384,256]{1,0:T(8,128)(2,1)}, bf16[384,256]{1,0:T(8,128)(2,1)}, u32[]{:S(2)}, u32[]{:S(2)}) collective-permute-start(bf16[384,256]{1,0:T(8,128)(2,1)} %slice.26), channel_id=1, source_target_pairs={{0,16},{8,24},{16,0},{24,8},{1,17},{9,25},{17,1},{25,9},{2,18},{10... | collective-permute-start | bytes 589832 | tf_op jit(solution)/shard_map/ppermute | solution.py:239
  73.2 14.0 %collective-permute-start.19 = (bf16[384,256]{1,0:T(8,128)(2,1)}, bf16[384,256]{1,0:T(8,128)(2,1)}, u32[]{:S(2)}, u32[]{:S(2)}) collective-permute-start(bf16[384,256]{1,0:T(8,128)(2,1)} %slice.27), channel_id=1, source_target_pairs={{0,8},{8,0},{16,24},{24,16},{1,9},{9,1},{17,25},{25,17},{2,10},{10... | collective-permute-start | bytes 589832 | tf_op jit(solution)/shard_map/ppermute | solution.py:239
  76.1 22.8 %collective-permute-start.29 = (bf16[384,256]{1,0:T(8,128)(2,1)}, bf16[384,256]{1,0:T(8,128)(2,1)}, u32[]{:S(2)}, u32[]{:S(2)}) collective-permute-start(bf16[384,256]{1,0:T(8,128)(2,1)} %slice.28), channel_id=1, source_target_pairs={{0,16},{8,24},{16,0},{24,8},{1,17},{9,25},{17,1},{25,9},{2,18},{10... | collective-permute-start | bytes 589832 | tf_op jit(solution)/shard_map/ppermute | solution.py:239
  78.6 23.9 %collective-permute-start.30 = (bf16[384,256]{1,0:T(8,128)(2,1)S(1)}, bf16[384,256]{1,0:T(8,128)(2,1)S(1)}, u32[]{:S(2)}, u32[]{:S(2)}) collective-permute-start(bf16[384,256]{1,0:T(8,128)(2,1)S(1)} %slice.29), channel_id=1, source_target_pairs={{0,8},{8,0},{16,24},{24,16},{1,9},{9,1},{17,25},{25,17},{2,10},{10... | collective-permute-start | bytes 589832 | tf_op jit(solution)/shard_map/ppermute | solution.py:239
  78.8 1.0 copy-start.7
  79.8 1.0 copy-start.9
  80.8 1.0 copy-start.17
  81.8 0.9 copy-start.20
  83.6 15.4 %copy-start.3 = (bf16[768,256]{1,0:T(8,128)(2,1)S(1)}, bf16[768,256]{1,0:T(8,128)(2,1)}, u32[]{:S(2)}) copy-start(bf16[768,256]{1,0:T(8,128)(2,1)} %copy-done.2) | copy-start | bytes 1179652
  83.6 15.4 %copy-start.5 = (bf16[768,256]{1,0:T(8,128)(2,1)S(1)}, bf16[768,256]{1,0:T(8,128)(2,1)}, u32[]{:S(2)}) copy-start(bf16[768,256]{1,0:T(8,128)(2,1)} %copy-done.4) | copy-start | bytes 1179652
  83.6 15.4 %copy-start.15 = (bf16[768,256]{1,0:T(8,128)(2,1)S(1)}, bf16[768,256]{1,0:T(8,128)(2,1)}, u32[]{:S(2)}) copy-start(bf16[768,256]{1,0:T(8,128)(2,1)} %copy-done.14) | copy-start | bytes 1179652
  86.5 19.7 %collective-permute-start.5 = (bf16[256,128]{1,0:T(8,128)(2,1)S(1)}, bf16[256,128]{1,0:T(8,128)(2,1)S(1)}, u32[]{:S(2)}, u32[]{:S(2)}) collective-permute-start(bf16[256,128]{1,0:T(8,128)(2,1)S(1)} %get-tuple-element.25), channel_id=1, source_target_pairs={{0,0},{1,4},{2,1},{3,5},{4,2},{5,6},{6,3},{7,7},{8,8},{9,12},{10,9... | collective-permute-start | bytes 196616 | tf_op jit(solution)/shard_map/ppermute | solution.py:254
  87.2 19.7 %collective-permute-start.6 = (bf16[256,128]{1,0:T(8,128)(2,1)S(1)}, bf16[256,128]{1,0:T(8,128)(2,1)S(1)}, u32[]{:S(2)}, u32[]{:S(2)}) collective-permute-start(bf16[256,128]{1,0:T(8,128)(2,1)S(1)} %get-tuple-element.26), channel_id=1, source_target_pairs={{0,1},{1,5},{2,2},{3,6},{4,3},{5,7},{6,0},{7,4},{8,9},{9,13},{10,1... | collective-permute-start | bytes 196616 | tf_op jit(solution)/shard_map/ppermute | solution.py:254
  98.9 12.5 %copy-start.13 = (bf16[768,256]{1,0:T(8,128)(2,1)S(1)}, bf16[768,256]{1,0:T(8,128)(2,1)}, u32[]{:S(2)}) copy-start(bf16[768,256]{1,0:T(8,128)(2,1)} %copy-done.12) | copy-start | bytes 1179652
  99.0 12.4 %collective-permute-start.7 = (bf16[256,128]{1,0:T(8,128)(2,1)S(1)}, bf16[256,128]{1,0:T(8,128)(2,1)S(1)}, u32[]{:S(2)}, u32[]{:S(2)}) collective-permute-start(bf16[256,128]{1,0:T(8,128)(2,1)S(1)} %get-tuple-element.27), channel_id=1, source_target_pairs={{0,2},{1,6},{2,3},{3,7},{4,0},{5,4},{6,1},{7,5},{8,10},{9,14},{10,... | collective-permute-start | bytes 196616 | tf_op jit(solution)/shard_map/ppermute | solution.py:254
  102.6 12.5 %collective-permute-start.8 = (bf16[256,128]{1,0:T(8,128)(2,1)S(1)}, bf16[256,128]{1,0:T(8,128)(2,1)S(1)}, u32[]{:S(2)}, u32[]{:S(2)}) collective-permute-start(bf16[256,128]{1,0:T(8,128)(2,1)S(1)} %get-tuple-element.28), channel_id=1, source_target_pairs={{0,3},{1,7},{2,0},{3,4},{4,1},{5,5},{6,2},{7,6},{8,11},{9,15},{10,... | collective-permute-start | bytes 196616 | tf_op jit(solution)/shard_map/ppermute | solution.py:254
  106.2 8.8 %copy-start.23 = (bf16[256,128]{1,0:T(8,128)(2,1)}, bf16[256,128]{1,0:T(8,128)(2,1)S(1)}, u32[]{:S(2)}) copy-start(bf16[256,128]{1,0:T(8,128)(2,1)S(1)} %collective-permute-done.5.refs_0_) | copy-start | bytes 196612
  106.2 14.1 %collective-permute-start.20 = (bf16[256,128]{1,0:T(8,128)(2,1)S(1)}, bf16[256,128]{1,0:T(8,128)(2,1)S(1)}, u32[]{:S(2)}, u32[]{:S(2)}) collective-permute-start(bf16[256,128]{1,0:T(8,128)(2,1)S(1)} %get-tuple-element.34), channel_id=1, source_target_pairs={{0,0},{1,4},{2,1},{3,5},{4,2},{5,6},{6,3},{7,7},{8,8},{9,12},{10,9... | collective-permute-start | bytes 196616 | tf_op jit(solution)/shard_map/ppermute | solution.py:254
  106.9 8.1 %copy-start.25 = (bf16[256,128]{1,0:T(8,128)(2,1)}, bf16[256,128]{1,0:T(8,128)(2,1)S(1)}, u32[]{:S(2)}) copy-start(bf16[256,128]{1,0:T(8,128)(2,1)S(1)} %collective-permute-done.6.refs_1_) | copy-start | bytes 196612
  106.9 15.6 %collective-permute-start.21 = (bf16[256,128]{1,0:T(8,128)(2,1)S(1)}, bf16[256,128]{1,0:T(8,128)(2,1)S(1)}, u32[]{:S(2)}, u32[]{:S(2)}) collective-permute-start(bf16[256,128]{1,0:T(8,128)(2,1)S(1)} %get-tuple-element.35), channel_id=1, source_target_pairs={{0,1},{1,5},{2,2},{3,6},{4,3},{5,7},{6,0},{7,4},{8,9},{9,13},{10,1... | collective-permute-start | bytes 196616 | tf_op jit(solution)/shard_map/ppermute | solution.py:254
  111.3 3.7 %copy-start.27 = (bf16[256,128]{1,0:T(8,128)(2,1)}, bf16[256,128]{1,0:T(8,128)(2,1)S(1)}, u32[]{:S(2)}) copy-start(bf16[256,128]{1,0:T(8,128)(2,1)S(1)} %collective-permute-done.7.refs_2_) | copy-start | bytes 196612
  111.4 16.6 %collective-permute-start.22 = (bf16[256,128]{1,0:T(8,128)(2,1)S(1)}, bf16[256,128]{1,0:T(8,128)(2,1)S(1)}, u32[]{:S(2)}, u32[]{:S(2)}) collective-permute-start(bf16[256,128]{1,0:T(8,128)(2,1)S(1)} %get-tuple-element.36), channel_id=1, source_target_pairs={{0,2},{1,6},{2,3},{3,7},{4,0},{5,4},{6,1},{7,5},{8,10},{9,14},{10,... | collective-permute-start | bytes 196616 | tf_op jit(solution)/shard_map/ppermute | solution.py:254
  115.7 26.2 %collective-permute-start.23 = (bf16[256,128]{1,0:T(8,128)(2,1)}, bf16[256,128]{1,0:T(8,128)(2,1)S(1)}, u32[]{:S(2)}, u32[]{:S(2)}) collective-permute-start(bf16[256,128]{1,0:T(8,128)(2,1)} %get-tuple-element.37), channel_id=1, source_target_pairs={{0,3},{1,7},{2,0},{3,4},{4,1},{5,5},{6,2},{7,6},{8,11},{9,15},{10,... | collective-permute-start | bytes 196616 | tf_op jit(solution)/shard_map/ppermute | solution.py:254
  121.0 21.6 %collective-permute-start.31 = (bf16[256,128]{1,0:T(8,128)(2,1)}, bf16[256,128]{1,0:T(8,128)(2,1)S(1)}, u32[]{:S(2)}, u32[]{:S(2)}) collective-permute-start(bf16[256,128]{1,0:T(8,128)(2,1)} %get-tuple-element.39), channel_id=1, source_target_pairs={{0,0},{1,4},{2,1},{3,5},{4,2},{5,6},{6,3},{7,7},{8,8},{9,12},{10,9... | collective-permute-start | bytes 196616 | tf_op jit(solution)/shard_map/ppermute | solution.py:254
  123.1 22.1 %collective-permute-start.32 = (bf16[256,128]{1,0:T(8,128)(2,1)}, bf16[256,128]{1,0:T(8,128)(2,1)S(1)}, u32[]{:S(2)}, u32[]{:S(2)}) collective-permute-start(bf16[256,128]{1,0:T(8,128)(2,1)} %get-tuple-element.40), channel_id=1, source_target_pairs={{0,1},{1,5},{2,2},{3,6},{4,3},{5,7},{6,0},{7,4},{8,9},{9,13},{10,1... | collective-permute-start | bytes 196616 | tf_op jit(solution)/shard_map/ppermute | solution.py:254
  128.5 20.3 %collective-permute-start.33 = (bf16[256,128]{1,0:T(8,128)(2,1)}, bf16[256,128]{1,0:T(8,128)(2,1)S(1)}, u32[]{:S(2)}, u32[]{:S(2)}) collective-permute-start(bf16[256,128]{1,0:T(8,128)(2,1)} %get-tuple-element.41), channel_id=1, source_target_pairs={{0,2},{1,6},{2,3},{3,7},{4,0},{5,4},{6,1},{7,5},{8,10},{9,14},{10,... | collective-permute-start | bytes 196616 | tf_op jit(solution)/shard_map/ppermute | solution.py:254
  128.5 20.4 %collective-permute-start.34 = (bf16[256,128]{1,0:T(8,128)(2,1)}, bf16[256,128]{1,0:T(8,128)(2,1)S(1)}, u32[]{:S(2)}, u32[]{:S(2)}) collective-permute-start(bf16[256,128]{1,0:T(8,128)(2,1)} %get-tuple-element.42), channel_id=1, source_target_pairs={{0,3},{1,7},{2,0},{3,4},{4,1},{5,5},{6,2},{7,6},{8,11},{9,15},{10,... | collective-permute-start | bytes 196616 | tf_op jit(solution)/shard_map/ppermute | solution.py:254
  139.3 7.0 %copy-start.30 = (bf16[256,128]{1,0:T(8,128)(2,1)S(1)}, bf16[256,128]{1,0:T(8,128)(2,1)}, u32[]{:S(2)}) copy-start(bf16[256,128]{1,0:T(8,128)(2,1)} %copy-done.29) | copy-start | bytes 196612
  139.3 7.0 %copy-start.32 = (bf16[256,128]{1,0:T(8,128)(2,1)S(1)}, bf16[256,128]{1,0:T(8,128)(2,1)}, u32[]{:S(2)}) copy-start(bf16[256,128]{1,0:T(8,128)(2,1)} %copy-done.31) | copy-start | bytes 196612
  139.3 7.0 %copy-start.34 = (bf16[256,128]{1,0:T(8,128)(2,1)S(1)}, bf16[256,128]{1,0:T(8,128)(2,1)}, u32[]{:S(2)}) copy-start(bf16[256,128]{1,0:T(8,128)(2,1)} %copy-done.33) | copy-start | bytes 196612
  141.8 12.8 %collective-permute-start.13 = (bf16[128,128]{1,0:T(8,128)(2,1)S(1)}, bf16[128,128]{1,0:T(8,128)(2,1)S(1)}, u32[]{:S(2)}, u32[]{:S(2)}) collective-permute-start(bf16[128,128]{1,0:T(8,128)(2,1)S(1)} %shard_map.85.refs_0_), channel_id=1, source_target_pairs={{0,2},{1,3},{2,0},{3,1},{4,6},{5,7},{6,4},{7,5},{8,10},{9,11},{10,... | collective-permute-start | bytes 98312 | tf_op jit(solution)/shard_map/ppermute | solution.py:243
  142.6 13.3 %collective-permute-start.14 = (bf16[128,128]{1,0:T(8,128)(2,1)S(1)}, bf16[128,128]{1,0:T(8,128)(2,1)S(1)}, u32[]{:S(2)}, u32[]{:S(2)}) collective-permute-start(bf16[128,128]{1,0:T(8,128)(2,1)S(1)} %shard_map.85.refs_0_), channel_id=1, source_target_pairs={{0,4},{1,5},{2,6},{3,7},{4,0},{5,1},{6,2},{7,3},{8,12},{9,13},{10,... | collective-permute-start | bytes 98312 | tf_op jit(solution)/shard_map/ppermute | solution.py:243
  145.2 10.6 %collective-permute-start.15 = (bf16[128,128]{1,0:T(8,128)(2,1)S(1)}, bf16[128,128]{1,0:T(8,128)(2,1)S(1)}, u32[]{:S(2)}, u32[]{:S(2)}) collective-permute-start(bf16[128,128]{1,0:T(8,128)(2,1)S(1)} %shard_map.85.refs_0_), channel_id=1, source_target_pairs={{0,6},{1,7},{2,4},{3,5},{4,2},{5,3},{6,0},{7,1},{8,14},{9,15},{10,... | collective-permute-start | bytes 98312 | tf_op jit(solution)/shard_map/ppermute | solution.py:243
  148.8 18.1 %copy-start.18 = (bf16[1,128,1536]{2,1,0:T(8,128)(2,1)S(1)}, bf16[1,128,1536]{2,1,0:T(8,128)(2,1)}, u32[]{:S(2)}) copy-start(bf16[1,128,1536]{2,1,0:T(8,128)(2,1)} %param.11) | copy-start | bytes 1179652
  148.8 10.3 %collective-permute-start.24 = (bf16[128,128]{1,0:T(8,128)(2,1)S(1)}, bf16[128,128]{1,0:T(8,128)(2,1)S(1)}, u32[]{:S(2)}, u32[]{:S(2)}) collective-permute-start(bf16[128,128]{1,0:T(8,128)(2,1)S(1)} %shard_map.87.refs_4_), channel_id=1, source_target_pairs={{0,2},{1,3},{2,0},{3,1},{4,6},{5,7},{6,4},{7,5},{8,10},{9,11},{10,... | collective-permute-start | bytes 98312 | tf_op jit(solution)/shard_map/ppermute | solution.py:243
  148.9 11.4 %collective-permute-start.25 = (bf16[128,128]{1,0:T(8,128)(2,1)S(1)}, bf16[128,128]{1,0:T(8,128)(2,1)S(1)}, u32[]{:S(2)}, u32[]{:S(2)}) collective-permute-start(bf16[128,128]{1,0:T(8,128)(2,1)S(1)} %shard_map.87.refs_4_), channel_id=1, source_target_pairs={{0,4},{1,5},{2,6},{3,7},{4,0},{5,1},{6,2},{7,3},{8,12},{9,13},{10,... | collective-permute-start | bytes 98312 | tf_op jit(solution)/shard_map/ppermute | solution.py:243
  154.7 5.9 %collective-permute-start.26 = (bf16[128,128]{1,0:T(8,128)(2,1)S(1)}, bf16[128,128]{1,0:T(8,128)(2,1)S(1)}, u32[]{:S(2)}, u32[]{:S(2)}) collective-permute-start(bf16[128,128]{1,0:T(8,128)(2,1)S(1)} %shard_map.87.refs_4_), channel_id=1, source_target_pairs={{0,6},{1,7},{2,4},{3,5},{4,2},{5,3},{6,0},{7,1},{8,14},{9,15},{10,... | collective-permute-start | bytes 98312 | tf_op jit(solution)/shard_map/ppermute | solution.py:243
  155.8 5.1 %collective-permute-start.35 = (bf16[128,128]{1,0:T(8,128)(2,1)S(1)}, bf16[128,128]{1,0:T(8,128)(2,1)S(1)}, u32[]{:S(2)}, u32[]{:S(2)}) collective-permute-start(bf16[128,128]{1,0:T(8,128)(2,1)S(1)} %shard_map.89.refs_8_), channel_id=1, source_target_pairs={{0,2},{1,3},{2,0},{3,1},{4,6},{5,7},{6,4},{7,5},{8,10},{9,11},{10,... | collective-permute-start | bytes 98312 | tf_op jit(solution)/shard_map/ppermute | solution.py:243
  155.8 5.2 %collective-permute-start.36 = (bf16[128,128]{1,0:T(8,128)(2,1)S(1)}, bf16[128,128]{1,0:T(8,128)(2,1)S(1)}, u32[]{:S(2)}, u32[]{:S(2)}) collective-permute-start(bf16[128,128]{1,0:T(8,128)(2,1)S(1)} %shard_map.89.refs_8_), channel_id=1, source_target_pairs={{0,4},{1,5},{2,6},{3,7},{4,0},{5,1},{6,2},{7,3},{8,12},{9,13},{10,... | collective-permute-start | bytes 98312 | tf_op jit(solution)/shard_map/ppermute | solution.py:243
  159.2 5.8 %collective-permute-start.37 = (bf16[128,128]{1,0:T(8,128)(2,1)S(1)}, bf16[128,128]{1,0:T(8,128)(2,1)S(1)}, u32[]{:S(2)}, u32[]{:S(2)}) collective-permute-start(bf16[128,128]{1,0:T(8,128)(2,1)S(1)} %shard_map.89.refs_8_), channel_id=1, source_target_pairs={{0,6},{1,7},{2,4},{3,5},{4,2},{5,3},{6,0},{7,1},{8,14},{9,15},{10,... | collective-permute-start | bytes 98312 | tf_op jit(solution)/shard_map/ppermute | solution.py:243
  160.3 6.6 %collective-permute-start.38 = (bf16[4,128,128]{2,1,0:T(8,128)(2,1)S(1)}, bf16[4,128,128]{2,1,0:T(8,128)(2,1)S(1)}, u32[]{:S(2)}, u32[]{:S(2)}) collective-permute-start(bf16[4,128,128]{2,1,0:T(8,128)(2,1)S(1)} %pad_maximum_fusion), channel_id=1, source_target_pairs={{0,1},{1,0},{2,3},{3,2},{4,5},{5,4},{6,7},{7,6},{8,9},{9,8},{10,11... | collective-permute-start | bytes 393224 | tf_op jit(solution)/shard_map/ppermute | solution.py:246
  160.6 6.3 %collective-permute-start.39 = (bf16[4,128,128]{2,1,0:T(8,128)(2,1)S(1)}, bf16[4,128,128]{2,1,0:T(8,128)(2,1)S(1)}, u32[]{:S(2)}, u32[]{:S(2)}) collective-permute-start(bf16[4,128,128]{2,1,0:T(8,128)(2,1)S(1)} %pad_maximum_fusion.1), channel_id=1, source_target_pairs={{0,1},{1,0},{2,3},{3,2},{4,5},{5,4},{6,7},{7,6},{8,9},{9,8},{10,11... | collective-permute-start | bytes 393224 | tf_op jit(solution)/shard_map/ppermute | solution.py:246
  165.0 2.0 %collective-permute-start.40 = (bf16[4,128,128]{2,1,0:T(8,128)(2,1)S(1)}, bf16[4,128,128]{2,1,0:T(8,128)(2,1)S(1)}, u32[]{:S(2)}, u32[]{:S(2)}) collective-permute-start(bf16[4,128,128]{2,1,0:T(8,128)(2,1)S(1)} %pad_maximum_fusion.2), channel_id=1, source_target_pairs={{0,1},{1,0},{2,3},{3,2},{4,5},{5,4},{6,7},{7,6},{8,9},{9,8},{10,11... | collective-permute-start | bytes 393224 | tf_op jit(solution)/shard_map/ppermute | solution.py:246
  (15 other events, 11.1 us)

commit v2 on v1

v2 whole, which is shorter than its diff:
```python
import math

import jax
import jax.numpy as jnp
from jax import lax
from jax.experimental import pallas as pl
from jax.experimental.pallas import tpu as pltpu
from jax.sharding import PartitionSpec as P

HD = 128
TILE = 128
GROUPS = 4
BF = jnp.bfloat16
F32 = jnp.float32
MIB = 1024 * 1024

SMEM_SPEC = pl.BlockSpec(memory_space=pltpu.SMEM)
ANY_SPEC = pl.BlockSpec(memory_space=pl.ANY)


def call(kernel, out_shape, scalars, arrays, scratch=(), limit=4, aliases=None):
    many = isinstance(out_shape, (list, tuple))
    return pl.pallas_call(
        kernel,
        out_shape=out_shape,
        in_specs=[SMEM_SPEC] * len(scalars) + [ANY_SPEC] * len(arrays),
        out_specs=[ANY_SPEC] * len(out_shape) if many else ANY_SPEC,
        scratch_shapes=list(scratch),
        input_output_aliases=aliases or {},
        compiler_params=pltpu.CompilerParams(vmem_limit_bytes=limit * MIB),
        cost_estimate=pl.CostEstimate(flops=0, bytes_accessed=0, transcendentals=0),
    )(*scalars, *arrays)


def stays(x):
    return pltpu.with_memory_space_constraint(x, pltpu.HBM)


def run_all(copies):
    for copy in copies:
        copy.start()
    for copy in copies:
        copy.wait()


def after(x, *events):
    def kernel(*refs):
        pass

    return call(kernel, jax.ShapeDtypeStruct(x.shape, x.dtype), [], [x, *events], aliases={0: 0})


def pack_weights(core, w_query, heads, per_group, events=()):
    rows, columns = w_query.shape
    half = columns // 2
    width = len(heads) * HD
    assert heads == list(range(heads[0], heads[0] + len(heads)))

    def kernel(core_ref, w_ref, *refs):
        out, buf, sem, out_sem = refs[-4:]
        copies = []
        for hi in range(2):
            at = pl.multiple_of(core_ref[0] * half + (hi * per_group + heads[0]) * HD, HD)
            copies.append(
                pltpu.make_async_copy(
                    w_ref.at[:, pl.ds(at, width)], buf.at[:, hi * width : (hi + 1) * width], sem.at[hi]
                )
            )
        run_all(copies)
        run_all([pltpu.make_async_copy(buf, out, out_sem)])

    return call(
        kernel,
        jax.ShapeDtypeStruct((rows, 2 * width), BF),
        [core],
        [stays(w_query), *events],
        [pltpu.VMEM((rows, 2 * width), BF), pltpu.SemaphoreType.DMA((2,)), pltpu.SemaphoreType.DMA],
    )


def pack_caches(key_block, value_block, events=()):
    branches, tokens, columns = key_block.shape
    width = columns // GROUPS

    def kernel(k_ref, v_ref, *refs):
        out, buf, sem, out_sem = refs[-4:]
        copies = []
        for n, ref in enumerate((k_ref, v_ref)):
            for g in range(GROUPS):
                copies.append(
                    pltpu.make_async_copy(
                        ref.at[:, :, g * width : (g + 1) * width], buf.at[g, n], sem.at[n * GROUPS + g]
                    )
                )
        run_all(copies)
        run_all([pltpu.make_async_copy(buf, out, out_sem)])

    shape = (GROUPS, 2, branches, tokens, width)
    return call(
        kernel,
        jax.ShapeDtypeStruct(shape, BF),
        [],
        [stays(key_block), stays(value_block), *events],
        [pltpu.VMEM(shape, BF), pltpu.SemaphoreType.DMA((2 * GROUPS,)), pltpu.SemaphoreType.DMA],
    )


def halves(by_x, by_y, events=()):
    rows, width = by_x.shape
    half = rows // 2

    def kernel(x_ref, y_ref, *refs):
        first, last, buf, sem, out_sem = refs[-5:]
        sources = (x_ref.at[:half], y_ref.at[half:])
        run_all([pltpu.make_async_copy(ref, buf.at[n], sem.at[n]) for n, ref in enumerate(sources)])
        run_all([pltpu.make_async_copy(buf.at[n], ref, out_sem.at[n]) for n, ref in enumerate((first, last))])

    return call(
        kernel,
        [jax.ShapeDtypeStruct((half, width), BF)] * 2,
        [],
        [by_x, by_y, *events],
        [
            pltpu.VMEM((2, half, width), BF),
            pltpu.SemaphoreType.DMA((2,)),
            pltpu.SemaphoreType.DMA((2,)),
        ],
    )


def stack(pieces, events=()):
    shape = (sum(p.shape[0] for p in pieces), *pieces[0].shape[1:])

    def kernel(*refs):
        out, buf, sem, out_sem = refs[-4:]
        copies, at = [], 0
        for n, piece in enumerate(pieces):
            copies.append(pltpu.make_async_copy(refs[n], buf.at[at : at + piece.shape[0]], sem.at[n]))
            at += piece.shape[0]
        run_all(copies)
        run_all([pltpu.make_async_copy(buf, out, out_sem)])

    return call(
        kernel,
        jax.ShapeDtypeStruct(shape, BF),
        [],
        [*pieces, *events],
        [pltpu.VMEM(shape, BF), pltpu.SemaphoreType.DMA((len(pieces),)), pltpu.SemaphoreType.DMA],
    )


def project(scalars, own, other, pieces, places, before=None, events=()):
    branches, rows, depth = own.shape
    chunk = depth // 4
    width = pieces[0].shape[1]
    part = width // 2
    count = len(pieces)
    sizes = [p.shape[0] for p in pieces]
    last = before is not None
    outs = 4 if last else 1

    def kernel(s_ref, own_ref, other_ref, *refs):
        w_refs = refs[:count]
        h_buf, w_buf, t_buf, q_buf, sem, out_sem = refs[-6:]
        out_refs = refs[-6 - outs : -6]
        image = s_ref[0]
        columns = [
            pl.ds(pl.multiple_of((image ^ m) * chunk + row, HD), size) for (m, row), size in zip(places, sizes)
        ]
        firsts = [sum(sizes[:n]) for n in range(count)]
        loads = []
        for n in range(count):
            here = pl.ds(firsts[n], sizes[n])
            loads.append([pltpu.make_async_copy(w_refs[n], w_buf.at[here], sem.at[n, 2])])
            for slot in range(2):
                mine, theirs = [
                    pltpu.make_async_copy(ref.at[:, :, columns[n]], h_buf.at[slot, :, :, here], sem.at[n, slot])
                    for ref in (own_ref, other_ref)
                ]
                loads[n].append(mine)

                @pl.when(s_ref[2 + slot] == 1)
                def _():
                    mine.start()

                @pl.when(s_ref[2 + slot] != 1)
                def _():
                    theirs.start()

            loads[n][0].start()
        if last:
            sums = pltpu.make_async_copy(refs[count], t_buf, out_sem.at[0])
            sums.start()
        total = [jnp.zeros((branches * rows, width), F32) for _ in range(2)]
        for n in range(count):
            here = slice(firsts[n], firsts[n] + sizes[n])
            for load in loads[n]:
                load.wait()
            for slot in range(2):
                total[slot] = total[slot] + jnp.dot(
                    h_buf[slot, :, :, here].reshape(branches * rows, sizes[n]),
                    w_buf[here],
                    preferred_element_type=F32,
                )
        if last:
            sums.wait()
            for slot in range(2):
                done = (t_buf[slot] + total[slot]).astype(BF)
                for hi in range(2):
                    q_buf[hi * 2 + slot] = done[:, hi * part : (hi + 1) * part]
            run_all(
                [
                    pltpu.make_async_copy(q_buf.at[(s_ref[1] + r) % 4], out, out_sem.at[r])
                    for r, out in enumerate(out_refs)
                ]
            )
        else:
            for slot in range(2):
                t_buf[slot] = total[slot]
            run_all([pltpu.make_async_copy(t_buf, out_refs[0], out_sem.at[0])])

    sums = (2, branches * rows, width)
    return call(
        kernel,
        [jax.ShapeDtypeStruct((branches * rows, part), BF)] * 4 if last else jax.ShapeDtypeStruct(sums, F32),
        [scalars],
        [own, other, *pieces, *([before] if last else []), *events],
        [
            pltpu.VMEM((2, branches, rows, sum(sizes)), BF),
            pltpu.VMEM((sum(sizes), width), BF),
            pltpu.VMEM(sums, F32),
            pltpu.VMEM((4, branches * rows, part), BF),
            pltpu.SemaphoreType.DMA((count, 3)),
            pltpu.SemaphoreType.DMA((4,)),
        ],
        limit=16,
    )


def attend(scalars, guide, queries, caches, first_head, events=()):
    rows, width = queries[0].shape[0] // 2, queries[0].shape[1]
    scale = 1.0 / math.sqrt(HD)
    count, kept = len(queries), len(caches)
    here = slice(first_head * HD, first_head * HD + width)
    sizes = [c.shape[0] * c.shape[3] for c in caches]
    keys_all = sum(sizes)

    def kernel(s_ref, g_ref, *refs):
        q_refs, c_refs = refs[:count], refs[count : count + kept]
        out, q_buf, c_bufs, out_buf, sem = refs[-4 - kept], refs[-3 - kept], refs[-2 - kept : -2], refs[-2], refs[-1]
        for r in range(count):

            @pl.when(s_ref[0] == r)
            def _():
                pltpu.make_async_copy(q_refs[r], q_buf, sem.at[0]).start()

        loads = [
            pltpu.make_async_copy(c_ref.at[:, n, :, :, here], c_buf.at[n], sem.at[1 + 2 * i + n])
            for n in range(2)
            for i, (c_ref, c_buf) in enumerate(zip(c_refs, c_bufs))
        ]
        for load in loads:
            load.start()
        pltpu.make_async_copy(q_refs[0], q_buf, sem.at[0]).wait()
        for load in loads[:kept]:
            load.wait()
        for head in range(width // HD):
            at = slice(head * HD, (head + 1) * HD)
            attended = []
            for b in range(2):
                q = q_buf[b * rows : (b + 1) * rows, at]
                scores = [
                    lax.dot_general(
                        q,
                        c_buf[0, :, b, :, at].reshape(size, HD),
                        (((1,), (1,)), ((), ())),
                        preferred_element_type=F32,
                    )
                    * scale
                    for c_buf, size in zip(c_bufs, sizes)
                ]
                top = jnp.max(scores[0], axis=-1, keepdims=True)
                for s in scores[1:]:
                    top = jnp.maximum(top, jnp.max(s, axis=-1, keepdims=True))
                exps = [jnp.exp(s - top) for s in scores]
                total = jnp.sum(exps[0], axis=-1, keepdims=True)
                for e in exps[1:]:
                    total = total + jnp.sum(e, axis=-1, keepdims=True)
                over = 1.0 / total
                if head == 0 and b == 0:
                    for load in loads[kept:]:
                        load.wait()
                result = jnp.zeros((rows, HD), F32)
                for e, c_buf, size in zip(exps, c_bufs, sizes):
                    w = (e * over).astype(BF)
                    result = result + jnp.dot(
                        w, c_buf[1, :, b, :, at].reshape(size, HD), preferred_element_type=F32
                    )
                attended.append(result)
            guided = attended[1] + g_ref[0] * (attended[0] - attended[1])
            out_buf[:, at] = guided.astype(BF)
        run_all([pltpu.make_async_copy(out_buf, out, sem.at[0])])

    return call(
        kernel,
        jax.ShapeDtypeStruct((rows, width), BF),
        [scalars, guide],
        [*queries, *caches, *events],
        [pltpu.VMEM((2 * rows, width), BF)]
        + [pltpu.VMEM((2, c.shape[0], c.shape[2], c.shape[3], width), BF) for c in caches]
        + [pltpu.VMEM((rows, width), BF), pltpu.SemaphoreType.DMA((1 + 2 * kept,))],
        limit=16 + 8 * (keys_all // 1024),
    )


def paste(scalars, previous, mine, others, firsts, per_group):
    rows, columns = previous.shape
    flat = [piece for part in mine for piece in part]
    rest = [piece for other in others for piece in other]
    parts = len(firsts)

    def kernel(s_ref, prev_ref, *refs):
        out, buf, sem, out_sem = refs[-4:]

        def place(k, m, width):
            at = pl.multiple_of(((s_ref[0] ^ m) * per_group + firsts[k]) * HD, HD)
            return buf.at[:, pl.ds(at, width)]

        taken = s_ref[1]
        for n in range(len(others)):
            taken = taken + s_ref[2 + n]

        @pl.when(taken == 0)
        def _():
            run_all([pltpu.make_async_copy(prev_ref, buf, sem.at[0])])

        @pl.when(s_ref[1] == 1)
        def _():
            copies = []
            for k in range(parts):
                for m in range(GROUPS):
                    piece = refs[k * GROUPS + m]
                    copies.append(
                        pltpu.make_async_copy(piece, place(k, m, piece.shape[1]), sem.at[k * GROUPS + m])
                    )
            run_all(copies)

        for n in range(len(others)):

            @pl.when(s_ref[2 + n] == 1)
            def _():
                copies = []
                for k in range(parts):
                    piece = refs[parts * GROUPS + n * parts + k]
                    for m in range(GROUPS):
                        copies.append(
                            pltpu.make_async_copy(
                                piece.at[m], place(k, m, piece.shape[2]), sem.at[k * GROUPS + m]
                            )
                        )
                run_all(copies)

        run_all([pltpu.make_async_copy(buf, out, out_sem)])

    return call(
        kernel,
        jax.ShapeDtypeStruct((rows, columns), BF),
        [scalars],
        [stays(previous), *flat, *rest],
        [
            pltpu.VMEM((rows, columns), BF),
            pltpu.SemaphoreType.DMA((parts * GROUPS,)),
            pltpu.SemaphoreType.DMA,
        ],
    )


def body(hidden, key_cache, value_cache, cached_out, w_query, guide, masked_tiles, mask_count):
    images = lax.axis_size("image")
    tokens = lax.axis_size("token")
    heads = key_cache.shape[3] // HD
    per_group = heads // GROUPS
    slots = masked_tiles.shape[1]
    layers = tokens // (2 * GROUPS)
    assert images == 4 and hidden.shape[1] == 1 and hidden.shape[2] == TILE
    assert tokens == layers * 2 * GROUPS and slots == 2 * layers and heads == per_group * GROUPS

    image = lax.axis_index("image")
    token = lax.axis_index("token")
    core = token % 2
    chip = token // 2
    z = chip // layers
    layer = chip % layers
    tiles = masked_tiles[0]

    def over_image(x, m):
        return lax.ppermute(x, "image", [(i, i ^ m) for i in range(images)])

    def over_z(x, m):
        span = 2 * layers
        return lax.ppermute(x, "token", [(t, ((t // span) ^ m) * span + t % span) for t in range(tokens)])

    def over_core(x):
        return lax.ppermute(x, "token", [(t, t ^ 1) for t in range(tokens)])

    def to_targets(x, r):
        pairs = []
        for t in range(tokens):
            c, at, s = t % 2, (t // 2) % layers, t // 2 // layers
            goal = (s + r) % 4
            pairs.append((t, ((2 * c + goal // 2) * layers + at) * 2 + goal % 2))
        return lax.ppermute(x, "token", pairs)

    layer_groups = [
        [(s * layers + at) * 2 + c for at in range(layers)] for s in range(GROUPS) for c in range(2)
    ]
    group_groups = [list(range(s * layers * 2, (s + 1) * layers * 2)) for s in range(GROUPS)]
    z_groups = [[s * 2 * layers + at for s in range(GROUPS)] for at in range(2 * layers)]

    plan = [list(range(per_group))]
    parts = len(plan)
    firsts = [p[0] for p in plan]
    half = w_query.shape[0] // 2
    near_places = [(0, 0), (1, 0), (2, 0)]
    far_places = [(3, 0), (3, half)]

    own_hidden = hidden[:, 0]
    other_hidden = over_core(own_hidden)

    def near(k, *events):
        own = pack_weights(core[None], w_query, plan[k], per_group, events)
        return [own, over_image(own, 1), over_image(own, 2)]

    def far(k, *events):
        first, last = halves(weights[k][1], weights[k][2], events)
        return [over_image(first, 2), over_image(last, 1)], first

    my_slot = layer * 2 + core
    my_tile = tiles[my_slot]
    target = 2 * (z % 2) + core
    owner_z = my_tile // 2 // layers
    choice = (target - owner_z) % 4

    def scalars_of(at):
        pair = tiles[2 * at : 2 * at + 2]
        return jnp.concatenate([jnp.stack([image, z]).astype(jnp.int32), (pair % 2 == core).astype(jnp.int32)])

    def begin(k, *events):
        return [
            project(scalars_of(at), own_hidden, other_hidden, weights[k], near_places, events=events)
            for at in range(layers)
        ]

    def finish(k, sums, came_far, *events):
        result = None
        for at in range(layers):
            sent = project(
                scalars_of(at), own_hidden, other_hidden, came_far, far_places, sums[at], events=events
            )
            came = [to_targets(x, r) for r, x in enumerate(sent)]
            if layers > 1:
                holds = (tiles[2 * at + core] // 2) % layers == layer
                came = [
                    lax.psum(jnp.where(holds, x, jnp.zeros_like(x)), "token", axis_index_groups=layer_groups)
                    for x in came
                ]
            if result is None:
                result = came
            else:
                result = [jnp.where(layer == at, new, old) for new, old in zip(came, result)]
        return result, sent[0]

    weights = [near(0)]

    blocks = pack_caches(key_cache[:, 0], value_cache[:, 0], weights[0][:1])
    gathered = lax.all_to_all(blocks, "token", 0, 0, axis_index_groups=z_groups)

    far_0, event = far(0, blocks)
    sums_0 = begin(0, event)
    queries_0, event = finish(0, sums_0, far_0)
    queries = [queries_0]

    gathered = after(gathered, event)
    if layers == 1:
        caches = [gathered, over_core(gathered)]
    else:
        everyone = lax.all_gather(gathered, "token", axis_index_groups=group_groups)
        caches = [everyone.reshape(-1, *gathered.shape[1:])]

    mine, others = [], []
    for k in range(parts):
        guided = attend(choice[None], guide, queries[k], caches, firsts[k])
        pieces = [guided] + [over_z(guided, m) for m in range(1, GROUPS)]
        mine.append(pieces)
        stacked = stack([p[None] for p in pieces])
        if layers == 1:
            others.append([over_core(stacked)])
        else:
            everyone = lax.all_gather(stacked, "token", axis_index_groups=group_groups)
            others.append([everyone[n] for n in range(slots)])

    in_use = jnp.arange(slots, dtype=jnp.int32) < mask_count[0]
    hit = ((tiles == token) & in_use).astype(jnp.int32)
    own_hit = hit[my_slot]
    other_hits = hit[1 - core][None] if layers == 1 else jnp.where(jnp.arange(slots) == my_slot, 0, hit)
    flags = jnp.concatenate([jnp.stack([z, own_hit]).astype(jnp.int32), other_hits])
    by_other = [[others[k][n] for k in range(parts)] for n in range(len(others[0]))]
    edited = paste(flags, cached_out[0], mine, by_other, firsts, per_group)
    return edited[None]


def solution(mesh):
    return jax.shard_map(
        body,
        mesh=mesh,
        in_specs=(
            P(None, "image", "token", None),
            P(None, "image", "token", None),
            P(None, "image", "token", None),
            P("image", "token", None),
            P("image", None),
            P("image"),
            P("image", None),
            P("image"),
        ),
        out_specs=P("image", "token", None),
        check_vma=False,
    )
```

time: 169 us -> 103 us (0.61)
  starting transfers between devices: 70.6 us -> 26.4 us
  local copies, waits for them, and re-layouts: 23.7 us -> 5.22 us
  waiting for transfers between devices: 48.8 us -> 44.2 us
    ppermute x12 -> x4, starting transfers between devices: 35.5 us -> 10.2 us  [to_targets(): return lax.ppermute(x, 'token', pairs)]
    ppermute x12 -> x3, waiting for transfers between devices: 31.3 us -> 6.9 us  [over_z(): lax.ppermute(x, 'token', [(t, (t // span ^ m) * span + t % span) for t in...]
    unnamed x79 -> x12, local copies, waits for them, and re-layouts: 19.3 us -> 3.96 us
    ppermute x12 -> x3, starting transfers between devices: 19.1 us -> 4.55 us  [over_z(): lax.ppermute(x, 'token', [(t, (t // span ^ m) * span + t % span) for t in...]
    ppermute x12 -> x4, waiting for transfers between devices: 17.4 us -> 29.7 us  [over_image(): return lax.ppermute(x, 'image', [(i, i ^ m) for i in range(images)])]
    ppermute x12 -> x4, starting transfers between devices: 15.5 us -> 5.23 us  [over_image(): return lax.ppermute(x, 'image', [(i, i ^ m) for i in range(images)])]
    ppermute x12 -> x4, waiting for transfers between devices: 0.03 us -> 7.52 us  [to_targets(): return lax.ppermute(x, 'token', pairs)]
    all_to_all x0 -> x1, starting transfers between devices: none -> 6.33 us  [body(): gathered = lax.all_to_all(blocks, 'token', 0, 0, axis_index_groups=z_groups)]
  transfers between devices with their start and end apart: 41 -> 15, of which waited for: 9 -> 9; matrix products, arithmetic and copies ran while one was open for 4% -> 3% of each run, Pallas kernels for 10% -> 10%
where the time goes in v2:
time: 103 us; the launch traced here: 102 us
  waiting for transfers between devices  44.2 us (43%)
  starting transfers between devices  26.4 us (26%)
  Pallas kernels  20.6 us (20%)
  local copies, waits for them, and re-layouts  5.22 us (5%)
  between operations  3.78 us (4%)
  other arithmetic  1.5 us (1%)
    ppermute x4, waiting for transfers between devices, over_image(): return lax.ppermute(x, 'image', [(i, i ^ m) for i in range(images)])  29.7 us
    pallas_call x9, Pallas kernels, call(): pl.pallas_call(kernel, out_shape=out_shape, in_specs=[SMEM_SPEC] * len(sc...  20.6 us
    ppermute x4, starting transfers between devices, to_targets(): return lax.ppermute(x, 'token', pairs)  10.2 us
    ppermute x4, waiting for transfers between devices, to_targets(): return lax.ppermute(x, 'token', pairs)  7.52 us
    ppermute x3, waiting for transfers between devices, over_z(): lax.ppermute(x, 'token', [(t, (t // span ^ m) * span + t % span) for t in...  6.9 us
    all_to_all x1, starting transfers between devices, body(): gathered = lax.all_to_all(blocks, 'token', 0, 0, axis_index_groups=z_groups)  6.33 us
    ppermute x4, starting transfers between devices, over_image(): return lax.ppermute(x, 'image', [(i, i ^ m) for i in range(images)])  5.23 us
    ppermute x3, starting transfers between devices, over_z(): lax.ppermute(x, 'token', [(t, (t // span ^ m) * span + t % span) for t in...  4.55 us
  transfers between devices with their start and end apart: 15, of which 9 were waited for; matrix products, arithmetic and copies ran while one was open for 3% of the time, Pallas kernels for 10%

profile of v2, /device:TPU:0, one launch (start us, length us, event | category | flops | bytes accessed | tf_op | source)
XLA Modules:
  0.0 101.7 jit_solution(17883458640891778000)
XLA Ops:
  0.0 1.5 %shard_map.82.refs_0_ = bf16[768,768]{1,0:T(8,128)(2,1)S(1)} custom-call(s32[1]{0:T(128)} %bitcast.8.core_ref, bf16[768,1536]{1,0:T(8,128)(2,1)} %w_ref.1), custom_call_target="tpu_custom_call" | custom-call | tf_op jit(solution)/shard_map/pallas_call | solution.py:23
  1.5 2.7 %shard_map.83.refs_0_ = bf16[4,2,2,128,384]{4,3,2,1,0:T(8,128)(2,1)} custom-call(bf16[2,128,1536]{2,1,0:T(8,128)(2,1)} %bitcast.26, bf16[2,128,1536]{2,1,0:T(8,128)(2,1)} %bitcast.27, bf16[768,768]{1,0:T(8,128)(2,1)S(1)} %shard_map.82.refs_0_), custom_call_target="tpu_custom_call" | custom-call | tf_op jit(solution)/shard_map/pallas_call | solution.py:23
  4.2 6.3 %all-to-all-start = ((bf16[4,2,2,128,384]{4,3,2,1,0:T(8,128)(2,1)}), bf16[4,2,2,128,384]{4,3,2,1,0:T(8,128)(2,1)S(1)}, u32[]{:S(2)}, u32[]{:S(2)}) async-start(bf16[4,2,2,128,384]{4,3,2,1,0:T(8,128)(2,1)} %shard_map.83.refs_0_), calls=%async_computation | async-start | bytes 3145728 | tf_op jit(solution)/shard_map/all_to_all | solution.py:476
  10.6 1.5 %collective-permute-start.1 = (bf16[768,768]{1,0:T(8,128)(2,1)S(1)}, bf16[768,768]{1,0:T(8,128)(2,1)S(1)}, u32[]{:S(2)}, u32[]{:S(2)}) collective-permute-start(bf16[768,768]{1,0:T(8,128)(2,1)S(1)} %shard_map.82.refs_0_), channel_id=1, source_target_pairs={{0,8},{8,0},{16,24},{24,16},{1,9},{9,1},{17,25},{25,17},{2,10},{10... | collective-permute-start | bytes 3538952 | tf_op jit(solution)/shard_map/ppermute | solution.py:397
  12.1 1.5 %collective-permute-start.2 = (bf16[768,768]{1,0:T(8,128)(2,1)S(1)}, bf16[768,768]{1,0:T(8,128)(2,1)S(1)}, u32[]{:S(2)}, u32[]{:S(2)}) collective-permute-start(bf16[768,768]{1,0:T(8,128)(2,1)S(1)} %shard_map.82.refs_0_), channel_id=1, source_target_pairs={{0,16},{8,24},{16,0},{24,8},{1,17},{9,25},{17,1},{25,9},{2,18},{10... | collective-permute-start | bytes 3538952 | tf_op jit(solution)/shard_map/ppermute | solution.py:397
  13.6 0.0 copy-start.5
  13.6 0.0 collective-permute-start
  13.6 24.4 %collective-permute-done.1.x_ref.refs_1_ = bf16[768,768]{1,0:T(8,128)(2,1)S(1)} collective-permute-done((bf16[768,768]{1,0:T(8,128)(2,1)S(1)}, bf16[768,768]{1,0:T(8,128)(2,1)S(1)}, u32[]{:S(2)}, u32[]{:S(2)}) %collective-permute-start.1) | collective-permute-done | bytes 1179680 | tf_op jit(solution)/shard_map/ppermute | solution.py:397
  38.0 0.0 copy-start.1
  38.0 1.2 %collective-permute-done.2.y_ref.refs_2_ = bf16[768,768]{1,0:T(8,128)(2,1)S(1)} collective-permute-done((bf16[768,768]{1,0:T(8,128)(2,1)S(1)}, bf16[768,768]{1,0:T(8,128)(2,1)S(1)}, u32[]{:S(2)}, u32[]{:S(2)}) %collective-permute-start.2) | collective-permute-done | bytes 1179680 | tf_op jit(solution)/shard_map/ppermute | solution.py:397
  39.2 0.0 copy-start.3
  39.2 1.5 %shard_map.84 = (bf16[384,768]{1,0:T(8,128)(2,1)}, bf16[384,768]{1,0:T(8,128)(2,1)}) custom-call(bf16[768,768]{1,0:T(8,128)(2,1)S(1)} %collective-permute-done.1.x_ref.refs_1_, bf16[768,768]{1,0:T(8,128)(2,1)S(1)} %collective-permute-done.2.y_ref.refs_2_, bf16[4,2,2,128,384]{4,3,2,1,0:T(8,128)(2,1)} %shard_map.83.refs_0_), custom_call_target="tpu_custom_call" | custom-call | tf_op jit(solution)/shard_map/pallas_call | solution.py:23
  40.7 0.0 copy-done.1
  40.7 0.0 copy-done.3
  40.7 1.6 %collective-permute-start.3 = (bf16[384,768]{1,0:T(8,128)(2,1)}, bf16[384,768]{1,0:T(8,128)(2,1)S(1)}, u32[]{:S(2)}, u32[]{:S(2)}) collective-permute-start(bf16[384,768]{1,0:T(8,128)(2,1)} %get-tuple-element.11.refs_3_), channel_id=1, source_target_pairs={{0,16},{8,24},{16,0},{24,8},{1,17},{9,25},{17,1},{25,9},{2,18},{10... | collective-permute-start | bytes 1769480 | tf_op jit(solution)/shard_map/ppermute | solution.py:397
  42.3 0.6 collective-permute-start.4
  43.6 0.0 copy-done.5
  43.6 0.1 pad_add_fusion.1.s_ref
  43.7 0.0 collective-permute-done.other_ref
  43.7 0.0 copy-start
  43.7 1.4 %copy-done = bf16[2,1,128,3072]{3,2,1,0:T(8,128)(2,1)S(1)} copy-done((bf16[2,1,128,3072]{3,2,1,0:T(8,128)(2,1)S(1)}, bf16[2,1,128,3072]{3,2,1,0:T(8,128)(2,1)}, u32[]{:S(2)}) %copy-start) | copy-done | bytes 1572888
  45.1 0.0 copy-start.2
  45.1 1.3 %copy-done.2 = bf16[768,768]{1,0:T(8,128)(2,1)S(1)} copy-done((bf16[768,768]{1,0:T(8,128)(2,1)S(1)}, bf16[768,768]{1,0:T(8,128)(2,1)}, u32[]{:S(2)}) %copy-start.2) | copy-done | bytes 1179672
  46.4 0.0 copy-start.4
  46.4 1.3 %copy-done.4 = bf16[768,768]{1,0:T(8,128)(2,1)S(1)} copy-done((bf16[768,768]{1,0:T(8,128)(2,1)S(1)}, bf16[768,768]{1,0:T(8,128)(2,1)}, u32[]{:S(2)}) %copy-start.4) | copy-done | bytes 1179672
  47.6 4.2 %shard_map.85.refs_2_ = f32[2,256,768]{2,1,0:T(8,128)S(1)} custom-call(s32[4]{0:T(128)S(1)} %pad_add_fusion.1.s_ref, bf16[2,128,3072]{2,1,0:T(8,128)(2,1)S(1)} %bitcast.20, bf16[2,128,3072]{2,1,0:T(8,128)(2,1)} %collective-permute-done.other_ref, bf16[768,768]{1,0:T(8,128)(2,1)S(1)} %shard_map.82.refs_0_, bf16[768,768]{1,0:T(8,128)(2,1)S(1)} %copy-done.2, ...), custom_call_target="tpu_custom_call" | custom-call | tf_op jit(solution)/shard_map/pallas_call | solution.py:23
  51.8 2.7 %collective-permute-done.3.refs_0_ = bf16[384,768]{1,0:T(8,128)(2,1)S(1)} collective-permute-done((bf16[384,768]{1,0:T(8,128)(2,1)}, bf16[384,768]{1,0:T(8,128)(2,1)S(1)}, u32[]{:S(2)}, u32[]{:S(2)}) %collective-permute-start.3) | collective-permute-done | bytes 589856 | tf_op jit(solution)/shard_map/ppermute | solution.py:397
  54.6 1.3 %collective-permute-done.4.refs_1_ = bf16[384,768]{1,0:T(8,128)(2,1)} collective-permute-done((bf16[384,768]{1,0:T(8,128)(2,1)}, bf16[384,768]{1,0:T(8,128)(2,1)}, u32[]{:S(2)}, u32[]{:S(2)}) %collective-permute-start.4) | collective-permute-done | bytes 589856 | tf_op jit(solution)/shard_map/ppermute | solution.py:397
  55.9 4.2 %shard_map.86 = (bf16[256,384]{1,0:T(8,128)(2,1)S(1)}, bf16[256,384]{1,0:T(8,128)(2,1)}, bf16[256,384]{1,0:T(8,128)(2,1)}, bf16[256,384]{1,0:T(8,128)(2,1)}) custom-call(s32[4]{0:T(128)S(1)} %pad_add_fusion.1.s_ref, bf16[2,128,3072]{2,1,0:T(8,128)(2,1)S(1)} %bitcast.21, bf16[2,128,3072]{2,1,0:T(8,128)(2,1)} %collective-permute-done.other_ref, ...), custom_call_target="tpu_custom_call" | custom-call | tf_op jit(solution)/shard_map/pallas_call | solution.py:23
  60.1 0.0 all-to-all-done.refs_0_
  60.1 0.1 collective-permute-start.9
  60.2 0.7 collective-permute-start.5
  60.9 5.6 %collective-permute-start.6 = (bf16[256,384]{1,0:T(8,128)(2,1)}, bf16[256,384]{1,0:T(8,128)(2,1)}, u32[]{:S(2)}, u32[]{:S(2)}) collective-permute-start(bf16[256,384]{1,0:T(8,128)(2,1)} %get-tuple-element.14), channel_id=1, source_target_pairs={{0,1},{1,5},{2,2},{3,6},{4,3},{5,7},{6,0},{7,4},{8,9},{9,13},{10,1... | collective-permute-start | bytes 589832 | tf_op jit(solution)/shard_map/ppermute | solution.py:412
  66.5 0.7 collective-permute-start.7
  67.2 3.1 %collective-permute-start.8 = (bf16[256,384]{1,0:T(8,128)(2,1)}, bf16[256,384]{1,0:T(8,128)(2,1)}, u32[]{:S(2)}, u32[]{:S(2)}) collective-permute-start(bf16[256,384]{1,0:T(8,128)(2,1)} %get-tuple-element.16), channel_id=1, source_target_pairs={{0,3},{1,7},{2,0},{3,4},{4,1},{5,5},{6,2},{7,6},{8,11},{9,15},{10,... | collective-permute-start | bytes 589832 | tf_op jit(solution)/shard_map/ppermute | solution.py:412
  70.4 0.6 constant_dynamic-slice_fusion
  73.9 0.0 collective-permute-done.5.refs_0_
  73.9 0.1 collective-permute-done.6.refs_1_
  74.1 7.4 %collective-permute-done.7.refs_2_ = bf16[256,384]{1,0:T(8,128)(2,1)} collective-permute-done((bf16[256,384]{1,0:T(8,128)(2,1)}, bf16[256,384]{1,0:T(8,128)(2,1)}, u32[]{:S(2)}, u32[]{:S(2)}) %collective-permute-start.7) | collective-permute-done | bytes 196640 | tf_op jit(solution)/shard_map/ppermute | solution.py:412
  81.4 0.0 collective-permute-done.8.refs_3_
  81.4 0.0 collective-permute-done.9.refs_5_
  81.4 3.6 %shard_map.88.refs_0_ = bf16[128,384]{1,0:T(8,128)(2,1)S(1)} custom-call(s32[1]{0:T(128)} %bitcast.5.s_ref, f32[1]{0:T(128)S(6)} %copy.11.g_ref, bf16[256,384]{1,0:T(8,128)(2,1)S(1)} %collective-permute-done.5.refs_0_, bf16[256,384]{1,0:T(8,128)(2,1)} %collective-permute-done.6.refs_1_, bf16[256,384]{1,0:T(8,128)(2,1)} %collective-permute-done.7.refs_2_, ...), custom_call_target="tpu_custom_call" | custom-call | tf_op jit(solution)/shard_map/pallas_call | solution.py:23
  85.0 0.1 collective-permute-start.10
  85.1 3.1 %collective-permute-start.11 = (bf16[128,384]{1,0:T(8,128)(2,1)S(1)}, bf16[128,384]{1,0:T(8,128)(2,1)S(1)}, u32[]{:S(2)}, u32[]{:S(2)}) collective-permute-start(bf16[128,384]{1,0:T(8,128)(2,1)S(1)} %shard_map.88.refs_0_), channel_id=1, source_target_pairs={{0,4},{1,5},{2,6},{3,7},{4,0},{5,1},{6,2},{7,3},{8,12},{9,13},{10,... | collective-permute-start | bytes 294920 | tf_op jit(solution)/shard_map/ppermute | solution.py:401
  88.2 1.4 %collective-permute-start.12 = (bf16[128,384]{1,0:T(8,128)(2,1)S(1)}, bf16[128,384]{1,0:T(8,128)(2,1)S(1)}, u32[]{:S(2)}, u32[]{:S(2)}) collective-permute-start(bf16[128,384]{1,0:T(8,128)(2,1)S(1)} %shard_map.88.refs_0_), channel_id=1, source_target_pairs={{0,6},{1,7},{2,4},{3,5},{4,2},{5,3},{6,0},{7,1},{8,14},{9,15},{10,... | collective-permute-start | bytes 294920 | tf_op jit(solution)/shard_map/ppermute | solution.py:401
  89.6 0.1 collective-permute-done.10.refs_1_
  89.7 1.4 %collective-permute-done.11.refs_2_ = bf16[128,384]{1,0:T(8,128)(2,1)S(1)} collective-permute-done((bf16[128,384]{1,0:T(8,128)(2,1)S(1)}, bf16[128,384]{1,0:T(8,128)(2,1)S(1)}, u32[]{:S(2)}, u32[]{:S(2)}) %collective-permute-start.11) | collective-permute-done | bytes 98336 | tf_op jit(solution)/shard_map/ppermute | solution.py:401
  91.1 5.4 %collective-permute-done.12.refs_3_ = bf16[128,384]{1,0:T(8,128)(2,1)S(1)} collective-permute-done((bf16[128,384]{1,0:T(8,128)(2,1)S(1)}, bf16[128,384]{1,0:T(8,128)(2,1)S(1)}, u32[]{:S(2)}, u32[]{:S(2)}) %collective-permute-start.12) | collective-permute-done | bytes 98336 | tf_op jit(solution)/shard_map/ppermute | solution.py:401
  96.5 0.7 shard_map.89
  97.2 0.1 collective-permute-start.13
  97.3 0.7 fusion.1
  98.0 1.4 %pad_add_fusion.s_ref = s32[3]{0:T(128)S(1)} fusion(s32[1]{0:T(128)} %get-tuple-element.20, s32[1]{0:T(128)} %get-tuple-element.19, s32[1]{0:T(128)} %bitcast), kind=kLoop, calls=%fused_computation.6 | loop fusion | flops 6 | bytes 24 | tf_op jit(solution)/shard_map/concatenate | solution.py:506
  99.4 0.0 collective-permute-done.13.refs_4_
  99.4 2.3 %shard_map.90 = bf16[128,1536]{1,0:T(8,128)(2,1)} custom-call(s32[3]{0:T(128)S(1)} %pad_add_fusion.s_ref, bf16[128,1536]{1,0:T(8,128)(2,1)} %bitcast.28, bf16[128,384]{1,0:T(8,128)(2,1)S(1)} %shard_map.88.refs_0_, bf16[128,384]{1,0:T(8,128)(2,1)S(1)} %collective-permute-done.10.refs_1_, bf16[128,384]{1,0:T(8,128)(2,1)S(1)} %collective-permute-done.11.refs_2_, ...), custom_call_target="tpu_custom_call" | custom-call | tf_op jit(solution)/shard_map/pallas_call | solution.py:23
  (2 shorter events, 0.0 us)
Async XLA Ops:
  4.2 55.8 %all-to-all-start = ((bf16[4,2,2,128,384]{4,3,2,1,0:T(8,128)(2,1)}), bf16[4,2,2,128,384]{4,3,2,1,0:T(8,128)(2,1)S(1)}, u32[]{:S(2)}, u32[]{:S(2)}) async-start(bf16[4,2,2,128,384]{4,3,2,1,0:T(8,128)(2,1)} %shard_map.83.refs_0_), calls=%async_computation | async-start | bytes 3145728 | tf_op jit(solution)/shard_map/all_to_all | solution.py:476
  10.6 27.4 %collective-permute-start.1 = (bf16[768,768]{1,0:T(8,128)(2,1)S(1)}, bf16[768,768]{1,0:T(8,128)(2,1)S(1)}, u32[]{:S(2)}, u32[]{:S(2)}) collective-permute-start(bf16[768,768]{1,0:T(8,128)(2,1)S(1)} %shard_map.82.refs_0_), channel_id=1, source_target_pairs={{0,8},{8,0},{16,24},{24,16},{1,9},{9,1},{17,25},{25,17},{2,10},{10... | collective-permute-start | bytes 3538952 | tf_op jit(solution)/shard_map/ppermute | solution.py:397
  12.1 27.1 %collective-permute-start.2 = (bf16[768,768]{1,0:T(8,128)(2,1)S(1)}, bf16[768,768]{1,0:T(8,128)(2,1)S(1)}, u32[]{:S(2)}, u32[]{:S(2)}) collective-permute-start(bf16[768,768]{1,0:T(8,128)(2,1)S(1)} %shard_map.82.refs_0_), channel_id=1, source_target_pairs={{0,16},{8,24},{16,0},{24,8},{1,17},{9,25},{17,1},{25,9},{2,18},{10... | collective-permute-start | bytes 3538952 | tf_op jit(solution)/shard_map/ppermute | solution.py:397
  13.6 30.0 %copy-start.5 = (s32[1,2]{1,0:T(1,128)S(1)}, s32[1,2]{1,0:T(1,128)}, u32[]{:S(2)}) copy-start(s32[1,2]{1,0:T(1,128)} %param.14) | copy-start | bytes 28
  13.6 30.1 %collective-permute-start = (bf16[2,128,3072]{2,1,0:T(8,128)(2,1)}, bf16[2,128,3072]{2,1,0:T(8,128)(2,1)}, u32[]{:S(2)}, u32[]{:S(2)}) collective-permute-start(bf16[2,128,3072]{2,1,0:T(8,128)(2,1)} %bitcast.19), channel_id=1, source_target_pairs={{0,1},{1,0},{2,3},{3,2},{4,5},{5,4},{6,7},{7,6},{8,9},{9,8},{10,11... | collective-permute-start | bytes 4718600 | tf_op jit(solution)/shard_map/ppermute | solution.py:404
  38.0 2.7 %copy-start.1 = (bf16[768,768]{1,0:T(8,128)(2,1)}, bf16[768,768]{1,0:T(8,128)(2,1)S(1)}, u32[]{:S(2)}) copy-start(bf16[768,768]{1,0:T(8,128)(2,1)S(1)} %collective-permute-done.1.x_ref.refs_1_) | copy-start | bytes 3538948
  39.2 1.5 %copy-start.3 = (bf16[768,768]{1,0:T(8,128)(2,1)}, bf16[768,768]{1,0:T(8,128)(2,1)S(1)}, u32[]{:S(2)}) copy-start(bf16[768,768]{1,0:T(8,128)(2,1)S(1)} %collective-permute-done.2.y_ref.refs_2_) | copy-start | bytes 3538948
  40.7 13.9 %collective-permute-start.3 = (bf16[384,768]{1,0:T(8,128)(2,1)}, bf16[384,768]{1,0:T(8,128)(2,1)S(1)}, u32[]{:S(2)}, u32[]{:S(2)}) collective-permute-start(bf16[384,768]{1,0:T(8,128)(2,1)} %get-tuple-element.11.refs_3_), channel_id=1, source_target_pairs={{0,16},{8,24},{16,0},{24,8},{1,17},{9,25},{17,1},{25,9},{2,18},{10... | collective-permute-start | bytes 1769480 | tf_op jit(solution)/shard_map/ppermute | solution.py:397
  42.3 13.6 %collective-permute-start.4 = (bf16[384,768]{1,0:T(8,128)(2,1)}, bf16[384,768]{1,0:T(8,128)(2,1)}, u32[]{:S(2)}, u32[]{:S(2)}) collective-permute-start(bf16[384,768]{1,0:T(8,128)(2,1)} %get-tuple-element.12), channel_id=1, source_target_pairs={{0,8},{8,0},{16,24},{24,16},{1,9},{9,1},{17,25},{25,17},{2,10},{10... | collective-permute-start | bytes 1769480 | tf_op jit(solution)/shard_map/ppermute | solution.py:397
  43.7 1.4 %copy-start = (bf16[2,1,128,3072]{3,2,1,0:T(8,128)(2,1)S(1)}, bf16[2,1,128,3072]{3,2,1,0:T(8,128)(2,1)}, u32[]{:S(2)}) copy-start(bf16[2,1,128,3072]{3,2,1,0:T(8,128)(2,1)} %param.8) | copy-start | bytes 4718596
  45.1 1.3 %copy-start.2 = (bf16[768,768]{1,0:T(8,128)(2,1)S(1)}, bf16[768,768]{1,0:T(8,128)(2,1)}, u32[]{:S(2)}) copy-start(bf16[768,768]{1,0:T(8,128)(2,1)} %copy-done.1) | copy-start | bytes 3538948
  46.4 1.3 %copy-start.4 = (bf16[768,768]{1,0:T(8,128)(2,1)S(1)}, bf16[768,768]{1,0:T(8,128)(2,1)}, u32[]{:S(2)}) copy-start(bf16[768,768]{1,0:T(8,128)(2,1)} %copy-done.3) | copy-start | bytes 3538948
  60.1 21.3 %collective-permute-start.9 = (bf16[4,2,2,128,384]{4,3,2,1,0:T(8,128)(2,1)S(1)}, bf16[4,2,2,128,384]{4,3,2,1,0:T(8,128)(2,1)S(1)}, u32[]{:S(2)}, u32[]{:S(2)}) collective-permute-start(bf16[4,2,2,128,384]{4,3,2,1,0:T(8,128)(2,1)S(1)} %shard_map.87.refs_4_), channel_id=1, source_target_pairs={{0,1},{1,0},{2,3},{3,2},{4,5},{5,4},{6,7},{7,6},{8,9},{9,8},{10,11... | collective-permute-start | bytes 4718600 | tf_op jit(solution)/shard_map/ppermute | solution.py:404
  60.2 13.7 %collective-permute-start.5 = (bf16[256,384]{1,0:T(8,128)(2,1)S(1)}, bf16[256,384]{1,0:T(8,128)(2,1)S(1)}, u32[]{:S(2)}, u32[]{:S(2)}) collective-permute-start(bf16[256,384]{1,0:T(8,128)(2,1)S(1)} %get-tuple-element.13.refs_1_), channel_id=1, source_target_pairs={{0,0},{1,4},{2,1},{3,5},{4,2},{5,6},{6,3},{7,7},{8,8},{9,12},{10,9... | collective-permute-start | bytes 589832 | tf_op jit(solution)/shard_map/ppermute | solution.py:412
  60.9 13.2 %collective-permute-start.6 = (bf16[256,384]{1,0:T(8,128)(2,1)}, bf16[256,384]{1,0:T(8,128)(2,1)}, u32[]{:S(2)}, u32[]{:S(2)}) collective-permute-start(bf16[256,384]{1,0:T(8,128)(2,1)} %get-tuple-element.14), channel_id=1, source_target_pairs={{0,1},{1,5},{2,2},{3,6},{4,3},{5,7},{6,0},{7,4},{8,9},{9,13},{10,1... | collective-permute-start | bytes 589832 | tf_op jit(solution)/shard_map/ppermute | solution.py:412
  66.5 14.9 %collective-permute-start.7 = (bf16[256,384]{1,0:T(8,128)(2,1)}, bf16[256,384]{1,0:T(8,128)(2,1)}, u32[]{:S(2)}, u32[]{:S(2)}) collective-permute-start(bf16[256,384]{1,0:T(8,128)(2,1)} %get-tuple-element.15), channel_id=1, source_target_pairs={{0,2},{1,6},{2,3},{3,7},{4,0},{5,4},{6,1},{7,5},{8,10},{9,14},{10,... | collective-permute-start | bytes 589832 | tf_op jit(solution)/shard_map/ppermute | solution.py:412
  67.2 14.2 %collective-permute-start.8 = (bf16[256,384]{1,0:T(8,128)(2,1)}, bf16[256,384]{1,0:T(8,128)(2,1)}, u32[]{:S(2)}, u32[]{:S(2)}) collective-permute-start(bf16[256,384]{1,0:T(8,128)(2,1)} %get-tuple-element.16), channel_id=1, source_target_pairs={{0,3},{1,7},{2,0},{3,4},{4,1},{5,5},{6,2},{7,6},{8,11},{9,15},{10,... | collective-permute-start | bytes 589832 | tf_op jit(solution)/shard_map/ppermute | solution.py:412
  85.0 4.7 %collective-permute-start.10 = (bf16[128,384]{1,0:T(8,128)(2,1)S(1)}, bf16[128,384]{1,0:T(8,128)(2,1)S(1)}, u32[]{:S(2)}, u32[]{:S(2)}) collective-permute-start(bf16[128,384]{1,0:T(8,128)(2,1)S(1)} %shard_map.88.refs_0_), channel_id=1, source_target_pairs={{0,2},{1,3},{2,0},{3,1},{4,6},{5,7},{6,4},{7,5},{8,10},{9,11},{10,... | collective-permute-start | bytes 294920 | tf_op jit(solution)/shard_map/ppermute | solution.py:401
  85.1 6.0 %collective-permute-start.11 = (bf16[128,384]{1,0:T(8,128)(2,1)S(1)}, bf16[128,384]{1,0:T(8,128)(2,1)S(1)}, u32[]{:S(2)}, u32[]{:S(2)}) collective-permute-start(bf16[128,384]{1,0:T(8,128)(2,1)S(1)} %shard_map.88.refs_0_), channel_id=1, source_target_pairs={{0,4},{1,5},{2,6},{3,7},{4,0},{5,1},{6,2},{7,3},{8,12},{9,13},{10,... | collective-permute-start | bytes 294920 | tf_op jit(solution)/shard_map/ppermute | solution.py:401
  88.2 8.3 %collective-permute-start.12 = (bf16[128,384]{1,0:T(8,128)(2,1)S(1)}, bf16[128,384]{1,0:T(8,128)(2,1)S(1)}, u32[]{:S(2)}, u32[]{:S(2)}) collective-permute-start(bf16[128,384]{1,0:T(8,128)(2,1)S(1)} %shard_map.88.refs_0_), channel_id=1, source_target_pairs={{0,6},{1,7},{2,4},{3,5},{4,2},{5,3},{6,0},{7,1},{8,14},{9,15},{10,... | collective-permute-start | bytes 294920 | tf_op jit(solution)/shard_map/ppermute | solution.py:401
  97.2 2.2 %collective-permute-start.13 = (bf16[4,128,384]{2,1,0:T(8,128)(2,1)S(1)}, bf16[4,128,384]{2,1,0:T(8,128)(2,1)S(1)}, u32[]{:S(2)}, u32[]{:S(2)}) collective-permute-start(bf16[4,128,384]{2,1,0:T(8,128)(2,1)S(1)} %shard_map.89), channel_id=1, source_target_pairs={{0,1},{1,0},{2,3},{3,2},{4,5},{5,4},{6,7},{7,6},{8,9},{9,8},{10,11... | collective-permute-start | bytes 1179656 | tf_op jit(solution)/shard_map/ppermute | solution.py:404

commit v3 on v2

v3 whole, which is shorter than its diff:
```python
import math

import jax
import jax.numpy as jnp
from jax import lax
from jax.experimental import pallas as pl
from jax.experimental.pallas import tpu as pltpu
from jax.sharding import PartitionSpec as P

HD = 128
TILE = 128
GROUPS = 4
BF = jnp.bfloat16
F32 = jnp.float32
MIB = 1024 * 1024

SMEM_SPEC = pl.BlockSpec(memory_space=pltpu.SMEM)
ANY_SPEC = pl.BlockSpec(memory_space=pl.ANY)
VMEM_SPEC = pl.BlockSpec(memory_space=pltpu.VMEM)


def call(kernel, out_shape, scalars, arrays, scratch=(), limit=4, aliases=None, spec=ANY_SPEC, out_spec=ANY_SPEC, flops=0):
    many = isinstance(out_shape, (list, tuple))
    return pl.pallas_call(
        kernel,
        out_shape=out_shape,
        in_specs=[SMEM_SPEC] * len(scalars) + (spec if isinstance(spec, list) else [spec] * len(arrays)),
        out_specs=[out_spec] * len(out_shape) if many else out_spec,
        scratch_shapes=list(scratch),
        input_output_aliases=aliases or {},
        compiler_params=pltpu.CompilerParams(vmem_limit_bytes=limit * MIB),
        cost_estimate=pl.CostEstimate(flops=flops, bytes_accessed=0, transcendentals=0),
    )(*scalars, *arrays)


def stays(x):
    return pltpu.with_memory_space_constraint(x, pltpu.HBM)


def run_all(copies):
    for copy in copies:
        copy.start()
    for copy in copies:
        copy.wait()


def run_both(loads, stores):
    for load in loads:
        load.start()
    for load, store in zip(loads, stores):
        load.wait()
        store.start()
    for store in stores:
        store.wait()


def after(x, *events):
    def kernel(*refs):
        pass

    return call(kernel, jax.ShapeDtypeStruct(x.shape, x.dtype), [], [x, *events], aliases={0: 0})


def pack_weights(core, w_query, heads_of, events=()):
    rows, columns = w_query.shape
    count = len(heads_of(0))
    shape = (rows, count * HD)

    def kernel(core_ref, w_ref, *refs):
        out, buf, sem, out_sem = refs[-4:]
        loads, stores = [], []
        for n, head in enumerate(heads_of(core_ref[0])):
            here = slice(n * HD, (n + 1) * HD)
            at = pl.ds(pl.multiple_of(head * HD, HD), HD)
            loads.append(pltpu.make_async_copy(w_ref.at[:, at], buf.at[:, here], sem.at[n]))
            stores.append(pltpu.make_async_copy(buf.at[:, here], out.at[:, here], out_sem.at[n]))
        run_both(loads, stores)

    return call(
        kernel,
        jax.ShapeDtypeStruct(shape, BF),
        [core],
        [stays(w_query), *events],
        [pltpu.VMEM(shape, BF), pltpu.SemaphoreType.DMA((count,)), pltpu.SemaphoreType.DMA((count,))],
    )


def pack_caches(key_block, value_block, events=()):
    branches, tokens, columns = key_block.shape
    width = columns // GROUPS

    def kernel(k_ref, v_ref, *refs):
        out, buf, sem, out_sem = refs[-4:]
        loads, stores = [], []
        for n, ref in enumerate((k_ref, v_ref)):
            for g in range(GROUPS):
                here = buf.at[g, n]
                loads.append(
                    pltpu.make_async_copy(
                        ref.at[:, :, g * width : (g + 1) * width], here, sem.at[n * GROUPS + g]
                    )
                )
                stores.append(pltpu.make_async_copy(here, out.at[g, n], out_sem.at[n * GROUPS + g]))
        run_both(loads, stores)

    shape = (GROUPS, 2, branches, tokens, width)
    return call(
        kernel,
        jax.ShapeDtypeStruct(shape, BF),
        [],
        [stays(key_block), stays(value_block), *events],
        [pltpu.VMEM(shape, BF), pltpu.SemaphoreType.DMA((2 * GROUPS,)), pltpu.SemaphoreType.DMA((2 * GROUPS,))],
    )


def halves(flags, by_x, by_y, events=()):
    rows, width = by_x.shape
    half = rows // 2

    def kernel(_, x_ref, y_ref, *refs):
        first, last, buf, sem, out_sem = refs[-5:]
        sources = (x_ref.at[:half], y_ref.at[half:])
        run_all([pltpu.make_async_copy(ref, buf.at[n], sem.at[n]) for n, ref in enumerate(sources)])
        run_all([pltpu.make_async_copy(buf.at[n], ref, out_sem.at[n]) for n, ref in enumerate((first, last))])

    return call(
        kernel,
        [jax.ShapeDtypeStruct((half, width), BF)] * 2,
        [flags],
        [by_x, by_y, *events],
        [
            pltpu.VMEM((2, half, width), BF),
            pltpu.SemaphoreType.DMA((2,)),
            pltpu.SemaphoreType.DMA((2,)),
        ],
    )


def stack(pieces):
    def kernel(*refs):
        for n in range(len(pieces)):
            refs[-1][n] = refs[n][...]

    return call(
        kernel,
        jax.ShapeDtypeStruct((len(pieces), *pieces[0].shape), BF),
        [],
        pieces,
        spec=VMEM_SPEC,
        out_spec=VMEM_SPEC,
    )


def begin_project(flags, at, own, other, pieces, far_rows, events=()):
    branches, rows, depth = own.shape
    chunk, width = pieces[0].shape
    count = len(pieces)
    both = branches * rows

    def kernel(s_ref, own_ref, other_ref, *refs):
        w_refs = refs[:count]
        t_ref, far_ref, h_buf, w_buf, sem = refs[-5:]
        loads = []
        for n in range(count + 1):
            columns = pl.ds(pl.multiple_of((s_ref[0] ^ n) * chunk, HD), chunk)
            loads.append([])
            if n < count:
                loads[n].append(pltpu.make_async_copy(w_refs[n], w_buf.at[n], sem.at[n, 2]))
                loads[n][0].start()
            for slot in range(2):
                for b in range(branches):
                    there = h_buf.at[n, slot] if n < count else far_ref.at[slot]
                    there = there.at[b * rows : (b + 1) * rows]
                    mine, theirs = [
                        pltpu.make_async_copy(ref.at[b, :, columns], there, sem.at[n, slot])
                        for ref in (own_ref, other_ref)
                    ]
                    loads[n].append(mine)

                    @pl.when(s_ref[at + slot] == 1)
                    def _():
                        mine.start()

                    @pl.when(s_ref[at + slot] != 1)
                    def _():
                        theirs.start()

        for n in range(count):
            for load in loads[n]:
                load.wait()
            for slot in range(2):
                product = jnp.dot(h_buf[n, slot], w_buf[n], preferred_element_type=F32)
                if n == 0:
                    t_ref[slot] = product
                else:
                    t_ref[slot] += product
        for load in loads[count]:
            load.wait()

    return call(
        kernel,
        [jax.ShapeDtypeStruct((2, both, width), F32), jax.ShapeDtypeStruct((2, both, far_rows), BF)],
        [flags],
        [own, other, *pieces, *events],
        [
            pltpu.VMEM((count, 2, both, chunk), BF),
            pltpu.VMEM((count, chunk, width), BF),
            pltpu.SemaphoreType.DMA((count + 1, 3)),
        ],
        limit=16,
        out_spec=VMEM_SPEC,
        flops=25_000_000_000,
    )


def finish_project(flags, sums, rows_far, pieces, earlier=None, events=()):
    _, both, width = sums.shape
    part = width // 2
    count = len(pieces)
    last = earlier is not None
    before = earlier.shape[2] if last else 0

    def kernel(s_ref, t_ref, far_ref, *refs):
        w_refs = refs[:count]
        q_buf = refs[-1]
        for slot in range(2):
            total, first = t_ref[slot], 0
            for w_ref in w_refs:
                size = w_ref.shape[0]
                total = total + jnp.dot(
                    far_ref[slot, :, first : first + size], w_ref[...], preferred_element_type=F32
                )
                first += size
            total = total.astype(BF)
            for hi in range(2):
                q_buf[hi * 2 + slot] = total[:, hi * part : (hi + 1) * part]
        if last:
            for r, out in enumerate(refs[-5:-1]):
                target = (s_ref[1] + r) % 4
                out[:, :before] = refs[count][target]
                out[:, before:] = q_buf[target]

    whole = jax.ShapeDtypeStruct((4, both, part), BF)
    piece = jax.ShapeDtypeStruct((both, before + part), BF)
    return call(
        kernel,
        [piece] * 4 if last else whole,
        [flags],
        [sums, rows_far, *pieces, *([earlier] if last else []), *events],
        [pltpu.VMEM((4, both, part), BF)] if last else [],
        limit=8,
        spec=[VMEM_SPEC] * (2 + count + last) + [ANY_SPEC] * len(events),
        out_spec=VMEM_SPEC,
    )


def attend(flags, guide, queries, caches):
    count, parts, kept = len(queries[0]), len(queries), len(caches)
    rows = queries[0][0].shape[0] // 2
    widths = [part[0].shape[1] for part in queries]
    scale = 1.0 / math.sqrt(HD)
    sizes = [c.shape[0] * c.shape[3] for c in caches]
    keys_all = sum(sizes)

    def kernel(s_ref, g_ref, *refs):
        q_refs, c_refs = refs[: parts * count], refs[parts * count : parts * count + kept]
        out, q_buf = refs[-2:]
        for r in range(count):

            @pl.when(s_ref[2] == r)
            def _():
                first = 0
                for k in range(parts):
                    q_buf[:, first : first + widths[k]] = q_refs[k * count + r][...]
                    first += widths[k]

        for head in range(sum(widths) // HD):
            at = slice(head * HD, (head + 1) * HD)
            attended = []
            for b in range(2):
                q = q_buf[b * rows : (b + 1) * rows, at]
                scores = [
                    lax.dot_general(
                        q,
                        c_ref[:, 0, b, :, at].reshape(size, HD),
                        (((1,), (1,)), ((), ())),
                        preferred_element_type=F32,
                    )
                    * scale
                    for c_ref, size in zip(c_refs, sizes)
                ]
                top = jnp.max(scores[0], axis=-1, keepdims=True)
                for s in scores[1:]:
                    top = jnp.maximum(top, jnp.max(s, axis=-1, keepdims=True))
                exps = [jnp.exp(s - top) for s in scores]
                total = jnp.sum(exps[0], axis=-1, keepdims=True)
                for e in exps[1:]:
                    total = total + jnp.sum(e, axis=-1, keepdims=True)
                over = 1.0 / total
                result = jnp.zeros((rows, HD), F32)
                for e, c_ref, size in zip(exps, c_refs, sizes):
                    w = (e * over).astype(BF)
                    result = result + jnp.dot(
                        w, c_ref[:, 1, b, :, at].reshape(size, HD), preferred_element_type=F32
                    )
                attended.append(result)
            guided = attended[1] + g_ref[0] * (attended[0] - attended[1])
            out[:, at] = guided.astype(BF)

    return call(
        kernel,
        jax.ShapeDtypeStruct((rows, sum(widths)), BF),
        [flags, guide],
        [q for part in queries for q in part] + caches,
        [pltpu.VMEM((2 * rows, sum(widths)), BF)],
        limit=8 + 8 * (keys_all // 1024),
        spec=VMEM_SPEC,
        out_spec=VMEM_SPEC,
    )


def paste(flags, previous, mine, others):
    rows, columns = previous.shape
    width = columns // GROUPS

    def kernel(s_ref, prev_ref, *refs):
        out, sem = refs[-2:]

        def place(m):
            return out.at[:, pl.ds(pl.multiple_of((s_ref[1] ^ m) * width, HD), width)]

        taken = s_ref[3]
        for n in range(len(others)):
            taken = taken + s_ref[4 + n]

        @pl.when(taken == 0)
        def _():
            run_all([pltpu.make_async_copy(prev_ref, out, sem.at[0])])

        @pl.when(s_ref[3] == 1)
        def _():
            run_all([pltpu.make_async_copy(refs[m], place(m), sem.at[m]) for m in range(GROUPS)])

        for n in range(len(others)):

            @pl.when(s_ref[4 + n] == 1)
            def _():
                run_all(
                    [pltpu.make_async_copy(refs[GROUPS + n].at[m], place(m), sem.at[m]) for m in range(GROUPS)]
                )

    return call(
        kernel,
        jax.ShapeDtypeStruct((rows, columns), BF),
        [flags],
        [previous, *mine, *others],
        [pltpu.SemaphoreType.DMA((GROUPS,))],
        spec=VMEM_SPEC,
    )


def body(hidden, key_cache, value_cache, cached_out, w_query, guide, masked_tiles, mask_count):
    images = lax.axis_size("image")
    tokens = lax.axis_size("token")
    heads = key_cache.shape[3] // HD
    per_group = heads // GROUPS
    slots = masked_tiles.shape[1]
    layers = tokens // (2 * GROUPS)
    assert images == 4 and hidden.shape[1] == 1 and hidden.shape[2] == TILE
    assert tokens == layers * 2 * GROUPS and slots == 2 * layers and heads == per_group * GROUPS

    image = lax.axis_index("image")
    token = lax.axis_index("token")
    core = token % 2
    chip = token // 2
    z = chip // layers
    layer = chip % layers
    tiles = masked_tiles[0]

    def over_image(x, m):
        return lax.ppermute(x, "image", [(i, i ^ m) for i in range(images)])

    def over_z(x, m):
        span = 2 * layers
        return lax.ppermute(x, "token", [(t, ((t // span) ^ m) * span + t % span) for t in range(tokens)])

    def over_core(x):
        return lax.ppermute(x, "token", [(t, t ^ 1) for t in range(tokens)])

    def to_targets(x, r):
        pairs = []
        for t in range(tokens):
            c, at, s = t % 2, (t // 2) % layers, t // 2 // layers
            goal = (s + r) % 4
            pairs.append((t, ((2 * c + goal // 2) * layers + at) * 2 + goal % 2))
        return lax.ppermute(x, "token", pairs)

    layer_groups = [
        [(s * layers + at) * 2 + c for at in range(layers)] for s in range(GROUPS) for c in range(2)
    ]
    group_groups = [list(range(s * layers * 2, (s + 1) * layers * 2)) for s in range(GROUPS)]
    z_groups = [[s * 2 * layers + at for s in range(GROUPS)] for at in range(2 * layers)]

    plan = [list(range(per_group - 1)), [per_group - 1]]

    def part_heads(k):
        return lambda c: [(2 * c + hi) * per_group + head for hi in range(2) for head in plan[k]]

    half = w_query.shape[0] // 2
    own_hidden = hidden[:, 0]
    other_hidden = over_core(own_hidden)

    my_slot = layer * 2 + core
    my_tile = tiles[my_slot]
    target = 2 * (z % 2) + core
    choice = (target - my_tile // 2 // layers) % 4
    in_use = jnp.arange(slots, dtype=jnp.int32) < mask_count[0]
    hit = ((tiles == token) & in_use).astype(jnp.int32)
    other_hits = hit[1 - core][None] if layers == 1 else jnp.where(jnp.arange(slots) == my_slot, 0, hit)
    is_own = (tiles % 2 == core).astype(jnp.int32)
    flags = jnp.concatenate(
        [jnp.stack([image, z, choice, hit[my_slot]]).astype(jnp.int32), other_hits, is_own]
    )
    pairs_from = 4 + other_hits.shape[0]

    def near(k, *events):
        own = pack_weights(core[None], w_query, part_heads(k), events)
        return [own, over_image(own, 1), over_image(own, 2)]

    def far(k, *events):
        first, last = halves(flags, weights[k][1], weights[k][2], events)
        return [over_image(first, 2), over_image(last, 1)], first

    def begin(k, *events):
        return [
            begin_project(
                flags, pairs_from + 2 * at, own_hidden, other_hidden, weights[k], w_query.shape[0], events
            )
            for at in range(layers)
        ]

    def finish(begun_0, far_0, begun_1, far_1, *events):
        result = None
        for at in range(layers):
            first = finish_project(flags, *begun_0[at], far_0, events=events)
            sent = finish_project(flags, *begun_1[at], far_1, first)
            came = [to_targets(x, r) for r, x in enumerate(sent)]
            if layers > 1:
                holds = (tiles[2 * at + core] // 2) % layers == layer
                came = [
                    lax.psum(jnp.where(holds, x, jnp.zeros_like(x)), "token", axis_index_groups=layer_groups)
                    for x in came
                ]
            if result is None:
                result = came
            else:
                result = [jnp.where(layer == at, new, old) for new, old in zip(came, result)]
        return result, sent[0]

    weights = [near(0)]
    blocks = pack_caches(key_cache[:, 0], value_cache[:, 0], weights[0][:1])
    gathered = lax.all_to_all(blocks, "token", 0, 0, axis_index_groups=z_groups)
    weights.append(near(1, blocks))
    far_0, event = far(0, weights[1][0])
    begun_0 = begin(0, event)
    far_1, event = far(1, begun_0[0][1])
    begun_1 = begin(1, event)
    queries, event = finish(begun_0, far_0, begun_1, far_1, begun_1[0][1])

    gathered = after(gathered, event, queries[0], queries[1])
    if layers == 1:
        caches = [gathered, over_core(gathered)]
    else:
        everyone = lax.all_gather(gathered, "token", axis_index_groups=group_groups)
        caches = [everyone.reshape(-1, *gathered.shape[1:])]

    guided = attend(flags, guide, [queries], caches)
    mine = [guided] + [over_z(guided, m) for m in range(1, GROUPS)]
    stacked = stack(mine)
    if layers == 1:
        others = [over_core(stacked)]
    else:
        everyone = lax.all_gather(stacked, "token", axis_index_groups=group_groups)
        others = [everyone[n] for n in range(slots)]
    return paste(flags, cached_out[0], mine, others)[None]


def solution(mesh):
    return jax.shard_map(
        body,
        mesh=mesh,
        in_specs=(
            P(None, "image", "token", None),
            P(None, "image", "token", None),
            P(None, "image", "token", None),
            P("image", "token", None),
            P("image", None),
            P("image"),
            P("image", None),
            P("image"),
        ),
        out_specs=P("image", "token", None),
        check_vma=False,
    )
```

time: 103 us -> 88.1 us (0.86)
  waiting for transfers between devices: 44.2 us -> 30.3 us
  local copies, waits for them, and re-layouts: 5.22 us -> 2.6 us
  starting transfers between devices: 26.4 us -> 28.4 us
  Pallas kernels: 20.6 us -> 22.2 us
  other arithmetic: 1.5 us -> 0.01 us
    ppermute x4 -> x8, waiting for transfers between devices: 29.7 us -> 7.96 us  [over_image(): return lax.ppermute(x, 'image', [(i, i ^ m) for i in range(images)])]
    ppermute x4, waiting for transfers between devices: 7.52 us -> 14.6 us  [to_targets(): return lax.ppermute(x, 'token', pairs)]
    unnamed x12 -> x6, local copies, waits for them, and re-layouts: 3.96 us -> 0.02 us
    ppermute x4 -> x8, starting transfers between devices: 5.23 us -> 8.96 us  [over_image(): return lax.ppermute(x, 'image', [(i, i ^ m) for i in range(images)])]
    ppermute x4, starting transfers between devices: 10.2 us -> 7.67 us  [to_targets(): return lax.ppermute(x, 'token', pairs)]
    ppermute x3, starting transfers between devices: 0.17 us -> 2.01 us  [over_core(): return lax.ppermute(x, 'token', [(t, t ^ 1) for t in range(tokens)])]
    pallas_call x9 -> x13, Pallas kernels: 20.6 us -> 22.2 us  [call(): pl.pallas_call(kernel, out_shape=out_shape, in_specs=[SMEM_SPEC] * len(sc...]
    concatenate x2 -> x0, other arithmetic: 1.49 us -> none  [the longest x1 1.41 us: body(): jnp.concatenate([jnp.stack([z, own_hit]).astype(jnp.int32), other_hits])]
  transfers between devices with their start and end apart: 15 -> 19, of which waited for: 9 -> 11; matrix products, arithmetic and copies ran while one was open for 3% -> 3% of each run, Pallas kernels for 10% -> 20%
where the time goes in v3:
time: 88.1 us; the launch traced here: 87.6 us
  waiting for transfers between devices  30.3 us (34%)
  starting transfers between devices  28.4 us (32%)
  Pallas kernels  22.2 us (25%)
  between operations  4.11 us (5%)
  local copies, waits for them, and re-layouts  2.6 us (3%)
    pallas_call x13, Pallas kernels, call(): pl.pallas_call(kernel, out_shape=out_shape, in_specs=[SMEM_SPEC] * len(sc...  22.2 us
    ppermute x4, waiting for transfers between devices, to_targets(): return lax.ppermute(x, 'token', pairs)  14.6 us
    ppermute x8, starting transfers between devices, over_image(): return lax.ppermute(x, 'image', [(i, i ^ m) for i in range(images)])  8.96 us
    ppermute x8, waiting for transfers between devices, over_image(): return lax.ppermute(x, 'image', [(i, i ^ m) for i in range(images)])  7.96 us
    ppermute x4, starting transfers between devices, to_targets(): return lax.ppermute(x, 'token', pairs)  7.67 us
    ppermute x3, waiting for transfers between devices, over_z(): lax.ppermute(x, 'token', [(t, (t // span ^ m) * span + t % span) for t in...  6.35 us
    all_to_all x1, starting transfers between devices, body(): gathered = lax.all_to_all(blocks, 'token', 0, 0, axis_index_groups=z_groups)  5.33 us
    ppermute x3, starting transfers between devices, over_z(): lax.ppermute(x, 'token', [(t, (t // span ^ m) * span + t % span) for t in...  4.45 us
  transfers between devices with their start and end apart: 19, of which 11 were waited for; matrix products, arithmetic and copies ran while one was open for 3% of the time, Pallas kernels for 20%

profile of v3, /device:TPU:0, one launch (start us, length us, event | category | flops | bytes accessed | tf_op | source)
XLA Modules:
  0.0 87.6 jit_solution(6073000200299059601)
XLA Ops:
  0.0 0.5 collective-permute-start
  0.5 1.3 %shard_map.82.refs_0_ = bf16[768,512]{1,0:T(8,128)(2,1)S(1)} custom-call(s32[1]{0:T(128)} %bitcast.8.core_ref, bf16[768,1536]{1,0:T(8,128)(2,1)} %w_ref.3), custom_call_target="tpu_custom_call" | custom-call | tf_op jit(solution)/shard_map/pallas_call | solution.py:24
  1.8 2.6 %collective-permute-start.3 = (bf16[768,512]{1,0:T(8,128)(2,1)S(1)}, bf16[768,512]{1,0:T(8,128)(2,1)S(1)}, u32[]{:S(2)}, u32[]{:S(2)}) collective-permute-start(bf16[768,512]{1,0:T(8,128)(2,1)S(1)} %shard_map.82.refs_0_), channel_id=1, source_target_pairs={{0,8},{8,0},{16,24},{24,16},{1,9},{9,1},{17,25},{25,17},{2,10},{10... | collective-permute-start | bytes 2359304 | tf_op jit(solution)/shard_map/ppermute | solution.py:381
  4.4 1.5 %collective-permute-start.4 = (bf16[768,512]{1,0:T(8,128)(2,1)S(1)}, bf16[768,512]{1,0:T(8,128)(2,1)}, u32[]{:S(2)}, u32[]{:S(2)}) collective-permute-start(bf16[768,512]{1,0:T(8,128)(2,1)S(1)} %shard_map.82.refs_0_), channel_id=1, source_target_pairs={{0,16},{8,24},{16,0},{24,8},{1,17},{9,25},{17,1},{25,9},{2,18},{10... | collective-permute-start | bytes 2359304 | tf_op jit(solution)/shard_map/ppermute | solution.py:381
  5.9 2.3 %shard_map.83.refs_0_ = bf16[4,2,2,128,384]{4,3,2,1,0:T(8,128)(2,1)} custom-call(bf16[2,128,1536]{2,1,0:T(8,128)(2,1)} %bitcast.19, bf16[2,128,1536]{2,1,0:T(8,128)(2,1)} %bitcast.20, bf16[768,512]{1,0:T(8,128)(2,1)S(1)} %shard_map.82.refs_0_), custom_call_target="tpu_custom_call" | custom-call | tf_op jit(solution)/shard_map/pallas_call | solution.py:24
  8.2 1.1 %shard_map.84.refs_0_ = bf16[768,256]{1,0:T(8,128)(2,1)S(1)} custom-call(s32[1]{0:T(128)} %bitcast.8.core_ref, bf16[768,1536]{1,0:T(8,128)(2,1)} %w_ref.3, bf16[4,2,2,128,384]{4,3,2,1,0:T(8,128)(2,1)} %shard_map.83.refs_0_), custom_call_target="tpu_custom_call" | custom-call | tf_op jit(solution)/shard_map/pallas_call | solution.py:24
  9.3 0.0 copy-start.2
  9.3 0.6 collective-permute-start.1
  9.9 0.1 collective-permute-start.2
  10.0 5.3 %all-to-all-start = ((bf16[4,2,2,128,384]{4,3,2,1,0:T(8,128)(2,1)}), bf16[4,2,2,128,384]{4,3,2,1,0:T(8,128)(2,1)S(1)}, u32[]{:S(2)}, u32[]{:S(2)}) async-start(bf16[4,2,2,128,384]{4,3,2,1,0:T(8,128)(2,1)} %shard_map.83.refs_0_), calls=%async_computation | async-start | bytes 3145728 | tf_op jit(solution)/shard_map/all_to_all | solution.py:462
  15.3 0.0 copy-done.2
  15.3 0.6 constant_dynamic-slice_fusion
  19.2 0.7 fusion.1
  19.9 1.3 %concatenate.3._.s_ref = s32[7]{0:T(128)S(1)} concatenate(s32[1]{0:T(128)} %bitcast, s32[1]{0:T(128)} %bitcast.1, s32[1]{0:T(128)} %bitcast.3, s32[1]{0:T(128)} %get-tuple-element.32, s32[1]{0:T(128)} %get-tuple-element.31, s32[2]{0:T(128)S(1)} %get-tuple-element.29), dimensions={0} | concatenate | bytes 56 | tf_op jit(solution)/shard_map/concatenate | solution.py:421
  21.2 0.0 copy-start.1
  21.2 1.5 %collective-permute-done.3.x_ref.refs_1_ = bf16[768,512]{1,0:T(8,128)(2,1)S(1)} collective-permute-done((bf16[768,512]{1,0:T(8,128)(2,1)S(1)}, bf16[768,512]{1,0:T(8,128)(2,1)S(1)}, u32[]{:S(2)}, u32[]{:S(2)}) %collective-permute-start.3) | collective-permute-done | bytes 786464 | tf_op jit(solution)/shard_map/ppermute | solution.py:381
  22.8 2.1 %collective-permute-done.4.y_ref.refs_2_ = bf16[768,512]{1,0:T(8,128)(2,1)} collective-permute-done((bf16[768,512]{1,0:T(8,128)(2,1)S(1)}, bf16[768,512]{1,0:T(8,128)(2,1)}, u32[]{:S(2)}, u32[]{:S(2)}) %collective-permute-start.4) | collective-permute-done | bytes 786464 | tf_op jit(solution)/shard_map/ppermute | solution.py:381
  24.8 2.1 %shard_map.85 = (bf16[384,512]{1,0:T(8,128)(2,1)S(1)}, bf16[384,512]{1,0:T(8,128)(2,1)S(1)}) custom-call(s32[7]{0:T(128)S(1)} %concatenate.3._.s_ref, bf16[768,512]{1,0:T(8,128)(2,1)S(1)} %collective-permute-done.3.x_ref.refs_1_, bf16[768,512]{1,0:T(8,128)(2,1)} %collective-permute-done.4.y_ref.refs_2_, bf16[768,256]{1,0:T(8,128)(2,1)S(1)} %shard_map.84.refs_0_), custom_call_target="tpu_custom_call" | custom-call | tf_op jit(solution)/shard_map/pallas_call | solution.py:24
  27.0 1.6 %collective-permute-start.7 = (bf16[384,512]{1,0:T(8,128)(2,1)S(1)}, bf16[384,512]{1,0:T(8,128)(2,1)S(1)}, u32[]{:S(2)}, u32[]{:S(2)}) collective-permute-start(bf16[384,512]{1,0:T(8,128)(2,1)S(1)} %get-tuple-element.17.refs_3_), channel_id=1, source_target_pairs={{0,16},{8,24},{16,0},{24,8},{1,17},{9,25},{17,1},{25,9},{2,18},{10... | collective-permute-start | bytes 1179656 | tf_op jit(solution)/shard_map/ppermute | solution.py:381
  28.6 0.5 collective-permute-start.8
  29.1 0.0 collective-permute-done.other_ref
  29.1 0.0 copy-done.1
  29.1 3.3 %shard_map.86 = (f32[2,256,512]{2,1,0:T(8,128)S(1)}, bf16[2,256,768]{2,1,0:T(8,128)(2,1)S(1)}) custom-call(s32[7]{0:T(128)S(1)} %concatenate.3._.s_ref, bf16[2,128,3072]{2,1,0:T(8,128)(2,1)S(1)} %bitcast.17, bf16[2,128,3072]{2,1,0:T(8,128)(2,1)} %collective-permute-done.other_ref, bf16[768,512]{1,0:T(8,128)(2,1)S(1)} %shard_map.82.refs_0_, ...), custom_call_target="tpu_custom_call" | custom-call | flops 24999999488 | tf_op jit(solution)/shard_map/pallas_call | solution.py:24
  32.4 0.0 collective-permute-done.1.x_ref.refs_1_
  32.4 0.8 collective-permute-done.2.y_ref.refs_2_
  33.3 2.1 %shard_map.87 = (bf16[384,256]{1,0:T(8,128)(2,1)S(1)}, bf16[384,256]{1,0:T(8,128)(2,1)S(1)}) custom-call(s32[7]{0:T(128)S(1)} %concatenate.3._.s_ref, bf16[768,256]{1,0:T(8,128)(2,1)} %collective-permute-done.1.x_ref.refs_1_, bf16[768,256]{1,0:T(8,128)(2,1)} %collective-permute-done.2.y_ref.refs_2_, bf16[2,256,768]{2,1,0:T(8,128)(2,1)S(1)} %get-tuple-element.18.refs_0_.far_ref), custom_call_target="tpu_custom_call" | custom-call | tf_op jit(solution)/shard_map/pallas_call | solution.py:24
  35.3 1.6 %collective-permute-start.5 = (bf16[384,256]{1,0:T(8,128)(2,1)S(1)}, bf16[384,256]{1,0:T(8,128)(2,1)S(1)}, u32[]{:S(2)}, u32[]{:S(2)}) collective-permute-start(bf16[384,256]{1,0:T(8,128)(2,1)S(1)} %get-tuple-element.19.refs_3_), channel_id=1, source_target_pairs={{0,16},{8,24},{16,0},{24,8},{1,17},{9,25},{17,1},{25,9},{2,18},{10... | collective-permute-start | bytes 589832 | tf_op jit(solution)/shard_map/ppermute | solution.py:381
  36.9 0.5 collective-permute-start.6
  37.5 2.9 %shard_map.88 = (f32[2,256,256]{2,1,0:T(8,128)S(1)}, bf16[2,256,768]{2,1,0:T(8,128)(2,1)S(1)}) custom-call(s32[7]{0:T(128)S(1)} %concatenate.3._.s_ref, bf16[2,128,3072]{2,1,0:T(8,128)(2,1)S(1)} %bitcast.18, bf16[2,128,3072]{2,1,0:T(8,128)(2,1)} %collective-permute-done.other_ref, bf16[768,256]{1,0:T(8,128)(2,1)S(1)} %shard_map.84.refs_0_, ...), custom_call_target="tpu_custom_call" | custom-call | flops 24999999488 | tf_op jit(solution)/shard_map/pallas_call | solution.py:24
  40.3 1.2 %collective-permute-done.7.refs_0_ = bf16[384,512]{1,0:T(8,128)(2,1)S(1)} collective-permute-done((bf16[384,512]{1,0:T(8,128)(2,1)S(1)}, bf16[384,512]{1,0:T(8,128)(2,1)S(1)}, u32[]{:S(2)}, u32[]{:S(2)}) %collective-permute-start.7) | collective-permute-done | bytes 393248 | tf_op jit(solution)/shard_map/ppermute | solution.py:381
  41.6 0.0 collective-permute-done.8.refs_1_
  41.6 1.2 %shard_map.89.refs_2_ = bf16[4,256,256]{2,1,0:T(8,128)(2,1)S(1)} custom-call(s32[7]{0:T(128)S(1)} %concatenate.3._.s_ref, f32[2,256,512]{2,1,0:T(8,128)S(1)} %get-tuple-element.23.t_ref, bf16[2,256,768]{2,1,0:T(8,128)(2,1)S(1)} %get-tuple-element.18.refs_0_.far_ref, bf16[384,512]{1,0:T(8,128)(2,1)S(1)} %collective-permute-done.7.refs_0_, ...), custom_call_target="tpu_custom_call" | custom-call | tf_op jit(solution)/shard_map/pallas_call | solution.py:24
  42.8 2.3 %collective-permute-done.5.refs_0_ = bf16[384,256]{1,0:T(8,128)(2,1)S(1)} collective-permute-done((bf16[384,256]{1,0:T(8,128)(2,1)S(1)}, bf16[384,256]{1,0:T(8,128)(2,1)S(1)}, u32[]{:S(2)}, u32[]{:S(2)}) %collective-permute-start.5) | collective-permute-done | bytes 196640 | tf_op jit(solution)/shard_map/ppermute | solution.py:381
  45.1 0.0 collective-permute-done.6.refs_1_
  45.1 1.0 %shard_map.90 = (bf16[256,384]{1,0:T(8,128)(2,1)S(1)}, bf16[256,384]{1,0:T(8,128)(2,1)S(1)}, bf16[256,384]{1,0:T(8,128)(2,1)S(1)}, bf16[256,384]{1,0:T(8,128)(2,1)S(1)}) custom-call(s32[7]{0:T(128)S(1)} %concatenate.3._.s_ref, f32[2,256,256]{2,1,0:T(8,128)S(1)} %get-tuple-element.20.t_ref, bf16[2,256,768]{2,1,0:T(8,128)(2,1)S(1)} %get-tuple-element.21.refs_2_.far_ref, ...), custom_call_target="tpu_custom_call" | custom-call | tf_op jit(solution)/shard_map/pallas_call | solution.py:24
  46.1 1.9 %collective-permute-start.10 = (bf16[256,384]{1,0:T(8,128)(2,1)S(1)}, bf16[256,384]{1,0:T(8,128)(2,1)S(1)}, u32[]{:S(2)}, u32[]{:S(2)}) collective-permute-start(bf16[256,384]{1,0:T(8,128)(2,1)S(1)} %get-tuple-element.26), channel_id=1, source_target_pairs={{0,1},{1,5},{2,2},{3,6},{4,3},{5,7},{6,0},{7,4},{8,9},{9,13},{10,1... | collective-permute-start | bytes 589832 | tf_op jit(solution)/shard_map/ppermute | solution.py:396
  48.1 0.7 collective-permute-start.9
  48.7 8.6 %collective-permute-done.10.refs_3_.refs_1_ = bf16[256,384]{1,0:T(8,128)(2,1)S(1)} collective-permute-done((bf16[256,384]{1,0:T(8,128)(2,1)S(1)}, bf16[256,384]{1,0:T(8,128)(2,1)S(1)}, u32[]{:S(2)}, u32[]{:S(2)}) %collective-permute-start.10) | collective-permute-done | bytes 196640 | tf_op jit(solution)/shard_map/ppermute | solution.py:396
  57.4 0.0 collective-permute-done.9.refs_2_.refs_0_
  57.4 0.0 all-to-all-done.refs_0_
  57.4 0.7 collective-permute-start.13
  58.1 3.1 %collective-permute-start.11 = (bf16[256,384]{1,0:T(8,128)(2,1)S(1)}, bf16[256,384]{1,0:T(8,128)(2,1)S(1)}, u32[]{:S(2)}, u32[]{:S(2)}) collective-permute-start(bf16[256,384]{1,0:T(8,128)(2,1)S(1)} %get-tuple-element.27), channel_id=1, source_target_pairs={{0,2},{1,6},{2,3},{3,7},{4,0},{5,4},{6,1},{7,5},{8,10},{9,14},{10,... | collective-permute-start | bytes 589832 | tf_op jit(solution)/shard_map/ppermute | solution.py:396
  61.2 2.0 %collective-permute-start.12 = (bf16[256,384]{1,0:T(8,128)(2,1)S(1)}, bf16[256,384]{1,0:T(8,128)(2,1)S(1)}, u32[]{:S(2)}, u32[]{:S(2)}) collective-permute-start(bf16[256,384]{1,0:T(8,128)(2,1)S(1)} %get-tuple-element.28), channel_id=1, source_target_pairs={{0,3},{1,7},{2,0},{3,4},{4,1},{5,5},{6,2},{7,6},{8,11},{9,15},{10,... | collective-permute-start | bytes 589832 | tf_op jit(solution)/shard_map/ppermute | solution.py:396
  63.8 0.0 copy-start
  63.8 3.6 %collective-permute-done.11.refs_2_ = bf16[256,384]{1,0:T(8,128)(2,1)S(1)} collective-permute-done((bf16[256,384]{1,0:T(8,128)(2,1)S(1)}, bf16[256,384]{1,0:T(8,128)(2,1)S(1)}, u32[]{:S(2)}, u32[]{:S(2)}) %collective-permute-start.11) | collective-permute-done | bytes 196640 | tf_op jit(solution)/shard_map/ppermute | solution.py:396
  67.4 2.4 %collective-permute-done.12.refs_3_ = bf16[256,384]{1,0:T(8,128)(2,1)S(1)} collective-permute-done((bf16[256,384]{1,0:T(8,128)(2,1)S(1)}, bf16[256,384]{1,0:T(8,128)(2,1)S(1)}, u32[]{:S(2)}, u32[]{:S(2)}) %collective-permute-start.12) | collective-permute-done | bytes 196640 | tf_op jit(solution)/shard_map/ppermute | solution.py:396
  69.8 0.0 collective-permute-done.13.refs_5_
  69.8 3.5 %shard_map.92.refs_0_ = bf16[128,384]{1,0:T(8,128)(2,1)S(1)} custom-call(s32[7]{0:T(128)S(1)} %concatenate.3._.s_ref, f32[1]{0:T(128)S(6)} %copy.11.g_ref, bf16[256,384]{1,0:T(8,128)(2,1)S(1)} %collective-permute-done.9.refs_2_.refs_0_, bf16[256,384]{1,0:T(8,128)(2,1)S(1)} %collective-permute-done.10.refs_3_.refs_1_, ...), custom_call_target="tpu_custom_call" | custom-call | tf_op jit(solution)/shard_map/pallas_call | solution.py:24
  73.3 0.5 collective-permute-start.14
  73.8 2.0 %collective-permute-start.15 = (bf16[128,384]{1,0:T(8,128)(2,1)S(1)}, bf16[128,384]{1,0:T(8,128)(2,1)S(1)}, u32[]{:S(2)}, u32[]{:S(2)}) collective-permute-start(bf16[128,384]{1,0:T(8,128)(2,1)S(1)} %shard_map.92.refs_0_), channel_id=1, source_target_pairs={{0,4},{1,5},{2,6},{3,7},{4,0},{5,1},{6,2},{7,3},{8,12},{9,13},{10,... | collective-permute-start | bytes 294920 | tf_op jit(solution)/shard_map/ppermute | solution.py:385
  75.8 2.0 %collective-permute-start.16 = (bf16[128,384]{1,0:T(8,128)(2,1)S(1)}, bf16[128,384]{1,0:T(8,128)(2,1)S(1)}, u32[]{:S(2)}, u32[]{:S(2)}) collective-permute-start(bf16[128,384]{1,0:T(8,128)(2,1)S(1)} %shard_map.92.refs_0_), channel_id=1, source_target_pairs={{0,6},{1,7},{2,4},{3,5},{4,2},{5,3},{6,0},{7,1},{8,14},{9,15},{10,... | collective-permute-start | bytes 294920 | tf_op jit(solution)/shard_map/ppermute | solution.py:385
  77.7 2.3 %collective-permute-done.14.refs_1_ = bf16[128,384]{1,0:T(8,128)(2,1)S(1)} collective-permute-done((bf16[128,384]{1,0:T(8,128)(2,1)S(1)}, bf16[128,384]{1,0:T(8,128)(2,1)S(1)}, u32[]{:S(2)}, u32[]{:S(2)}) %collective-permute-start.14) | collective-permute-done | bytes 98336 | tf_op jit(solution)/shard_map/ppermute | solution.py:385
  80.0 0.0 collective-permute-done.15.refs_2_
  80.0 4.1 %collective-permute-done.16.refs_3_ = bf16[128,384]{1,0:T(8,128)(2,1)S(1)} collective-permute-done((bf16[128,384]{1,0:T(8,128)(2,1)S(1)}, bf16[128,384]{1,0:T(8,128)(2,1)S(1)}, u32[]{:S(2)}, u32[]{:S(2)}) %collective-permute-start.16) | collective-permute-done | bytes 98336 | tf_op jit(solution)/shard_map/ppermute | solution.py:385
  84.1 0.8 collective-permute-start.17
  85.0 1.3 %collective-permute-done.17.refs_4_ = bf16[4,128,384]{2,1,0:T(8,128)(2,1)S(1)} collective-permute-done((bf16[4,128,384]{2,1,0:T(8,128)(2,1)S(1)}, bf16[4,128,384]{2,1,0:T(8,128)(2,1)S(1)}, u32[]{:S(2)}, u32[]{:S(2)}) %collective-permute-start.17) | collective-permute-done | bytes 393248 | tf_op jit(solution)/shard_map/ppermute | solution.py:388
  86.3 0.0 copy-done
  86.3 1.3 %shard_map.94 = bf16[128,1536]{1,0:T(8,128)(2,1)} custom-call(s32[7]{0:T(128)S(1)} %concatenate.3._.s_ref, bf16[128,1536]{1,0:T(8,128)(2,1)S(1)} %bitcast.15, bf16[128,384]{1,0:T(8,128)(2,1)S(1)} %shard_map.92.refs_0_, bf16[128,384]{1,0:T(8,128)(2,1)S(1)} %collective-permute-done.14.refs_1_, bf16[128,384]{1,0:T(8,128)(2,1)S(1)} %collective-permute-done.15.refs_2_, ...), custom_call_target="tpu_custom_call" | custom-call | tf_op jit(solution)/shard_map/pallas_call | solution.py:24
  (3 shorter events, 0.0 us)
Async XLA Ops:
  0.0 29.1 %collective-permute-start = (bf16[2,128,3072]{2,1,0:T(8,128)(2,1)}, bf16[2,128,3072]{2,1,0:T(8,128)(2,1)}, u32[]{:S(2)}, u32[]{:S(2)}) collective-permute-start(bf16[2,128,3072]{2,1,0:T(8,128)(2,1)} %bitcast.16), channel_id=1, source_target_pairs={{0,1},{1,0},{2,3},{3,2},{4,5},{5,4},{6,7},{7,6},{8,9},{9,8},{10,11... | collective-permute-start | bytes 4718600 | tf_op jit(solution)/shard_map/ppermute | solution.py:388
  1.8 20.9 %collective-permute-start.3 = (bf16[768,512]{1,0:T(8,128)(2,1)S(1)}, bf16[768,512]{1,0:T(8,128)(2,1)S(1)}, u32[]{:S(2)}, u32[]{:S(2)}) collective-permute-start(bf16[768,512]{1,0:T(8,128)(2,1)S(1)} %shard_map.82.refs_0_), channel_id=1, source_target_pairs={{0,8},{8,0},{16,24},{24,16},{1,9},{9,1},{17,25},{25,17},{2,10},{10... | collective-permute-start | bytes 2359304 | tf_op jit(solution)/shard_map/ppermute | solution.py:381
  4.4 20.5 %collective-permute-start.4 = (bf16[768,512]{1,0:T(8,128)(2,1)S(1)}, bf16[768,512]{1,0:T(8,128)(2,1)}, u32[]{:S(2)}, u32[]{:S(2)}) collective-permute-start(bf16[768,512]{1,0:T(8,128)(2,1)S(1)} %shard_map.82.refs_0_), channel_id=1, source_target_pairs={{0,16},{8,24},{16,0},{24,8},{1,17},{9,25},{17,1},{25,9},{2,18},{10... | collective-permute-start | bytes 2359304 | tf_op jit(solution)/shard_map/ppermute | solution.py:381
  9.3 6.0 %copy-start.2 = (s32[1,2]{1,0:T(1,128)S(1)}, s32[1,2]{1,0:T(1,128)}, u32[]{:S(2)}) copy-start(s32[1,2]{1,0:T(1,128)} %param.14) | copy-start | bytes 28
  9.3 23.1 %collective-permute-start.1 = (bf16[768,256]{1,0:T(8,128)(2,1)S(1)}, bf16[768,256]{1,0:T(8,128)(2,1)}, u32[]{:S(2)}, u32[]{:S(2)}) collective-permute-start(bf16[768,256]{1,0:T(8,128)(2,1)S(1)} %shard_map.84.refs_0_), channel_id=1, source_target_pairs={{0,8},{8,0},{16,24},{24,16},{1,9},{9,1},{17,25},{25,17},{2,10},{10... | collective-permute-start | bytes 1179656 | tf_op jit(solution)/shard_map/ppermute | solution.py:381
  9.9 23.3 %collective-permute-start.2 = (bf16[768,256]{1,0:T(8,128)(2,1)S(1)}, bf16[768,256]{1,0:T(8,128)(2,1)}, u32[]{:S(2)}, u32[]{:S(2)}) collective-permute-start(bf16[768,256]{1,0:T(8,128)(2,1)S(1)} %shard_map.84.refs_0_), channel_id=1, source_target_pairs={{0,16},{8,24},{16,0},{24,8},{1,17},{9,25},{17,1},{25,9},{2,18},{10... | collective-permute-start | bytes 1179656 | tf_op jit(solution)/shard_map/ppermute | solution.py:381
  10.0 47.4 %all-to-all-start = ((bf16[4,2,2,128,384]{4,3,2,1,0:T(8,128)(2,1)}), bf16[4,2,2,128,384]{4,3,2,1,0:T(8,128)(2,1)S(1)}, u32[]{:S(2)}, u32[]{:S(2)}) async-start(bf16[4,2,2,128,384]{4,3,2,1,0:T(8,128)(2,1)} %shard_map.83.refs_0_), calls=%async_computation | async-start | bytes 3145728 | tf_op jit(solution)/shard_map/all_to_all | solution.py:462
  21.2 7.9 %copy-start.1 = (bf16[2,1,128,3072]{3,2,1,0:T(8,128)(2,1)S(1)}, bf16[2,1,128,3072]{3,2,1,0:T(8,128)(2,1)}, u32[]{:S(2)}) copy-start(bf16[2,1,128,3072]{3,2,1,0:T(8,128)(2,1)} %param.8) | copy-start | bytes 4718596
  27.0 14.6 %collective-permute-start.7 = (bf16[384,512]{1,0:T(8,128)(2,1)S(1)}, bf16[384,512]{1,0:T(8,128)(2,1)S(1)}, u32[]{:S(2)}, u32[]{:S(2)}) collective-permute-start(bf16[384,512]{1,0:T(8,128)(2,1)S(1)} %get-tuple-element.17.refs_3_), channel_id=1, source_target_pairs={{0,16},{8,24},{16,0},{24,8},{1,17},{9,25},{17,1},{25,9},{2,18},{10... | collective-permute-start | bytes 1179656 | tf_op jit(solution)/shard_map/ppermute | solution.py:381
  28.6 13.0 %collective-permute-start.8 = (bf16[384,512]{1,0:T(8,128)(2,1)S(1)}, bf16[384,512]{1,0:T(8,128)(2,1)S(1)}, u32[]{:S(2)}, u32[]{:S(2)}) collective-permute-start(bf16[384,512]{1,0:T(8,128)(2,1)S(1)} %get-tuple-element.24), channel_id=1, source_target_pairs={{0,8},{8,0},{16,24},{24,16},{1,9},{9,1},{17,25},{25,17},{2,10},{10... | collective-permute-start | bytes 1179656 | tf_op jit(solution)/shard_map/ppermute | solution.py:381
  35.3 9.8 %collective-permute-start.5 = (bf16[384,256]{1,0:T(8,128)(2,1)S(1)}, bf16[384,256]{1,0:T(8,128)(2,1)S(1)}, u32[]{:S(2)}, u32[]{:S(2)}) collective-permute-start(bf16[384,256]{1,0:T(8,128)(2,1)S(1)} %get-tuple-element.19.refs_3_), channel_id=1, source_target_pairs={{0,16},{8,24},{16,0},{24,8},{1,17},{9,25},{17,1},{25,9},{2,18},{10... | collective-permute-start | bytes 589832 | tf_op jit(solution)/shard_map/ppermute | solution.py:381
  36.9 8.2 %collective-permute-start.6 = (bf16[384,256]{1,0:T(8,128)(2,1)S(1)}, bf16[384,256]{1,0:T(8,128)(2,1)S(1)}, u32[]{:S(2)}, u32[]{:S(2)}) collective-permute-start(bf16[384,256]{1,0:T(8,128)(2,1)S(1)} %get-tuple-element.22), channel_id=1, source_target_pairs={{0,8},{8,0},{16,24},{24,16},{1,9},{9,1},{17,25},{25,17},{2,10},{10... | collective-permute-start | bytes 589832 | tf_op jit(solution)/shard_map/ppermute | solution.py:381
  46.1 11.2 %collective-permute-start.10 = (bf16[256,384]{1,0:T(8,128)(2,1)S(1)}, bf16[256,384]{1,0:T(8,128)(2,1)S(1)}, u32[]{:S(2)}, u32[]{:S(2)}) collective-permute-start(bf16[256,384]{1,0:T(8,128)(2,1)S(1)} %get-tuple-element.26), channel_id=1, source_target_pairs={{0,1},{1,5},{2,2},{3,6},{4,3},{5,7},{6,0},{7,4},{8,9},{9,13},{10,1... | collective-permute-start | bytes 589832 | tf_op jit(solution)/shard_map/ppermute | solution.py:396
  48.1 9.3 %collective-permute-start.9 = (bf16[256,384]{1,0:T(8,128)(2,1)S(1)}, bf16[256,384]{1,0:T(8,128)(2,1)S(1)}, u32[]{:S(2)}, u32[]{:S(2)}) collective-permute-start(bf16[256,384]{1,0:T(8,128)(2,1)S(1)} %get-tuple-element.25.refs_1_), channel_id=1, source_target_pairs={{0,0},{1,4},{2,1},{3,5},{4,2},{5,6},{6,3},{7,7},{8,8},{9,12},{10,9... | collective-permute-start | bytes 589832 | tf_op jit(solution)/shard_map/ppermute | solution.py:396
  57.4 12.4 %collective-permute-start.13 = (bf16[4,2,2,128,384]{4,3,2,1,0:T(8,128)(2,1)S(1)}, bf16[4,2,2,128,384]{4,3,2,1,0:T(8,128)(2,1)S(1)}, u32[]{:S(2)}, u32[]{:S(2)}) collective-permute-start(bf16[4,2,2,128,384]{4,3,2,1,0:T(8,128)(2,1)S(1)} %shard_map.91.refs_4_), channel_id=1, source_target_pairs={{0,1},{1,0},{2,3},{3,2},{4,5},{5,4},{6,7},{7,6},{8,9},{9,8},{10,11... | collective-permute-start | bytes 4718600 | tf_op jit(solution)/shard_map/ppermute | solution.py:388
  58.1 9.3 %collective-permute-start.11 = (bf16[256,384]{1,0:T(8,128)(2,1)S(1)}, bf16[256,384]{1,0:T(8,128)(2,1)S(1)}, u32[]{:S(2)}, u32[]{:S(2)}) collective-permute-start(bf16[256,384]{1,0:T(8,128)(2,1)S(1)} %get-tuple-element.27), channel_id=1, source_target_pairs={{0,2},{1,6},{2,3},{3,7},{4,0},{5,4},{6,1},{7,5},{8,10},{9,14},{10,... | collective-permute-start | bytes 589832 | tf_op jit(solution)/shard_map/ppermute | solution.py:396
  61.2 8.6 %collective-permute-start.12 = (bf16[256,384]{1,0:T(8,128)(2,1)S(1)}, bf16[256,384]{1,0:T(8,128)(2,1)S(1)}, u32[]{:S(2)}, u32[]{:S(2)}) collective-permute-start(bf16[256,384]{1,0:T(8,128)(2,1)S(1)} %get-tuple-element.28), channel_id=1, source_target_pairs={{0,3},{1,7},{2,0},{3,4},{4,1},{5,5},{6,2},{7,6},{8,11},{9,15},{10,... | collective-permute-start | bytes 589832 | tf_op jit(solution)/shard_map/ppermute | solution.py:396
  63.8 22.5 %copy-start = (bf16[1,128,1536]{2,1,0:T(8,128)(2,1)S(1)}, bf16[1,128,1536]{2,1,0:T(8,128)(2,1)}, u32[]{:S(2)}) copy-start(bf16[1,128,1536]{2,1,0:T(8,128)(2,1)} %param.11) | copy-start | bytes 1179652
  73.3 6.7 %collective-permute-start.14 = (bf16[128,384]{1,0:T(8,128)(2,1)S(1)}, bf16[128,384]{1,0:T(8,128)(2,1)S(1)}, u32[]{:S(2)}, u32[]{:S(2)}) collective-permute-start(bf16[128,384]{1,0:T(8,128)(2,1)S(1)} %shard_map.92.refs_0_), channel_id=1, source_target_pairs={{0,2},{1,3},{2,0},{3,1},{4,6},{5,7},{6,4},{7,5},{8,10},{9,11},{10,... | collective-permute-start | bytes 294920 | tf_op jit(solution)/shard_map/ppermute | solution.py:385
  73.8 6.3 %collective-permute-start.15 = (bf16[128,384]{1,0:T(8,128)(2,1)S(1)}, bf16[128,384]{1,0:T(8,128)(2,1)S(1)}, u32[]{:S(2)}, u32[]{:S(2)}) collective-permute-start(bf16[128,384]{1,0:T(8,128)(2,1)S(1)} %shard_map.92.refs_0_), channel_id=1, source_target_pairs={{0,4},{1,5},{2,6},{3,7},{4,0},{5,1},{6,2},{7,3},{8,12},{9,13},{10,... | collective-permute-start | bytes 294920 | tf_op jit(solution)/shard_map/ppermute | solution.py:385
  75.8 8.3 %collective-permute-start.16 = (bf16[128,384]{1,0:T(8,128)(2,1)S(1)}, bf16[128,384]{1,0:T(8,128)(2,1)S(1)}, u32[]{:S(2)}, u32[]{:S(2)}) collective-permute-start(bf16[128,384]{1,0:T(8,128)(2,1)S(1)} %shard_map.92.refs_0_), channel_id=1, source_target_pairs={{0,6},{1,7},{2,4},{3,5},{4,2},{5,3},{6,0},{7,1},{8,14},{9,15},{10,... | collective-permute-start | bytes 294920 | tf_op jit(solution)/shard_map/ppermute | solution.py:385
  84.1 2.2 %collective-permute-start.17 = (bf16[4,128,384]{2,1,0:T(8,128)(2,1)S(1)}, bf16[4,128,384]{2,1,0:T(8,128)(2,1)S(1)}, u32[]{:S(2)}, u32[]{:S(2)}) collective-permute-start(bf16[4,128,384]{2,1,0:T(8,128)(2,1)S(1)} %shard_map.93), channel_id=1, source_target_pairs={{0,1},{1,0},{2,3},{3,2},{4,5},{5,4},{6,7},{7,6},{8,9},{9,8},{10,11... | collective-permute-start | bytes 1179656 | tf_op jit(solution)/shard_map/ppermute | solution.py:388

commit v4 on v3

--- a/solution.py
+++ b/solution.py
@@ -133,21 +133,6 @@
             pltpu.SemaphoreType.DMA((2,)),
             pltpu.SemaphoreType.DMA((2,)),
         ],
-    )
-
-
-def stack(pieces):
-    def kernel(*refs):
-        for n in range(len(pieces)):
-            refs[-1][n] = refs[n][...]
-
-    return call(
-        kernel,
-        jax.ShapeDtypeStruct((len(pieces), *pieces[0].shape), BF),
-        [],
-        pieces,
-        spec=VMEM_SPEC,
-        out_spec=VMEM_SPEC,
     )
 
 
@@ -213,17 +198,16 @@
     )
 
 
-def finish_project(flags, sums, rows_far, pieces, earlier=None, events=()):
+def finish_project(flags, first_at, sums, rows_far, pieces, earlier=(), events=()):
     _, both, width = sums.shape
     part = width // 2
-    count = len(pieces)
-    last = earlier is not None
-    before = earlier.shape[2] if last else 0
+    count, kept = len(pieces), len(earlier)
+    before = earlier[0].shape[1] if earlier else 0
 
     def kernel(s_ref, t_ref, far_ref, *refs):
-        w_refs = refs[:count]
-        q_buf = refs[-1]
-        for slot in range(2):
+        w_refs, e_refs, out_refs = refs[:count], refs[count : count + kept], refs[-4:]
+        for n in range(2):
+            slot = s_ref[first_at] if n == 0 else 1
             total, first = t_ref[slot], 0
             for w_ref in w_refs:
                 size = w_ref.shape[0]
@@ -233,88 +217,104 @@
                 first += size
             total = total.astype(BF)
             for hi in range(2):
-                q_buf[hi * 2 + slot] = total[:, hi * part : (hi + 1) * part]
-        if last:
-            for r, out in enumerate(refs[-5:-1]):
-                target = (s_ref[1] + r) % 4
-                out[:, :before] = refs[count][target]
-                out[:, before:] = q_buf[target]
-
-    whole = jax.ShapeDtypeStruct((4, both, part), BF)
-    piece = jax.ShapeDtypeStruct((both, before + part), BF)
-    return call(
-        kernel,
-        [piece] * 4 if last else whole,
+                out_refs[n * 2 + hi][:, before:] = total[:, hi * part : (hi + 1) * part]
+        for e_ref, out in zip(e_refs, out_refs):
+            out[:, :before] = e_ref[...]
+
+    return call(
+        kernel,
+        [jax.ShapeDtypeStruct((both, before + part), BF)] * 4,
         [flags],
-        [sums, rows_far, *pieces, *([earlier] if last else []), *events],
-        [pltpu.VMEM((4, both, part), BF)] if last else [],
+        [sums, rows_far, *pieces, *earlier, *events],
         limit=8,
-        spec=[VMEM_SPEC] * (2 + count + last) + [ANY_SPEC] * len(events),
+        spec=[VMEM_SPEC] * (2 + count + kept) + [ANY_SPEC] * len(events),
         out_spec=VMEM_SPEC,
     )
 
 
-def attend(flags, guide, queries, caches):
-    count, parts, kept = len(queries[0]), len(queries), len(caches)
-    rows = queries[0][0].shape[0] // 2
-    widths = [part[0].shape[1] for part in queries]
+def attend(flags, guide, queries, caches, q_spec=VMEM_SPEC):
+    count, kept = len(queries), len(caches)
+    rows, width = queries[0].shape[0] // 2, queries[0].shape[1]
+    heads = width // HD
     scale = 1.0 / math.sqrt(HD)
     sizes = [c.shape[0] * c.shape[3] for c in caches]
+    firsts = [sum(sizes[:i]) for i in range(kept)]
     keys_all = sum(sizes)
+    step = 32 * 1024 // keys_all
+    places = [(b, head) for b in range(2) for head in range(heads // 2 * 2)]
+    places += [(b, head) for head in range(heads // 2 * 2, heads) for b in range(2)]
 
     def kernel(s_ref, g_ref, *refs):
-        q_refs, c_refs = refs[: parts * count], refs[parts * count : parts * count + kept]
-        out, q_buf = refs[-2:]
+        q_refs, c_refs = refs[:count], refs[count : count + kept]
+        out, q_buf, two_buf, s_buf, w_buf, sem = refs[-6:]
         for r in range(count):
 
             @pl.when(s_ref[2] == r)
             def _():
-                first = 0
-                for k in range(parts):
-                    q_buf[:, first : first + widths[k]] = q_refs[k * count + r][...]
-                    first += widths[k]
-
-        for head in range(sum(widths) // HD):
-            at = slice(head * HD, (head + 1) * HD)
-            attended = []
-            for b in range(2):
-                q = q_buf[b * rows : (b + 1) * rows, at]
-                scores = [
-                    lax.dot_general(
-                        q,
-                        c_ref[:, 0, b, :, at].reshape(size, HD),
-                        (((1,), (1,)), ((), ())),
-                        preferred_element_type=F32,
-                    )
-                    * scale
-                    for c_ref, size in zip(c_refs, sizes)
-                ]
-                top = jnp.max(scores[0], axis=-1, keepdims=True)
-                for s in scores[1:]:
-                    top = jnp.maximum(top, jnp.max(s, axis=-1, keepdims=True))
-                exps = [jnp.exp(s - top) for s in scores]
-                total = jnp.sum(exps[0], axis=-1, keepdims=True)
-                for e in exps[1:]:
-                    total = total + jnp.sum(e, axis=-1, keepdims=True)
-                over = 1.0 / total
-                result = jnp.zeros((rows, HD), F32)
-                for e, c_ref, size in zip(exps, c_refs, sizes):
-                    w = (e * over).astype(BF)
-                    result = result + jnp.dot(
-                        w, c_ref[:, 1, b, :, at].reshape(size, HD), preferred_element_type=F32
-                    )
-                attended.append(result)
-            guided = attended[1] + g_ref[0] * (attended[0] - attended[1])
-            out[:, at] = guided.astype(BF)
-
-    return call(
-        kernel,
-        jax.ShapeDtypeStruct((rows, sum(widths)), BF),
+                if q_spec is VMEM_SPEC:
+                    q_buf[...] = q_refs[r][...]
+                else:
+                    pltpu.make_async_copy(q_refs[r], q_buf, sem).start()
+
+        if q_spec is not VMEM_SPEC:
+            pltpu.make_async_copy(q_refs[0], q_buf, sem).wait()
+        attended = {}
+        for n in range(0, len(places), 2):
+            pair = places[n : n + 2]
+            (b0, h0), (b1, h1) = pair
+            turn = n // 2 % 2
+            q0 = q_buf[b0 * rows : (b0 + 1) * rows, h0 * HD : (h0 + 1) * HD]
+            q1 = q_buf[b1 * rows : (b1 + 1) * rows, h1 * HD : (h1 + 1) * HD]
+            none = jnp.zeros_like(q0)
+            q = jnp.concatenate(
+                [jnp.concatenate([q0, none], axis=1), jnp.concatenate([none, q1], axis=1)], axis=0
+            )
+
+            def sides(c_ref, kind, size, first):
+                if b0 == b1:
+                    return c_ref[:, kind, b0, :, h0 * HD : (h1 + 1) * HD].reshape(size, 2 * HD)
+                here = slice(first, first + size)
+                two_buf[kind, here, :HD] = c_ref[:, kind, b0, :, h0 * HD : (h0 + 1) * HD].reshape(size, HD)
+                two_buf[kind, here, HD:] = c_ref[:, kind, b1, :, h1 * HD : (h1 + 1) * HD].reshape(size, HD)
+                return two_buf[kind, here]
+
+            for c_ref, size, first in zip(c_refs, sizes, firsts):
+                s_buf[turn, :, first : first + size] = lax.dot_general(
+                    q, sides(c_ref, 0, size, first), (((1,), (1,)), ((), ())), preferred_element_type=F32
+                )
+            for row in range(0, 2 * rows, step):
+                here = slice(row, row + step)
+                scores = s_buf[turn, here] * scale
+                exps = jnp.exp(scores - jnp.max(scores, axis=-1, keepdims=True))
+                over = 1.0 / jnp.sum(exps, axis=-1, keepdims=True)
+                w_buf[turn, here] = (exps * over).astype(BF)
+            result = jnp.zeros((2 * rows, 2 * HD), F32)
+            for c_ref, size, first in zip(c_refs, sizes, firsts):
+                result = result + jnp.dot(
+                    w_buf[turn, :, first : first + size],
+                    sides(c_ref, 1, size, first),
+                    preferred_element_type=F32,
+                )
+            attended[pair[0]] = result[:rows, :HD]
+            attended[pair[1]] = result[rows:, HD:]
+        for head in range(heads):
+            guided = attended[1, head] + g_ref[0] * (attended[0, head] - attended[1, head])
+            out[:, head * HD : (head + 1) * HD] = guided.astype(BF)
+
+    return call(
+        kernel,
+        jax.ShapeDtypeStruct((rows, width), BF),
         [flags, guide],
-        [q for part in queries for q in part] + caches,
-        [pltpu.VMEM((2 * rows, sum(widths)), BF)],
-        limit=8 + 8 * (keys_all // 1024),
-        spec=VMEM_SPEC,
+        [*queries, *caches],
+        [
+            pltpu.VMEM((2 * rows, width), BF),
+            pltpu.VMEM((2, keys_all, 2 * HD), BF),
+            pltpu.VMEM((2, 2 * rows, keys_all), F32),
+            pltpu.VMEM((2, 2 * rows, keys_all), BF),
+            pltpu.SemaphoreType.DMA,
+        ],
+        limit=6 + 8 * (keys_all // 1024),
+        spec=[q_spec] * count + [VMEM_SPEC] * kept,
         out_spec=VMEM_SPEC,
     )
 
@@ -346,14 +346,17 @@
             @pl.when(s_ref[4 + n] == 1)
             def _():
                 run_all(
-                    [pltpu.make_async_copy(refs[GROUPS + n].at[m], place(m), sem.at[m]) for m in range(GROUPS)]
+                    [
+                        pltpu.make_async_copy(refs[GROUPS * (1 + n) + m], place(m), sem.at[m])
+                        for m in range(GROUPS)
+                    ]
                 )
 
     return call(
         kernel,
         jax.ShapeDtypeStruct((rows, columns), BF),
         [flags],
-        [previous, *mine, *others],
+        [previous, *mine, *[piece for other in others for piece in other]],
         [pltpu.SemaphoreType.DMA((GROUPS,))],
         spec=VMEM_SPEC,
     )
@@ -387,12 +390,7 @@
     def over_core(x):
         return lax.ppermute(x, "token", [(t, t ^ 1) for t in range(tokens)])
 
-    def to_targets(x, r):
-        pairs = []
-        for t in range(tokens):
-            c, at, s = t % 2, (t // 2) % layers, t // 2 // layers
-            goal = (s + r) % 4
-            pairs.append((t, ((2 * c + goal // 2) * layers + at) * 2 + goal % 2))
+    def send(x, pairs):
         return lax.ppermute(x, "token", pairs)
 
     layer_groups = [
@@ -410,18 +408,26 @@
     own_hidden = hidden[:, 0]
     other_hidden = over_core(own_hidden)
 
-    my_slot = layer * 2 + core
-    my_tile = tiles[my_slot]
-    target = 2 * (z % 2) + core
-    choice = (target - my_tile // 2 // layers) % 4
     in_use = jnp.arange(slots, dtype=jnp.int32) < mask_count[0]
     hit = ((tiles == token) & in_use).astype(jnp.int32)
+    my_slot = layer * 2 + core
     other_hits = hit[1 - core][None] if layers == 1 else jnp.where(jnp.arange(slots) == my_slot, 0, hit)
     is_own = (tiles % 2 == core).astype(jnp.int32)
+    if layers == 1:
+        owners = [tiles[0] // 2, tiles[1] // 2]
+        second = jnp.where(mask_count[0] > 1, owners[1], jnp.where(owners[0] < GROUPS // 2, GROUPS - 1, 0))
+        which = owners[0] * GROUPS + second
+        slot_first = (z != owners[0]).astype(jnp.int32)
+        choice = z % 2
+        extra = jnp.stack([slot_first, which]).astype(jnp.int32)
+    else:
+        choice = 0
+        extra = jnp.zeros((2,), jnp.int32)
     flags = jnp.concatenate(
-        [jnp.stack([image, z, choice, hit[my_slot]]).astype(jnp.int32), other_hits, is_own]
+        [jnp.stack([image, z, choice, hit[my_slot]]).astype(jnp.int32), other_hits, is_own, extra]
     )
     pairs_from = 4 + other_hits.shape[0]
+    first_at = pairs_from + slots
 
     def near(k, *events):
         own = pack_weights(core[None], w_query, part_heads(k), events)
@@ -439,23 +445,9 @@
             for at in range(layers)
         ]
 
-    def finish(begun_0, far_0, begun_1, far_1, *events):
-        result = None
-        for at in range(layers):
-            first = finish_project(flags, *begun_0[at], far_0, events=events)
-            sent = finish_project(flags, *begun_1[at], far_1, first)
-            came = [to_targets(x, r) for r, x in enumerate(sent)]
-            if layers > 1:
-                holds = (tiles[2 * at + core] // 2) % layers == layer
-                came = [
-                    lax.psum(jnp.where(holds, x, jnp.zeros_like(x)), "token", axis_index_groups=layer_groups)
-                    for x in came
-                ]
-            if result is None:
-                result = came
-            else:
-                result = [jnp.where(layer == at, new, old) for new, old in zip(came, result)]
-        return result, sent[0]
+    def finish(at, *events):
+        first = finish_project(flags, first_at, *begun_0[at], far_0, events=events)
+        return finish_project(flags, first_at, *begun_1[at], far_1, first)
 
     weights = [near(0)]
     blocks = pack_caches(key_cache[:, 0], value_cache[:, 0], weights[0][:1])
@@ -465,23 +457,60 @@
     begun_0 = begin(0, event)
     far_1, event = far(1, begun_0[0][1])
     begun_1 = begin(1, event)
-    queries, event = finish(begun_0, far_0, begun_1, far_1, begun_1[0][1])
-
-    gathered = after(gathered, event, queries[0], queries[1])
+
     if layers == 1:
+        sent = finish(0, begun_1[0][1])
+        gathered = after(gathered, sent[0])
         caches = [gathered, over_core(gathered)]
+
+        def ask(first, second):
+            def spread(x, hi, chips):
+                return send(
+                    x, [(2 * chips[slot] + c, 2 * (2 * c + hi) + slot) for slot in range(2) for c in range(2)]
+                )
+
+            def branch(sent):
+                if first != second:
+                    return [spread(sent[hi], hi, (first, second)) for hi in range(2)]
+                far_end = GROUPS - 1 if first < GROUPS // 2 else 0
+                for_first = [spread(sent[hi], hi, (first, far_end)) for hi in range(2)]
+                for_second = [spread(sent[2 + hi], hi, (far_end, first)) for hi in range(2)]
+                return [jnp.where(core == 0, a, b) for a, b in zip(for_first, for_second)]
+
+            return branch
+
+        branches = [ask(a, b) for a in range(GROUPS) for b in range(GROUPS)]
+        queries = lax.switch(which, branches, sent)
     else:
+        queries = None
+        for at in range(layers):
+            sent = finish(at, begun_1[at][1])
+            sent = jnp.stack([sent[0], sent[2], sent[1], sent[3]])
+            came = []
+            for r in range(4):
+                pairs = []
+                for t in range(tokens):
+                    c, here, s = t % 2, (t // 2) % layers, t // 2 // layers
+                    goal = (s + r) % 4
+                    pairs.append((t, ((2 * c + goal // 2) * layers + here) * 2 + goal % 2))
+                came.append(send(sent[(z + r) % 4], pairs))
+            slot = 2 * at + core
+            choice = (2 * (z % 2) + core - tiles[slot] // 2 // layers) % 4
+            holds = (tiles[slot] // 2) % layers == layer
+            came = jnp.where(holds, jnp.stack(came)[choice], jnp.zeros_like(came[0]))
+            came = lax.psum(came, "token", axis_index_groups=layer_groups)
+            queries = came if queries is None else jnp.where(layer == at, came, queries)
+        queries = [queries]
         everyone = lax.all_gather(gathered, "token", axis_index_groups=group_groups)
         caches = [everyone.reshape(-1, *gathered.shape[1:])]
 
-    guided = attend(flags, guide, [queries], caches)
+    guided = attend(flags, guide, queries, caches, ANY_SPEC)
     mine = [guided] + [over_z(guided, m) for m in range(1, GROUPS)]
-    stacked = stack(mine)
     if layers == 1:
-        others = [over_core(stacked)]
+        others = [[over_core(piece) for piece in mine]]
     else:
-        everyone = lax.all_gather(stacked, "token", axis_index_groups=group_groups)
-        others = [everyone[n] for n in range(slots)]
+        everyone = [lax.all_gather(piece, "token", axis_index_groups=group_groups) for piece in mine]
+        others = [[pieces[n] for pieces in everyone] for n in range(slots)]
     return paste(flags, cached_out[0], mine, others)[None]
 
 

time: 88.1 us -> 81.3 us (0.923)
  waiting for transfers between devices: 30.3 us -> 23.2 us
  starting transfers between devices: 28.4 us -> 25.5 us
  between operations: 4.11 us -> 6.63 us
    ppermute x4 -> x2, waiting for transfers between devices: 14.6 us -> 5.07 us  [send(): return lax.ppermute(x, 'token', pairs)]
    all_to_all x1, waiting for transfers between devices: 0.01 us -> 4.94 us  [body(): gathered = lax.all_to_all(blocks, 'token', 0, 0, axis_index_groups=z_groups)]
    ppermute x4 -> x2, starting transfers between devices: 7.67 us -> 4.4 us  [send(): return lax.ppermute(x, 'token', pairs)]
    ppermute x8, waiting for transfers between devices: 7.96 us -> 5.61 us  [over_image(): return lax.ppermute(x, 'image', [(i, i ^ m) for i in range(images)])]
    ppermute x3, starting transfers between devices: 4.45 us -> 5.85 us  [over_z(): lax.ppermute(x, 'token', [(t, (t // span ^ m) * span + t % span) for t in...]
    ppermute x3 -> x6, starting transfers between devices: 2.01 us -> 0.97 us  [over_core(): return lax.ppermute(x, 'token', [(t, t ^ 1) for t in range(tokens)])]
    pallas_call x13 -> x12, Pallas kernels: 22.2 us -> 22.8 us  [call(): pl.pallas_call(kernel, out_shape=out_shape, in_specs=[SMEM_SPEC] * len(sc...]
  transfers between devices with their start and end apart: 19 -> 20, of which waited for: 11 -> 10; matrix products, arithmetic and copies ran while one was open for 3% -> 3% of each run, Pallas kernels for 20% -> 22%
where the time goes in v4:
time: 81.3 us; the launch traced here: 80.7 us
  starting transfers between devices  25.5 us (31%)
  waiting for transfers between devices  23.2 us (29%)
  Pallas kernels  22.8 us (28%)
  between operations  6.63 us (8%)
  local copies, waits for them, and re-layouts  2.53 us (3%)
    pallas_call x12, Pallas kernels, call(): pl.pallas_call(kernel, out_shape=out_shape, in_specs=[SMEM_SPEC] * len(sc...  22.8 us
    ppermute x8, starting transfers between devices, over_image(): return lax.ppermute(x, 'image', [(i, i ^ m) for i in range(images)])  8.96 us
    ppermute x3, waiting for transfers between devices, over_z(): lax.ppermute(x, 'token', [(t, (t // span ^ m) * span + t % span) for t in...  6.65 us
    ppermute x3, starting transfers between devices, over_z(): lax.ppermute(x, 'token', [(t, (t // span ^ m) * span + t % span) for t in...  5.85 us
    ppermute x8, waiting for transfers between devices, over_image(): return lax.ppermute(x, 'image', [(i, i ^ m) for i in range(images)])  5.61 us
    all_to_all x1, starting transfers between devices, body(): gathered = lax.all_to_all(blocks, 'token', 0, 0, axis_index_groups=z_groups)  5.33 us
    ppermute x2, waiting for transfers between devices, send(): return lax.ppermute(x, 'token', pairs)  5.07 us
    all_to_all x1, waiting for transfers between devices, body(): gathered = lax.all_to_all(blocks, 'token', 0, 0, axis_index_groups=z_groups)  4.94 us
  transfers between devices with their start and end apart: 20, of which 10 were waited for; matrix products, arithmetic and copies ran while one was open for 3% of the time, Pallas kernels for 22%

profile of v4, /device:TPU:0, one launch (start us, length us, event | category | flops | bytes accessed | tf_op | source)
XLA Modules:
  0.0 80.7 jit_solution(8209209577915088100)
XLA Ops:
  0.0 0.5 collective-permute-start.40
  0.5 1.3 %shard_map.82.refs_0_ = bf16[768,512]{1,0:T(8,128)(2,1)S(1)} custom-call(s32[1]{0:T(128)} %bitcast.11.core_ref, bf16[768,1536]{1,0:T(8,128)(2,1)} %w_ref.3), custom_call_target="tpu_custom_call" | custom-call | tf_op jit(solution)/shard_map/pallas_call | solution.py:24
  1.8 2.6 %collective-permute-start.43 = (bf16[768,512]{1,0:T(8,128)(2,1)S(1)}, bf16[768,512]{1,0:T(8,128)(2,1)S(1)}, u32[]{:S(2)}, u32[]{:S(2)}) collective-permute-start(bf16[768,512]{1,0:T(8,128)(2,1)S(1)} %shard_map.82.refs_0_), channel_id=1, source_target_pairs={{0,8},{8,0},{16,24},{24,16},{1,9},{9,1},{17,25},{25,17},{2,10},{10... | collective-permute-start | bytes 2359304 | tf_op jit(solution)/shard_map/ppermute | solution.py:384
  4.4 1.5 %collective-permute-start.44 = (bf16[768,512]{1,0:T(8,128)(2,1)S(1)}, bf16[768,512]{1,0:T(8,128)(2,1)}, u32[]{:S(2)}, u32[]{:S(2)}) collective-permute-start(bf16[768,512]{1,0:T(8,128)(2,1)S(1)} %shard_map.82.refs_0_), channel_id=1, source_target_pairs={{0,16},{8,24},{16,0},{24,8},{1,17},{9,25},{17,1},{25,9},{2,18},{10... | collective-permute-start | bytes 2359304 | tf_op jit(solution)/shard_map/ppermute | solution.py:384
  5.9 2.3 %shard_map.83.refs_0_ = bf16[4,2,2,128,384]{4,3,2,1,0:T(8,128)(2,1)} custom-call(bf16[2,128,1536]{2,1,0:T(8,128)(2,1)} %bitcast.23, bf16[2,128,1536]{2,1,0:T(8,128)(2,1)} %bitcast.24, bf16[768,512]{1,0:T(8,128)(2,1)S(1)} %shard_map.82.refs_0_), custom_call_target="tpu_custom_call" | custom-call | tf_op jit(solution)/shard_map/pallas_call | solution.py:24
  8.2 1.1 %shard_map.84.refs_0_ = bf16[768,256]{1,0:T(8,128)(2,1)S(1)} custom-call(s32[1]{0:T(128)} %bitcast.11.core_ref, bf16[768,1536]{1,0:T(8,128)(2,1)} %w_ref.3, bf16[4,2,2,128,384]{4,3,2,1,0:T(8,128)(2,1)} %shard_map.83.refs_0_), custom_call_target="tpu_custom_call" | custom-call | tf_op jit(solution)/shard_map/pallas_call | solution.py:24
  9.3 0.0 copy-start.2
  9.3 0.6 collective-permute-start.41
  9.9 0.1 collective-permute-start.42
  10.0 5.3 %all-to-all-start = ((bf16[4,2,2,128,384]{4,3,2,1,0:T(8,128)(2,1)}), bf16[4,2,2,128,384]{4,3,2,1,0:T(8,128)(2,1)S(1)}, u32[]{:S(2)}, u32[]{:S(2)}) async-start(bf16[4,2,2,128,384]{4,3,2,1,0:T(8,128)(2,1)} %shard_map.83.refs_0_), calls=%async_computation | async-start | bytes 3145728 | tf_op jit(solution)/shard_map/all_to_all | solution.py:454
  15.3 0.0 copy-done.2
  15.3 0.6 fusion.1
  21.8 0.6 fusion.2
  22.4 1.3 %concatenate.3._.s_ref = s32[9]{0:T(128)S(1)} concatenate(s32[1]{0:T(128)} %bitcast, s32[1]{0:T(128)} %bitcast.1, s32[1]{0:T(128)} %bitcast.2, s32[1]{0:T(128)} %get-tuple-element.178, s32[1]{0:T(128)} %get-tuple-element.177, s32[2]{0:T(128)S(1)} %get-tuple-element.175, s32[1]{0:T(128)} %bitcast.6, s32[1]{0:T(128)} %bitcast.8), dimensions={0} | concatenate | bytes 72 | tf_op jit(solution)/shard_map/concatenate | solution.py:426
  23.7 0.0 copy-start.1
  23.7 0.0 collective-permute-done.43.x_ref.refs_1_
  23.7 1.1 %collective-permute-done.44.y_ref.refs_2_ = bf16[768,512]{1,0:T(8,128)(2,1)} collective-permute-done((bf16[768,512]{1,0:T(8,128)(2,1)S(1)}, bf16[768,512]{1,0:T(8,128)(2,1)}, u32[]{:S(2)}, u32[]{:S(2)}) %collective-permute-start.44) | collective-permute-done | bytes 786464 | tf_op jit(solution)/shard_map/ppermute | solution.py:384
  24.8 2.1 %shard_map.85 = (bf16[384,512]{1,0:T(8,128)(2,1)S(1)}, bf16[384,512]{1,0:T(8,128)(2,1)S(1)}) custom-call(s32[9]{0:T(128)S(1)} %concatenate.3._.s_ref, bf16[768,512]{1,0:T(8,128)(2,1)S(1)} %collective-permute-done.43.x_ref.refs_1_, bf16[768,512]{1,0:T(8,128)(2,1)} %collective-permute-done.44.y_ref.refs_2_, bf16[768,256]{1,0:T(8,128)(2,1)S(1)} %shard_map.84.refs_0_), custom_call_target="tpu_custom_call" | custom-call | tf_op jit(solution)/shard_map/pallas_call | solution.py:24
  27.0 1.6 %collective-permute-start.47 = (bf16[384,512]{1,0:T(8,128)(2,1)S(1)}, bf16[384,512]{1,0:T(8,128)(2,1)S(1)}, u32[]{:S(2)}, u32[]{:S(2)}) collective-permute-start(bf16[384,512]{1,0:T(8,128)(2,1)S(1)} %get-tuple-element.155.refs_3_), channel_id=1, source_target_pairs={{0,16},{8,24},{16,0},{24,8},{1,17},{9,25},{17,1},{25,9},{2,18},{10... | collective-permute-start | bytes 1179656 | tf_op jit(solution)/shard_map/ppermute | solution.py:384
  28.6 0.5 collective-permute-start.48
  29.1 0.0 collective-permute-done.40.other_ref
  29.1 0.0 copy-done.1
  29.1 3.2 %shard_map.86 = (f32[2,256,512]{2,1,0:T(8,128)S(1)}, bf16[2,256,768]{2,1,0:T(8,128)(2,1)S(1)}) custom-call(s32[9]{0:T(128)S(1)} %concatenate.3._.s_ref, bf16[2,128,3072]{2,1,0:T(8,128)(2,1)S(1)} %bitcast.21, bf16[2,128,3072]{2,1,0:T(8,128)(2,1)} %collective-permute-done.40.other_ref, bf16[768,512]{1,0:T(8,128)(2,1)S(1)} %shard_map.82.refs_0_, ...), custom_call_target="tpu_custom_call" | custom-call | flops 24999999488 | tf_op jit(solution)/shard_map/pallas_call | solution.py:24
  32.3 0.0 collective-permute-done.41.x_ref.refs_1_
  32.4 0.9 %collective-permute-done.42.y_ref.refs_2_ = bf16[768,256]{1,0:T(8,128)(2,1)} collective-permute-done((bf16[768,256]{1,0:T(8,128)(2,1)S(1)}, bf16[768,256]{1,0:T(8,128)(2,1)}, u32[]{:S(2)}, u32[]{:S(2)}) %collective-permute-start.42) | collective-permute-done | bytes 393248 | tf_op jit(solution)/shard_map/ppermute | solution.py:384
  33.3 2.1 %shard_map.87 = (bf16[384,256]{1,0:T(8,128)(2,1)S(1)}, bf16[384,256]{1,0:T(8,128)(2,1)S(1)}) custom-call(s32[9]{0:T(128)S(1)} %concatenate.3._.s_ref, bf16[768,256]{1,0:T(8,128)(2,1)} %collective-permute-done.41.x_ref.refs_1_, bf16[768,256]{1,0:T(8,128)(2,1)} %collective-permute-done.42.y_ref.refs_2_, bf16[2,256,768]{2,1,0:T(8,128)(2,1)S(1)} %get-tuple-element.156.refs_0_.far_ref), custom_call_target="tpu_custom_call" | custom-call | tf_op jit(solution)/shard_map/pallas_call | solution.py:24
  35.3 1.6 %collective-permute-start.45 = (bf16[384,256]{1,0:T(8,128)(2,1)S(1)}, bf16[384,256]{1,0:T(8,128)(2,1)S(1)}, u32[]{:S(2)}, u32[]{:S(2)}) collective-permute-start(bf16[384,256]{1,0:T(8,128)(2,1)S(1)} %get-tuple-element.157.refs_3_), channel_id=1, source_target_pairs={{0,16},{8,24},{16,0},{24,8},{1,17},{9,25},{17,1},{25,9},{2,18},{10... | collective-permute-start | bytes 589832 | tf_op jit(solution)/shard_map/ppermute | solution.py:384
  36.9 0.5 collective-permute-start.46
  37.5 2.8 %shard_map.88 = (f32[2,256,256]{2,1,0:T(8,128)S(1)}, bf16[2,256,768]{2,1,0:T(8,128)(2,1)S(1)}) custom-call(s32[9]{0:T(128)S(1)} %concatenate.3._.s_ref, bf16[2,128,3072]{2,1,0:T(8,128)(2,1)S(1)} %bitcast.22, bf16[2,128,3072]{2,1,0:T(8,128)(2,1)} %collective-permute-done.40.other_ref, bf16[768,256]{1,0:T(8,128)(2,1)S(1)} %shard_map.84.refs_0_, ...), custom_call_target="tpu_custom_call" | custom-call | flops 24999999488 | tf_op jit(solution)/shard_map/pallas_call | solution.py:24
  40.3 1.3 %collective-permute-done.47.refs_0_ = bf16[384,512]{1,0:T(8,128)(2,1)S(1)} collective-permute-done((bf16[384,512]{1,0:T(8,128)(2,1)S(1)}, bf16[384,512]{1,0:T(8,128)(2,1)S(1)}, u32[]{:S(2)}, u32[]{:S(2)}) %collective-permute-start.47) | collective-permute-done | bytes 393248 | tf_op jit(solution)/shard_map/ppermute | solution.py:384
  41.6 0.0 collective-permute-done.48.refs_1_
  41.6 1.2 %shard_map.89 = (bf16[256,256]{1,0:T(8,128)(2,1)S(1)}, bf16[256,256]{1,0:T(8,128)(2,1)S(1)}, bf16[256,256]{1,0:T(8,128)(2,1)S(1)}, bf16[256,256]{1,0:T(8,128)(2,1)S(1)}) custom-call(s32[9]{0:T(128)S(1)} %concatenate.3._.s_ref, f32[2,256,512]{2,1,0:T(8,128)S(1)} %get-tuple-element.161.t_ref, bf16[2,256,768]{2,1,0:T(8,128)(2,1)S(1)} %get-tuple-element.156.refs_0_.far_ref, ...), custom_call_target="tpu_custom_call" | custom-call | tf_op jit(solution)/shard_map/pallas_call | solution.py:24
  42.8 2.3 %collective-permute-done.45.refs_0_ = bf16[384,256]{1,0:T(8,128)(2,1)S(1)} collective-permute-done((bf16[384,256]{1,0:T(8,128)(2,1)S(1)}, bf16[384,256]{1,0:T(8,128)(2,1)S(1)}, u32[]{:S(2)}, u32[]{:S(2)}) %collective-permute-start.45) | collective-permute-done | bytes 196640 | tf_op jit(solution)/shard_map/ppermute | solution.py:384
  45.1 0.0 collective-permute-done.46.refs_1_
  45.1 1.8 %shard_map.90 = (bf16[256,384]{1,0:T(8,128)(2,1)S(1)}, bf16[256,384]{1,0:T(8,128)(2,1)}, bf16[256,384]{1,0:T(8,128)(2,1)}, bf16[256,384]{1,0:T(8,128)(2,1)}) custom-call(s32[9]{0:T(128)S(1)} %concatenate.3._.s_ref, f32[2,256,256]{2,1,0:T(8,128)S(1)} %get-tuple-element.158.t_ref, bf16[2,256,768]{2,1,0:T(8,128)(2,1)S(1)} %get-tuple-element.159.refs_2_.far_ref, ...), custom_call_target="tpu_custom_call" | custom-call | tf_op jit(solution)/shard_map/pallas_call | solution.py:24
  46.9 4.9 %all-to-all-done.refs_0_ = bf16[4,2,2,128,384]{4,3,2,1,0:T(8,128)(2,1)S(1)} async-done(((bf16[4,2,2,128,384]{4,3,2,1,0:T(8,128)(2,1)}), bf16[4,2,2,128,384]{4,3,2,1,0:T(8,128)(2,1)S(1)}, u32[]{:S(2)}, u32[]{:S(2)}) %all-to-all-start) | async-done | bytes 1572896 | tf_op jit(solution)/shard_map/all_to_all | solution.py:454
  51.8 0.0 collective-permute-start.49
  52.5 9.5 %conditional.1 = (bf16[256,384]{1,0:T(8,128)(2,1)}, bf16[256,384]{1,0:T(8,128)(2,1)}) conditional(s32[]{:T(128)} %clamp.3, (s32[]{:T(128)}, bf16[256,384]{1,0:T(8,128)(2,1)S(1)}, bf16[256,384]{1,0:T(8,128)(2,1)}, bf16[256,384]{1,0:T(8,128)(2,1)}, bf16[256,384]{1,0:T(8,128)(2,1)}) %tuple.69, ...), branch_computations={%region_0.1_spmd, %region_1.2_spmd, %region_2.3_spmd, %region_3.4_... | conditional | flops 196609 | bytes 4325563 | solution.py:483
  52.5 2.4 %collective-permute-start.18 = (bf16[256,384]{1,0:T(8,128)(2,1)S(1)}, bf16[256,384]{1,0:T(8,128)(2,1)}, u32[]{:S(2)}, u32[]{:S(2)}) collective-permute-start(bf16[256,384]{1,0:T(8,128)(2,1)S(1)} %get-tuple-element.126), channel_id=1, source_target_pairs={{6,0},{7,4},{0,1},{1,5},{14,8},{15,12},{8,9},{9,13},{22,16},{23,20... | collective-permute-start | bytes 589832 | tf_op jit(solution)/shard_map/cond/branch_12_fun/ppermute | solution.py:394
  55.0 2.0 %collective-permute-start.19 = (bf16[256,384]{1,0:T(8,128)(2,1)}, bf16[256,384]{1,0:T(8,128)(2,1)}, u32[]{:S(2)}, u32[]{:S(2)}) collective-permute-start(bf16[256,384]{1,0:T(8,128)(2,1)} %get-tuple-element.127), channel_id=1, source_target_pairs={{6,2},{7,6},{0,3},{1,7},{14,10},{15,14},{8,11},{9,15},{22,18},{23,... | collective-permute-start | bytes 589832 | tf_op jit(solution)/shard_map/cond/branch_12_fun/ppermute | solution.py:394
  56.9 5.1 %collective-permute-done.18 = bf16[256,384]{1,0:T(8,128)(2,1)} collective-permute-done((bf16[256,384]{1,0:T(8,128)(2,1)S(1)}, bf16[256,384]{1,0:T(8,128)(2,1)}, u32[]{:S(2)}, u32[]{:S(2)}) %collective-permute-start.18) | collective-permute-done | bytes 196640 | tf_op jit(solution)/shard_map/cond/branch_12_fun/ppermute | solution.py:394
  62.0 0.0 collective-permute-done.19
  62.0 0.0 collective-permute-done.49.refs_3_
  62.0 0.0 copy-start
  62.0 3.4 %shard_map.92.refs_0_ = bf16[128,384]{1,0:T(8,128)(2,1)S(1)} custom-call(s32[9]{0:T(128)S(1)} %concatenate.3._.s_ref, f32[1]{0:T(128)S(6)} %copy.43.g_ref, bf16[256,384]{1,0:T(8,128)(2,1)} %get-tuple-element.171.refs_0_, bf16[256,384]{1,0:T(8,128)(2,1)} %get-tuple-element.172.refs_1_, bf16[4,2,2,128,384]{4,3,2,1,0:T(8,128)(2,1)S(1)} %shard_map.91.refs_2_, ...), custom_call_target="tpu_custom_call" | custom-call | tf_op jit(solution)/shard_map/pallas_call | solution.py:24
  65.4 3.4 %collective-permute-start.50 = (bf16[128,384]{1,0:T(8,128)(2,1)S(1)}, bf16[128,384]{1,0:T(8,128)(2,1)S(1)}, u32[]{:S(2)}, u32[]{:S(2)}) collective-permute-start(bf16[128,384]{1,0:T(8,128)(2,1)S(1)} %shard_map.92.refs_0_), channel_id=1, source_target_pairs={{0,2},{1,3},{2,0},{3,1},{4,6},{5,7},{6,4},{7,5},{8,10},{9,11},{10,... | collective-permute-start | bytes 294920 | tf_op jit(solution)/shard_map/ppermute | solution.py:388
  68.8 0.0 collective-permute-start.51
  68.9 2.4 %collective-permute-start.52 = (bf16[128,384]{1,0:T(8,128)(2,1)S(1)}, bf16[128,384]{1,0:T(8,128)(2,1)S(1)}, u32[]{:S(2)}, u32[]{:S(2)}) collective-permute-start(bf16[128,384]{1,0:T(8,128)(2,1)S(1)} %shard_map.92.refs_0_), channel_id=1, source_target_pairs={{0,6},{1,7},{2,4},{3,5},{4,2},{5,3},{6,0},{7,1},{8,14},{9,15},{10,... | collective-permute-start | bytes 294920 | tf_op jit(solution)/shard_map/ppermute | solution.py:388
  71.3 0.0 collective-permute-start.53
  71.3 1.2 %collective-permute-done.50.refs_1_ = bf16[128,384]{1,0:T(8,128)(2,1)S(1)} collective-permute-done((bf16[128,384]{1,0:T(8,128)(2,1)S(1)}, bf16[128,384]{1,0:T(8,128)(2,1)S(1)}, u32[]{:S(2)}, u32[]{:S(2)}) %collective-permute-start.50) | collective-permute-done | bytes 98336 | tf_op jit(solution)/shard_map/ppermute | solution.py:388
  72.5 0.0 collective-permute-start.54
  72.5 5.5 %collective-permute-done.51.refs_2_ = bf16[128,384]{1,0:T(8,128)(2,1)S(1)} collective-permute-done((bf16[128,384]{1,0:T(8,128)(2,1)S(1)}, bf16[128,384]{1,0:T(8,128)(2,1)S(1)}, u32[]{:S(2)}, u32[]{:S(2)}) %collective-permute-start.51) | collective-permute-done | bytes 98336 | tf_op jit(solution)/shard_map/ppermute | solution.py:388
  77.9 0.0 collective-permute-start.55
  77.9 0.0 collective-permute-done.52.refs_3_
  78.0 0.5 collective-permute-start.56
  78.5 0.0 collective-permute-done.53.refs_4_
  78.5 0.0 collective-permute-done.54.refs_5_
  78.5 0.8 collective-permute-done.55.refs_6_
  79.2 0.2 collective-permute-done.56.refs_7_
  79.4 0.0 copy-done
  79.4 1.3 %shard_map.93 = bf16[128,1536]{1,0:T(8,128)(2,1)} custom-call(s32[9]{0:T(128)S(1)} %concatenate.3._.s_ref, bf16[128,1536]{1,0:T(8,128)(2,1)S(1)} %bitcast.19, bf16[128,384]{1,0:T(8,128)(2,1)S(1)} %shard_map.92.refs_0_, bf16[128,384]{1,0:T(8,128)(2,1)S(1)} %collective-permute-done.50.refs_1_, bf16[128,384]{1,0:T(8,128)(2,1)S(1)} %collective-permute-done.51.refs_2_, ...), custom_call_target="tpu_custom_call" | custom-call | tf_op jit(solution)/shard_map/pallas_call | solution.py:24
  (2 shorter events, 0.0 us)
Async XLA Ops:
  0.0 29.1 %collective-permute-start.40 = (bf16[2,128,3072]{2,1,0:T(8,128)(2,1)}, bf16[2,128,3072]{2,1,0:T(8,128)(2,1)}, u32[]{:S(2)}, u32[]{:S(2)}) collective-permute-start(bf16[2,128,3072]{2,1,0:T(8,128)(2,1)} %bitcast.20), channel_id=1, source_target_pairs={{0,1},{1,0},{2,3},{3,2},{4,5},{5,4},{6,7},{7,6},{8,9},{9,8},{10,11... | collective-permute-start | bytes 4718600 | tf_op jit(solution)/shard_map/ppermute | solution.py:391
  1.8 21.9 %collective-permute-start.43 = (bf16[768,512]{1,0:T(8,128)(2,1)S(1)}, bf16[768,512]{1,0:T(8,128)(2,1)S(1)}, u32[]{:S(2)}, u32[]{:S(2)}) collective-permute-start(bf16[768,512]{1,0:T(8,128)(2,1)S(1)} %shard_map.82.refs_0_), channel_id=1, source_target_pairs={{0,8},{8,0},{16,24},{24,16},{1,9},{9,1},{17,25},{25,17},{2,10},{10... | collective-permute-start | bytes 2359304 | tf_op jit(solution)/shard_map/ppermute | solution.py:384
  4.4 20.5 %collective-permute-start.44 = (bf16[768,512]{1,0:T(8,128)(2,1)S(1)}, bf16[768,512]{1,0:T(8,128)(2,1)}, u32[]{:S(2)}, u32[]{:S(2)}) collective-permute-start(bf16[768,512]{1,0:T(8,128)(2,1)S(1)} %shard_map.82.refs_0_), channel_id=1, source_target_pairs={{0,16},{8,24},{16,0},{24,8},{1,17},{9,25},{17,1},{25,9},{2,18},{10... | collective-permute-start | bytes 2359304 | tf_op jit(solution)/shard_map/ppermute | solution.py:384
  9.3 6.0 %copy-start.2 = (s32[1,2]{1,0:T(1,128)S(1)}, s32[1,2]{1,0:T(1,128)}, u32[]{:S(2)}) copy-start(s32[1,2]{1,0:T(1,128)} %param.30) | copy-start | bytes 28
  9.3 23.0 %collective-permute-start.41 = (bf16[768,256]{1,0:T(8,128)(2,1)S(1)}, bf16[768,256]{1,0:T(8,128)(2,1)}, u32[]{:S(2)}, u32[]{:S(2)}) collective-permute-start(bf16[768,256]{1,0:T(8,128)(2,1)S(1)} %shard_map.84.refs_0_), channel_id=1, source_target_pairs={{0,8},{8,0},{16,24},{24,16},{1,9},{9,1},{17,25},{25,17},{2,10},{10... | collective-permute-start | bytes 1179656 | tf_op jit(solution)/shard_map/ppermute | solution.py:384
  9.9 23.3 %collective-permute-start.42 = (bf16[768,256]{1,0:T(8,128)(2,1)S(1)}, bf16[768,256]{1,0:T(8,128)(2,1)}, u32[]{:S(2)}, u32[]{:S(2)}) collective-permute-start(bf16[768,256]{1,0:T(8,128)(2,1)S(1)} %shard_map.84.refs_0_), channel_id=1, source_target_pairs={{0,16},{8,24},{16,0},{24,8},{1,17},{9,25},{17,1},{25,9},{2,18},{10... | collective-permute-start | bytes 1179656 | tf_op jit(solution)/shard_map/ppermute | solution.py:384
  10.0 41.8 %all-to-all-start = ((bf16[4,2,2,128,384]{4,3,2,1,0:T(8,128)(2,1)}), bf16[4,2,2,128,384]{4,3,2,1,0:T(8,128)(2,1)S(1)}, u32[]{:S(2)}, u32[]{:S(2)}) async-start(bf16[4,2,2,128,384]{4,3,2,1,0:T(8,128)(2,1)} %shard_map.83.refs_0_), calls=%async_computation | async-start | bytes 3145728 | tf_op jit(solution)/shard_map/all_to_all | solution.py:454
  23.7 5.4 %copy-start.1 = (bf16[2,1,128,3072]{3,2,1,0:T(8,128)(2,1)S(1)}, bf16[2,1,128,3072]{3,2,1,0:T(8,128)(2,1)}, u32[]{:S(2)}) copy-start(bf16[2,1,128,3072]{3,2,1,0:T(8,128)(2,1)} %param.24) | copy-start | bytes 4718596
  27.0 14.6 %collective-permute-start.47 = (bf16[384,512]{1,0:T(8,128)(2,1)S(1)}, bf16[384,512]{1,0:T(8,128)(2,1)S(1)}, u32[]{:S(2)}, u32[]{:S(2)}) collective-permute-start(bf16[384,512]{1,0:T(8,128)(2,1)S(1)} %get-tuple-element.155.refs_3_), channel_id=1, source_target_pairs={{0,16},{8,24},{16,0},{24,8},{1,17},{9,25},{17,1},{25,9},{2,18},{10... | collective-permute-start | bytes 1179656 | tf_op jit(solution)/shard_map/ppermute | solution.py:384
  28.6 13.0 %collective-permute-start.48 = (bf16[384,512]{1,0:T(8,128)(2,1)S(1)}, bf16[384,512]{1,0:T(8,128)(2,1)S(1)}, u32[]{:S(2)}, u32[]{:S(2)}) collective-permute-start(bf16[384,512]{1,0:T(8,128)(2,1)S(1)} %get-tuple-element.162), channel_id=1, source_target_pairs={{0,8},{8,0},{16,24},{24,16},{1,9},{9,1},{17,25},{25,17},{2,10},{10... | collective-permute-start | bytes 1179656 | tf_op jit(solution)/shard_map/ppermute | solution.py:384
  35.3 9.8 %collective-permute-start.45 = (bf16[384,256]{1,0:T(8,128)(2,1)S(1)}, bf16[384,256]{1,0:T(8,128)(2,1)S(1)}, u32[]{:S(2)}, u32[]{:S(2)}) collective-permute-start(bf16[384,256]{1,0:T(8,128)(2,1)S(1)} %get-tuple-element.157.refs_3_), channel_id=1, source_target_pairs={{0,16},{8,24},{16,0},{24,8},{1,17},{9,25},{17,1},{25,9},{2,18},{10... | collective-permute-start | bytes 589832 | tf_op jit(solution)/shard_map/ppermute | solution.py:384
  36.9 8.2 %collective-permute-start.46 = (bf16[384,256]{1,0:T(8,128)(2,1)S(1)}, bf16[384,256]{1,0:T(8,128)(2,1)S(1)}, u32[]{:S(2)}, u32[]{:S(2)}) collective-permute-start(bf16[384,256]{1,0:T(8,128)(2,1)S(1)} %get-tuple-element.160), channel_id=1, source_target_pairs={{0,8},{8,0},{16,24},{24,16},{1,9},{9,1},{17,25},{25,17},{2,10},{10... | collective-permute-start | bytes 589832 | tf_op jit(solution)/shard_map/ppermute | solution.py:384
  51.8 10.2 %collective-permute-start.49 = (bf16[4,2,2,128,384]{4,3,2,1,0:T(8,128)(2,1)S(1)}, bf16[4,2,2,128,384]{4,3,2,1,0:T(8,128)(2,1)S(1)}, u32[]{:S(2)}, u32[]{:S(2)}) collective-permute-start(bf16[4,2,2,128,384]{4,3,2,1,0:T(8,128)(2,1)S(1)} %shard_map.91.refs_2_), channel_id=1, source_target_pairs={{0,1},{1,0},{2,3},{3,2},{4,5},{5,4},{6,7},{7,6},{8,9},{9,8},{10,11... | collective-permute-start | bytes 4718600 | tf_op jit(solution)/shard_map/ppermute | solution.py:391
  52.5 9.5 %collective-permute-start.18 = (bf16[256,384]{1,0:T(8,128)(2,1)S(1)}, bf16[256,384]{1,0:T(8,128)(2,1)}, u32[]{:S(2)}, u32[]{:S(2)}) collective-permute-start(bf16[256,384]{1,0:T(8,128)(2,1)S(1)} %get-tuple-element.126), channel_id=1, source_target_pairs={{6,0},{7,4},{0,1},{1,5},{14,8},{15,12},{8,9},{9,13},{22,16},{23,20... | collective-permute-start | bytes 589832 | tf_op jit(solution)/shard_map/cond/branch_12_fun/ppermute | solution.py:394
  55.0 7.0 %collective-permute-start.19 = (bf16[256,384]{1,0:T(8,128)(2,1)}, bf16[256,384]{1,0:T(8,128)(2,1)}, u32[]{:S(2)}, u32[]{:S(2)}) collective-permute-start(bf16[256,384]{1,0:T(8,128)(2,1)} %get-tuple-element.127), channel_id=1, source_target_pairs={{6,2},{7,6},{0,3},{1,7},{14,10},{15,14},{8,11},{9,15},{22,18},{23,... | collective-permute-start | bytes 589832 | tf_op jit(solution)/shard_map/cond/branch_12_fun/ppermute | solution.py:394
  62.0 17.4 %copy-start = (bf16[1,128,1536]{2,1,0:T(8,128)(2,1)S(1)}, bf16[1,128,1536]{2,1,0:T(8,128)(2,1)}, u32[]{:S(2)}) copy-start(bf16[1,128,1536]{2,1,0:T(8,128)(2,1)} %param.27) | copy-start | bytes 1179652
  65.4 7.0 %collective-permute-start.50 = (bf16[128,384]{1,0:T(8,128)(2,1)S(1)}, bf16[128,384]{1,0:T(8,128)(2,1)S(1)}, u32[]{:S(2)}, u32[]{:S(2)}) collective-permute-start(bf16[128,384]{1,0:T(8,128)(2,1)S(1)} %shard_map.92.refs_0_), channel_id=1, source_target_pairs={{0,2},{1,3},{2,0},{3,1},{4,6},{5,7},{6,4},{7,5},{8,10},{9,11},{10,... | collective-permute-start | bytes 294920 | tf_op jit(solution)/shard_map/ppermute | solution.py:388
  68.8 9.1 %collective-permute-start.51 = (bf16[128,384]{1,0:T(8,128)(2,1)S(1)}, bf16[128,384]{1,0:T(8,128)(2,1)S(1)}, u32[]{:S(2)}, u32[]{:S(2)}) collective-permute-start(bf16[128,384]{1,0:T(8,128)(2,1)S(1)} %shard_map.92.refs_0_), channel_id=1, source_target_pairs={{0,4},{1,5},{2,6},{3,7},{4,0},{5,1},{6,2},{7,3},{8,12},{9,13},{10,... | collective-permute-start | bytes 294920 | tf_op jit(solution)/shard_map/ppermute | solution.py:388
  68.9 9.1 %collective-permute-start.52 = (bf16[128,384]{1,0:T(8,128)(2,1)S(1)}, bf16[128,384]{1,0:T(8,128)(2,1)S(1)}, u32[]{:S(2)}, u32[]{:S(2)}) collective-permute-start(bf16[128,384]{1,0:T(8,128)(2,1)S(1)} %shard_map.92.refs_0_), channel_id=1, source_target_pairs={{0,6},{1,7},{2,4},{3,5},{4,2},{5,3},{6,0},{7,1},{8,14},{9,15},{10,... | collective-permute-start | bytes 294920 | tf_op jit(solution)/shard_map/ppermute | solution.py:388
  71.3 7.2 %collective-permute-start.53 = (bf16[128,384]{1,0:T(8,128)(2,1)S(1)}, bf16[128,384]{1,0:T(8,128)(2,1)S(1)}, u32[]{:S(2)}, u32[]{:S(2)}) collective-permute-start(bf16[128,384]{1,0:T(8,128)(2,1)S(1)} %shard_map.92.refs_0_), channel_id=1, source_target_pairs={{0,1},{1,0},{2,3},{3,2},{4,5},{5,4},{6,7},{7,6},{8,9},{9,8},{10,11... | collective-permute-start | bytes 294920 | tf_op jit(solution)/shard_map/ppermute | solution.py:391
  72.5 6.0 %collective-permute-start.54 = (bf16[128,384]{1,0:T(8,128)(2,1)S(1)}, bf16[128,384]{1,0:T(8,128)(2,1)S(1)}, u32[]{:S(2)}, u32[]{:S(2)}) collective-permute-start(bf16[128,384]{1,0:T(8,128)(2,1)S(1)} %collective-permute-done.50.refs_1_), channel_id=1, source_target_pairs={{0,1},{1,0},{2,3},{3,2},{4,5},{5,4},{6,7},{7,6},{8,9},{9,8},{10,11... | collective-permute-start | bytes 294920 | tf_op jit(solution)/shard_map/ppermute | solution.py:391
  77.9 1.3 %collective-permute-start.55 = (bf16[128,384]{1,0:T(8,128)(2,1)S(1)}, bf16[128,384]{1,0:T(8,128)(2,1)S(1)}, u32[]{:S(2)}, u32[]{:S(2)}) collective-permute-start(bf16[128,384]{1,0:T(8,128)(2,1)S(1)} %collective-permute-done.51.refs_2_), channel_id=1, source_target_pairs={{0,1},{1,0},{2,3},{3,2},{4,5},{5,4},{6,7},{7,6},{8,9},{9,8},{10,11... | collective-permute-start | bytes 294920 | tf_op jit(solution)/shard_map/ppermute | solution.py:391
  78.0 1.5 %collective-permute-start.56 = (bf16[128,384]{1,0:T(8,128)(2,1)S(1)}, bf16[128,384]{1,0:T(8,128)(2,1)S(1)}, u32[]{:S(2)}, u32[]{:S(2)}) collective-permute-start(bf16[128,384]{1,0:T(8,128)(2,1)S(1)} %collective-permute-done.52.refs_3_), channel_id=1, source_target_pairs={{0,1},{1,0},{2,3},{3,2},{4,5},{5,4},{6,7},{7,6},{8,9},{9,8},{10,11... | collective-permute-start | bytes 294920 | tf_op jit(solution)/shard_map/ppermute | solution.py:391

commit v5 on v4

--- a/solution.py
+++ b/solution.py
@@ -67,21 +67,25 @@
     shape = (rows, count * HD)
 
     def kernel(core_ref, w_ref, *refs):
-        out, buf, sem, out_sem = refs[-4:]
-        loads, stores = [], []
-        for n, head in enumerate(heads_of(core_ref[0])):
-            here = slice(n * HD, (n + 1) * HD)
-            at = pl.ds(pl.multiple_of(head * HD, HD), HD)
-            loads.append(pltpu.make_async_copy(w_ref.at[:, at], buf.at[:, here], sem.at[n]))
-            stores.append(pltpu.make_async_copy(buf.at[:, here], out.at[:, here], out_sem.at[n]))
-        run_both(loads, stores)
+        out, sem = refs[-2:]
+        run_all(
+            [
+                pltpu.make_async_copy(
+                    w_ref.at[:, pl.ds(pl.multiple_of(head * HD, HD), HD)],
+                    out.at[:, n * HD : (n + 1) * HD],
+                    sem.at[n],
+                )
+                for n, head in enumerate(heads_of(core_ref[0]))
+            ]
+        )
 
     return call(
         kernel,
         jax.ShapeDtypeStruct(shape, BF),
         [core],
         [stays(w_query), *events],
-        [pltpu.VMEM(shape, BF), pltpu.SemaphoreType.DMA((count,)), pltpu.SemaphoreType.DMA((count,))],
+        [pltpu.SemaphoreType.DMA((count,))],
+        out_spec=VMEM_SPEC,
     )
 
 
@@ -118,46 +122,54 @@
     half = rows // 2
 
     def kernel(_, x_ref, y_ref, *refs):
-        first, last, buf, sem, out_sem = refs[-5:]
-        sources = (x_ref.at[:half], y_ref.at[half:])
-        run_all([pltpu.make_async_copy(ref, buf.at[n], sem.at[n]) for n, ref in enumerate(sources)])
-        run_all([pltpu.make_async_copy(buf.at[n], ref, out_sem.at[n]) for n, ref in enumerate((first, last))])
+        first, last, sem = refs[-3:]
+        run_all(
+            [
+                pltpu.make_async_copy(x_ref.at[:half], first, sem.at[0]),
+                pltpu.make_async_copy(y_ref.at[half:], last, sem.at[1]),
+            ]
+        )
 
     return call(
         kernel,
         [jax.ShapeDtypeStruct((half, width), BF)] * 2,
         [flags],
         [by_x, by_y, *events],
-        [
-            pltpu.VMEM((2, half, width), BF),
-            pltpu.SemaphoreType.DMA((2,)),
-            pltpu.SemaphoreType.DMA((2,)),
-        ],
-    )
-
-
-def begin_project(flags, at, own, other, pieces, far_rows, events=()):
+        [pltpu.SemaphoreType.DMA((2,))],
+        out_spec=VMEM_SPEC,
+    )
+
+
+def begin_project(flags, at, core_at, own, other, w_query, heads_of, pieces, far_rows, events=()):
     branches, rows, depth = own.shape
     chunk, width = pieces[0].shape
-    count = len(pieces)
+    count = 1 + len(pieces)
     both = branches * rows
 
-    def kernel(s_ref, own_ref, other_ref, *refs):
-        w_refs = refs[:count]
-        t_ref, far_ref, h_buf, w_buf, sem = refs[-5:]
+    def kernel(s_ref, own_ref, other_ref, w_ref, *refs):
+        t_ref, far_ref, h_buf, w_buf, sem, w_sem = refs[-6:]
         loads = []
         for n in range(count + 1):
             columns = pl.ds(pl.multiple_of((s_ref[0] ^ n) * chunk, HD), chunk)
             loads.append([])
-            if n < count:
-                loads[n].append(pltpu.make_async_copy(w_refs[n], w_buf.at[n], sem.at[n, 2]))
+            if n == 0:
+                for k, head in enumerate(heads_of(s_ref[core_at])):
+                    columns_of = pl.ds(pl.multiple_of(head * HD, HD), HD)
+                    loads[n].append(
+                        pltpu.make_async_copy(
+                            w_ref.at[:, columns_of], w_buf.at[n, :, k * HD : (k + 1) * HD], w_sem.at[k]
+                        )
+                    )
+                    loads[n][k].start()
+            elif n < count:
+                loads[n].append(pltpu.make_async_copy(refs[n - 1], w_buf.at[n], w_sem.at[width // HD + n]))
                 loads[n][0].start()
             for slot in range(2):
                 for b in range(branches):
                     there = h_buf.at[n, slot] if n < count else far_ref.at[slot]
                     there = there.at[b * rows : (b + 1) * rows]
                     mine, theirs = [
-                        pltpu.make_async_copy(ref.at[b, :, columns], there, sem.at[n, slot])
+                        pltpu.make_async_copy(ref.at[b, :, columns], there, sem.at[n, slot, b])
                         for ref in (own_ref, other_ref)
                     ]
                     loads[n].append(mine)
@@ -186,11 +198,12 @@
         kernel,
         [jax.ShapeDtypeStruct((2, both, width), F32), jax.ShapeDtypeStruct((2, both, far_rows), BF)],
         [flags],
-        [own, other, *pieces, *events],
+        [own, other, stays(w_query), *pieces, *events],
         [
             pltpu.VMEM((count, 2, both, chunk), BF),
             pltpu.VMEM((count, chunk, width), BF),
-            pltpu.SemaphoreType.DMA((count + 1, 3)),
+            pltpu.SemaphoreType.DMA((count + 1, 2, branches)),
+            pltpu.SemaphoreType.DMA((width // HD + count,)),
         ],
         limit=16,
         out_spec=VMEM_SPEC,
@@ -206,8 +219,8 @@
 
     def kernel(s_ref, t_ref, far_ref, *refs):
         w_refs, e_refs, out_refs = refs[:count], refs[count : count + kept], refs[-4:]
-        for n in range(2):
-            slot = s_ref[first_at] if n == 0 else 1
+
+        def make(n, slot):
             total, first = t_ref[slot], 0
             for w_ref in w_refs:
                 size = w_ref.shape[0]
@@ -217,9 +230,16 @@
                 first += size
             total = total.astype(BF)
             for hi in range(2):
-                out_refs[n * 2 + hi][:, before:] = total[:, hi * part : (hi + 1) * part]
-        for e_ref, out in zip(e_refs, out_refs):
-            out[:, :before] = e_ref[...]
+                out = out_refs[n * 2 + hi]
+                out[:, before:] = total[:, hi * part : (hi + 1) * part]
+                if e_refs:
+                    out[:, :before] = e_refs[n * 2 + hi][...]
+
+        make(0, s_ref[first_at])
+
+        @pl.when(s_ref[first_at + 3] == 1)
+        def _():
+            make(1, 1)
 
     return call(
         kernel,
@@ -243,6 +263,7 @@
     step = 32 * 1024 // keys_all
     places = [(b, head) for b in range(2) for head in range(heads // 2 * 2)]
     places += [(b, head) for head in range(heads // 2 * 2, heads) for b in range(2)]
+    assert heads == 3
 
     def kernel(s_ref, g_ref, *refs):
         q_refs, c_refs = refs[:count], refs[count : count + kept]
@@ -256,6 +277,12 @@
                 else:
                     pltpu.make_async_copy(q_refs[r], q_buf, sem).start()
 
+        for b, head in places[2 * (heads // 2 * 2) :]:
+            for c_ref, size, first in zip(c_refs, sizes, firsts):
+                for kind in range(2):
+                    two_buf[kind, first : first + size, b * HD : (b + 1) * HD] = c_ref[
+                        :, kind, b, :, head * HD : (head + 1) * HD
+                    ].reshape(size, HD)
         if q_spec is not VMEM_SPEC:
             pltpu.make_async_copy(q_refs[0], q_buf, sem).wait()
         attended = {}
@@ -273,10 +300,7 @@
             def sides(c_ref, kind, size, first):
                 if b0 == b1:
                     return c_ref[:, kind, b0, :, h0 * HD : (h1 + 1) * HD].reshape(size, 2 * HD)
-                here = slice(first, first + size)
-                two_buf[kind, here, :HD] = c_ref[:, kind, b0, :, h0 * HD : (h0 + 1) * HD].reshape(size, HD)
-                two_buf[kind, here, HD:] = c_ref[:, kind, b1, :, h1 * HD : (h1 + 1) * HD].reshape(size, HD)
-                return two_buf[kind, here]
+                return two_buf[kind, first : first + size]
 
             for c_ref, size, first in zip(c_refs, sizes, firsts):
                 s_buf[turn, :, first : first + size] = lax.dot_general(
@@ -419,10 +443,11 @@
         which = owners[0] * GROUPS + second
         slot_first = (z != owners[0]).astype(jnp.int32)
         choice = z % 2
-        extra = jnp.stack([slot_first, which]).astype(jnp.int32)
+        shared = owners[0] == second
+        extra = jnp.stack([slot_first, which, core, shared]).astype(jnp.int32)
     else:
         choice = 0
-        extra = jnp.zeros((2,), jnp.int32)
+        extra = jnp.stack([0, 0, core, 1]).astype(jnp.int32)
     flags = jnp.concatenate(
         [jnp.stack([image, z, choice, hit[my_slot]]).astype(jnp.int32), other_hits, is_own, extra]
     )
@@ -440,7 +465,16 @@
     def begin(k, *events):
         return [
             begin_project(
-                flags, pairs_from + 2 * at, own_hidden, other_hidden, weights[k], w_query.shape[0], events
+                flags,
+                pairs_from + 2 * at,
+                first_at + 2,
+                own_hidden,
+                other_hidden,
+                w_query,
+                part_heads(k),
+                weights[k][1:],
+                w_query.shape[0],
+                events,
             )
             for at in range(layers)
         ]

time: 81.3 us -> 86.5 us (1.064)
  the two profiles are of different devices: /device:TPU:0 before, /device:TPU:13 now
where the time goes in v5:
time: 86.5 us; the launch traced here: 85.8 us
  starting transfers between devices  30.1 us (35%)
  Pallas kernels  22.6 us (26%)
  waiting for transfers between devices  20.6 us (24%)
  between operations  6.63 us (8%)
  other arithmetic  3.28 us (4%)
  local copies, waits for them, and re-layouts  2.54 us (3%)
    pallas_call x12, Pallas kernels, call(): pl.pallas_call(kernel, out_shape=out_shape, in_specs=[SMEM_SPEC] * len(sc...  22.6 us
    ppermute x3, starting transfers between devices, over_z(): lax.ppermute(x, 'token', [(t, (t // span ^ m) * span + t % span) for t in...  9.08 us
    ppermute x8, waiting for transfers between devices, over_image(): return lax.ppermute(x, 'image', [(i, i ^ m) for i in range(images)])  8.61 us
    ppermute x6, starting transfers between devices, over_core(): return lax.ppermute(x, 'token', [(t, t ^ 1) for t in range(tokens)])  7.09 us
    ppermute x3, waiting for transfers between devices, over_z(): lax.ppermute(x, 'token', [(t, (t // span ^ m) * span + t % span) for t in...  5.34 us
    ppermute x4, waiting for transfers between devices, send(): return lax.ppermute(x, 'token', pairs)  4.98 us
    all_to_all x1, starting transfers between devices, body(): gathered = lax.all_to_all(blocks, 'token', 0, 0, axis_index_groups=z_groups)  4.76 us
    ppermute x8, starting transfers between devices, over_image(): return lax.ppermute(x, 'image', [(i, i ^ m) for i in range(images)])  4.61 us
  transfers between devices with their start and end apart: 22, of which 12 were waited for; matrix products, arithmetic and copies ran while one was open for 7% of the time, Pallas kernels for 21%

profile of v5, /device:TPU:13, one launch (start us, length us, event | category | flops | bytes accessed | tf_op | source)
XLA Modules:
  0.0 85.8 jit_solution(9557159359975200214)
XLA Ops:
  0.0 0.7 collective-permute-start.40
  0.7 1.3 %shard_map.82.refs_0_ = bf16[768,512]{1,0:T(8,128)(2,1)S(1)} custom-call(s32[1]{0:T(128)} %bitcast.9.core_ref, bf16[768,1536]{1,0:T(8,128)(2,1)} %w_ref.7), custom_call_target="tpu_custom_call" | custom-call | tf_op jit(solution)/shard_map/pallas_call | solution.py:24
  2.0 1.3 %collective-permute-start.43 = (bf16[768,512]{1,0:T(8,128)(2,1)S(1)}, bf16[768,512]{1,0:T(8,128)(2,1)S(1)}, u32[]{:S(2)}, u32[]{:S(2)}) collective-permute-start(bf16[768,512]{1,0:T(8,128)(2,1)S(1)} %shard_map.82.refs_0_), channel_id=1, source_target_pairs={{0,8},{8,0},{16,24},{24,16},{1,9},{9,1},{17,25},{25,17},{2,10},{10... | collective-permute-start | bytes 2359304 | tf_op jit(solution)/shard_map/ppermute | solution.py:408
  3.2 0.2 collective-permute-start.44
  3.5 2.3 %shard_map.83.refs_0_ = bf16[4,2,2,128,384]{4,3,2,1,0:T(8,128)(2,1)} custom-call(bf16[2,128,1536]{2,1,0:T(8,128)(2,1)} %bitcast.24, bf16[2,128,1536]{2,1,0:T(8,128)(2,1)} %bitcast.25, bf16[768,512]{1,0:T(8,128)(2,1)S(1)} %shard_map.82.refs_0_), custom_call_target="tpu_custom_call" | custom-call | tf_op jit(solution)/shard_map/pallas_call | solution.py:24
  5.8 1.1 %shard_map.84.refs_0_ = bf16[768,256]{1,0:T(8,128)(2,1)S(1)} custom-call(s32[1]{0:T(128)} %bitcast.9.core_ref, bf16[768,1536]{1,0:T(8,128)(2,1)} %w_ref.7, bf16[4,2,2,128,384]{4,3,2,1,0:T(8,128)(2,1)} %shard_map.83.refs_0_), custom_call_target="tpu_custom_call" | custom-call | tf_op jit(solution)/shard_map/pallas_call | solution.py:24
  6.9 0.0 copy-start.2
  6.9 0.3 collective-permute-start.41
  7.2 1.2 %collective-permute-start.42 = (bf16[768,256]{1,0:T(8,128)(2,1)S(1)}, bf16[768,256]{1,0:T(8,128)(2,1)}, u32[]{:S(2)}, u32[]{:S(2)}) collective-permute-start(bf16[768,256]{1,0:T(8,128)(2,1)S(1)} %shard_map.84.refs_0_), channel_id=1, source_target_pairs={{0,16},{8,24},{16,0},{24,8},{1,17},{9,25},{17,1},{25,9},{2,18},{10... | collective-permute-start | bytes 1179656 | tf_op jit(solution)/shard_map/ppermute | solution.py:408
  8.4 4.8 %all-to-all-start = ((bf16[4,2,2,128,384]{4,3,2,1,0:T(8,128)(2,1)}), bf16[4,2,2,128,384]{4,3,2,1,0:T(8,128)(2,1)S(1)}, u32[]{:S(2)}, u32[]{:S(2)}) async-start(bf16[4,2,2,128,384]{4,3,2,1,0:T(8,128)(2,1)} %shard_map.83.refs_0_), calls=%async_computation | async-start | bytes 3145728 | tf_op jit(solution)/shard_map/all_to_all | solution.py:488
  13.2 0.0 copy-done.2
  13.2 0.6 fusion.1
  19.6 0.6 fusion.2
  20.3 1.3 %concatenate.3._.s_ref = s32[11]{0:T(128)S(1)} concatenate(s32[1]{0:T(128)} %bitcast, s32[1]{0:T(128)} %bitcast.1, s32[1]{0:T(128)} %bitcast.2, s32[1]{0:T(128)} %get-tuple-element.178, s32[1]{0:T(128)} %get-tuple-element.177, s32[2]{0:T(128)S(1)} %get-tuple-element.175, s32[1]{0:T(128)} %bitcast.6, s32[1]{0:T(128)} %bitcast.8, s32[1]{0:T(128)} %bitcast.9.core_ref, s32[1]{0:T(128)} %bitcast.10), dimensions={0} | concatenate | bytes 88 | tf_op jit(solution)/shard_map/concatenate | solution.py:451
  21.6 0.0 collective-permute-done.43.x_ref.refs_0_
  21.6 0.6 collective-permute-done.44.y_ref.refs_1_
  22.2 1.7 %shard_map.85 = (bf16[384,512]{1,0:T(8,128)(2,1)S(1)}, bf16[384,512]{1,0:T(8,128)(2,1)S(1)}) custom-call(s32[11]{0:T(128)S(1)} %concatenate.3._.s_ref, bf16[768,512]{1,0:T(8,128)(2,1)S(1)} %collective-permute-done.43.x_ref.refs_0_, bf16[768,512]{1,0:T(8,128)(2,1)} %collective-permute-done.44.y_ref.refs_1_, bf16[768,256]{1,0:T(8,128)(2,1)S(1)} %shard_map.84.refs_0_), custom_call_target="tpu_custom_call" | custom-call | tf_op jit(solution)/shard_map/pallas_call | solution.py:24
  23.9 0.3 collective-permute-start.47
  24.2 0.6 collective-permute-start.48
  24.9 0.0 collective-permute-done.40.other_ref
  24.9 0.0 copy-done.1
  24.9 3.6 %shard_map.86 = (f32[2,256,512]{2,1,0:T(8,128)S(1)}, bf16[2,256,768]{2,1,0:T(8,128)(2,1)S(1)}) custom-call(s32[11]{0:T(128)S(1)} %concatenate.3._.s_ref, bf16[2,128,3072]{2,1,0:T(8,128)(2,1)S(1)} %bitcast.22, bf16[2,128,3072]{2,1,0:T(8,128)(2,1)} %collective-permute-done.40.other_ref, bf16[768,1536]{1,0:T(8,128)(2,1)} %w_ref.7, ...), custom_call_target="tpu_custom_call" | custom-call | flops 24999999488 | tf_op jit(solution)/shard_map/pallas_call | solution.py:24
  28.5 1.2 %collective-permute-done.41.x_ref.refs_0_ = bf16[768,256]{1,0:T(8,128)(2,1)} collective-permute-done((bf16[768,256]{1,0:T(8,128)(2,1)S(1)}, bf16[768,256]{1,0:T(8,128)(2,1)}, u32[]{:S(2)}, u32[]{:S(2)}) %collective-permute-start.41) | collective-permute-done | bytes 393248 | tf_op jit(solution)/shard_map/ppermute | solution.py:408
  29.7 0.9 %collective-permute-done.42.y_ref.refs_1_ = bf16[768,256]{1,0:T(8,128)(2,1)} collective-permute-done((bf16[768,256]{1,0:T(8,128)(2,1)S(1)}, bf16[768,256]{1,0:T(8,128)(2,1)}, u32[]{:S(2)}, u32[]{:S(2)}) %collective-permute-start.42) | collective-permute-done | bytes 393248 | tf_op jit(solution)/shard_map/ppermute | solution.py:408
  30.6 1.6 %shard_map.87 = (bf16[384,256]{1,0:T(8,128)(2,1)S(1)}, bf16[384,256]{1,0:T(8,128)(2,1)S(1)}) custom-call(s32[11]{0:T(128)S(1)} %concatenate.3._.s_ref, bf16[768,256]{1,0:T(8,128)(2,1)} %collective-permute-done.41.x_ref.refs_0_, bf16[768,256]{1,0:T(8,128)(2,1)} %collective-permute-done.42.y_ref.refs_1_, ...), custom_call_target="tpu_custom_call" | custom-call | tf_op jit(solution)/shard_map/pallas_call | solution.py:24
  32.2 0.3 collective-permute-start.45
  32.5 0.3 collective-permute-start.46
  32.8 3.0 %shard_map.88 = (f32[2,256,256]{2,1,0:T(8,128)S(1)}, bf16[2,256,768]{2,1,0:T(8,128)(2,1)S(1)}) custom-call(s32[11]{0:T(128)S(1)} %concatenate.3._.s_ref, bf16[2,128,3072]{2,1,0:T(8,128)(2,1)S(1)} %bitcast.23, bf16[2,128,3072]{2,1,0:T(8,128)(2,1)} %collective-permute-done.40.other_ref, bf16[768,1536]{1,0:T(8,128)(2,1)} %w_ref.7, ...), custom_call_target="tpu_custom_call" | custom-call | flops 24999999488 | tf_op jit(solution)/shard_map/pallas_call | solution.py:24
  35.8 3.1 %collective-permute-done.47.refs_0_ = bf16[384,512]{1,0:T(8,128)(2,1)S(1)} collective-permute-done((bf16[384,512]{1,0:T(8,128)(2,1)S(1)}, bf16[384,512]{1,0:T(8,128)(2,1)S(1)}, u32[]{:S(2)}, u32[]{:S(2)}) %collective-permute-start.47) | collective-permute-done | bytes 393248 | tf_op jit(solution)/shard_map/ppermute | solution.py:408
  38.9 0.0 collective-permute-done.48.refs_1_
  38.9 1.4 %shard_map.89 = (bf16[256,256]{1,0:T(8,128)(2,1)S(1)}, bf16[256,256]{1,0:T(8,128)(2,1)S(1)}, bf16[256,256]{1,0:T(8,128)(2,1)S(1)}, bf16[256,256]{1,0:T(8,128)(2,1)S(1)}) custom-call(s32[11]{0:T(128)S(1)} %concatenate.3._.s_ref, f32[2,256,512]{2,1,0:T(8,128)S(1)} %get-tuple-element.161.t_ref, bf16[2,256,768]{2,1,0:T(8,128)(2,1)S(1)} %get-tuple-element.156.refs_0_.far_ref, ...), custom_call_target="tpu_custom_call" | custom-call | tf_op jit(solution)/shard_map/pallas_call | solution.py:24
  40.3 2.8 %collective-permute-done.45.refs_0_ = bf16[384,256]{1,0:T(8,128)(2,1)S(1)} collective-permute-done((bf16[384,256]{1,0:T(8,128)(2,1)S(1)}, bf16[384,256]{1,0:T(8,128)(2,1)S(1)}, u32[]{:S(2)}, u32[]{:S(2)}) %collective-permute-start.45) | collective-permute-done | bytes 196640 | tf_op jit(solution)/shard_map/ppermute | solution.py:408
  43.2 0.0 collective-permute-done.46.refs_1_
  43.2 1.9 %shard_map.90 = (bf16[256,384]{1,0:T(8,128)(2,1)S(1)}, bf16[256,384]{1,0:T(8,128)(2,1)}, bf16[256,384]{1,0:T(8,128)(2,1)}, bf16[256,384]{1,0:T(8,128)(2,1)}) custom-call(s32[11]{0:T(128)S(1)} %concatenate.3._.s_ref, f32[2,256,256]{2,1,0:T(8,128)S(1)} %get-tuple-element.158.t_ref, bf16[2,256,768]{2,1,0:T(8,128)(2,1)S(1)} %get-tuple-element.159.refs_2_.far_ref, ...), custom_call_target="tpu_custom_call" | custom-call | tf_op jit(solution)/shard_map/pallas_call | solution.py:24
  45.1 0.7 all-to-all-done.refs_0_
  45.8 2.3 %collective-permute-start.49 = (bf16[4,2,2,128,384]{4,3,2,1,0:T(8,128)(2,1)S(1)}, bf16[4,2,2,128,384]{4,3,2,1,0:T(8,128)(2,1)S(1)}, u32[]{:S(2)}, u32[]{:S(2)}) collective-permute-start(bf16[4,2,2,128,384]{4,3,2,1,0:T(8,128)(2,1)S(1)} %shard_map.91.refs_2_), channel_id=1, source_target_pairs={{0,1},{1,0},{2,3},{3,2},{4,5},{5,4},{6,7},{7,6},{8,9},{9,8},{10,11... | collective-permute-start | bytes 4718600 | tf_op jit(solution)/shard_map/ppermute | solution.py:415
  48.8 12.9 %conditional.1 = (bf16[256,384]{1,0:T(8,128)(2,1)}, bf16[256,384]{1,0:T(8,128)(2,1)}) conditional(s32[]{:T(128)} %clamp.3, (s32[]{:T(128)}, bf16[256,384]{1,0:T(8,128)(2,1)S(1)}, bf16[256,384]{1,0:T(8,128)(2,1)}, bf16[256,384]{1,0:T(8,128)(2,1)}, bf16[256,384]{1,0:T(8,128)(2,1)}) %tuple.69, ...), branch_computations={%region_0.1_spmd, %region_1.2_spmd, %region_2.3_spmd, %region_3.4_... | conditional | flops 196609 | bytes 4325563 | solution.py:517
  48.8 1.3 %collective-permute-start.34 = (bf16[256,384]{1,0:T(8,128)(2,1)}, bf16[256,384]{1,0:T(8,128)(2,1)}, u32[]{:S(2)}, u32[]{:S(2)}) collective-permute-start(bf16[256,384]{1,0:T(8,128)(2,1)} %get-tuple-element.122), channel_id=1, source_target_pairs={{4,2},{5,6},{0,3},{1,7},{12,10},{13,14},{8,11},{9,15},{20,18},{21,... | collective-permute-start | bytes 589832 | tf_op jit(solution)/shard_map/cond/branch_10_fun/ppermute | solution.py:418
  50.1 1.3 %collective-permute-start.35 = (bf16[256,384]{1,0:T(8,128)(2,1)}, bf16[256,384]{1,0:T(8,128)(2,1)}, u32[]{:S(2)}, u32[]{:S(2)}) collective-permute-start(bf16[256,384]{1,0:T(8,128)(2,1)} %get-tuple-element.123), channel_id=1, source_target_pairs={{0,2},{1,6},{4,3},{5,7},{8,10},{9,14},{12,11},{13,15},{16,18},{17,... | collective-permute-start | bytes 589832 | tf_op jit(solution)/shard_map/cond/branch_10_fun/ppermute | solution.py:418
  51.4 0.7 collective-permute-start.32
  52.1 1.3 %collective-permute-start.33 = (bf16[256,384]{1,0:T(8,128)(2,1)}, bf16[256,384]{1,0:T(8,128)(2,1)}, u32[]{:S(2)}, u32[]{:S(2)}) collective-permute-start(bf16[256,384]{1,0:T(8,128)(2,1)} %get-tuple-element.121), channel_id=1, source_target_pairs={{0,0},{1,4},{4,1},{5,5},{8,8},{9,12},{12,9},{13,13},{16,16},{17,20... | collective-permute-start | bytes 589832 | tf_op jit(solution)/shard_map/cond/branch_10_fun/ppermute | solution.py:418
  53.4 3.6 %collective-permute-done.34 = bf16[256,384]{1,0:T(8,128)(2,1)} collective-permute-done((bf16[256,384]{1,0:T(8,128)(2,1)}, bf16[256,384]{1,0:T(8,128)(2,1)}, u32[]{:S(2)}, u32[]{:S(2)}) %collective-permute-start.34) | collective-permute-done | bytes 196640 | tf_op jit(solution)/shard_map/cond/branch_10_fun/ppermute | solution.py:418
  57.1 1.3 %collective-permute-done.35 = bf16[256,384]{1,0:T(8,128)(2,1)} collective-permute-done((bf16[256,384]{1,0:T(8,128)(2,1)}, bf16[256,384]{1,0:T(8,128)(2,1)}, u32[]{:S(2)}, u32[]{:S(2)}) %collective-permute-start.35) | collective-permute-done | bytes 196640 | tf_op jit(solution)/shard_map/cond/branch_10_fun/ppermute | solution.py:418
  58.4 1.6 %broadcast_select_fusion.4 = bf16[256,384]{1,0:T(8,128)(2,1)} fusion(bf16[256,384]{1,0:T(8,128)(2,1)} %collective-permute-done.34, bf16[256,384]{1,0:T(8,128)(2,1)} %collective-permute-done.35, pred[]{:T(512)S(6)} %eq.30), kind=kLoop, calls=%fused_computation.4 | loop fusion | flops 98304 | bytes 589825 | tf_op jit(solution)/shard_map/cond/branch_10_fun/jit(_where)/select_n | solution.py:512
  60.0 0.0 collective-permute-done.32
  60.0 0.0 collective-permute-done.33
  60.0 1.6 %broadcast_select_fusion.5 = bf16[256,384]{1,0:T(8,128)(2,1)} fusion(bf16[256,384]{1,0:T(8,128)(2,1)S(1)} %collective-permute-done.32, bf16[256,384]{1,0:T(8,128)(2,1)} %collective-permute-done.33, pred[]{:T(512)S(6)} %eq.30), kind=kLoop, calls=%fused_computation.5 | loop fusion | flops 98304 | bytes 589825 | tf_op jit(solution)/shard_map/cond/branch_10_fun/jit(_where)/select_n | solution.py:512
  61.7 0.0 collective-permute-done.49.refs_3_
  61.7 3.3 %shard_map.92.refs_0_ = bf16[128,384]{1,0:T(8,128)(2,1)S(1)} custom-call(s32[11]{0:T(128)S(1)} %concatenate.3._.s_ref, f32[1]{0:T(128)S(6)} %copy.43.g_ref, bf16[256,384]{1,0:T(8,128)(2,1)} %get-tuple-element.171.refs_0_, bf16[256,384]{1,0:T(8,128)(2,1)} %get-tuple-element.172.refs_1_, bf16[4,2,2,128,384]{4,3,2,1,0:T(8,128)(2,1)S(1)} %shard_map.91.refs_2_, ...), custom_call_target="tpu_custom_call" | custom-call | tf_op jit(solution)/shard_map/pallas_call | solution.py:24
  65.0 7.8 %collective-permute-start.50 = (bf16[128,384]{1,0:T(8,128)(2,1)S(1)}, bf16[128,384]{1,0:T(8,128)(2,1)S(1)}, u32[]{:S(2)}, u32[]{:S(2)}) collective-permute-start(bf16[128,384]{1,0:T(8,128)(2,1)S(1)} %shard_map.92.refs_0_), channel_id=1, source_target_pairs={{0,2},{1,3},{2,0},{3,1},{4,6},{5,7},{6,4},{7,5},{8,10},{9,11},{10,... | collective-permute-start | bytes 294920 | tf_op jit(solution)/shard_map/ppermute | solution.py:412
  72.8 0.0 collective-permute-start.51
  72.8 1.3 %collective-permute-start.52 = (bf16[128,384]{1,0:T(8,128)(2,1)S(1)}, bf16[128,384]{1,0:T(8,128)(2,1)S(1)}, u32[]{:S(2)}, u32[]{:S(2)}) collective-permute-start(bf16[128,384]{1,0:T(8,128)(2,1)S(1)} %shard_map.92.refs_0_), channel_id=1, source_target_pairs={{0,6},{1,7},{2,4},{3,5},{4,2},{5,3},{6,0},{7,1},{8,14},{9,15},{10,... | collective-permute-start | bytes 294920 | tf_op jit(solution)/shard_map/ppermute | solution.py:412
  74.1 0.8 collective-permute-start.53
  74.9 1.6 %collective-permute-done.50.refs_1_ = bf16[128,384]{1,0:T(8,128)(2,1)S(1)} collective-permute-done((bf16[128,384]{1,0:T(8,128)(2,1)S(1)}, bf16[128,384]{1,0:T(8,128)(2,1)S(1)}, u32[]{:S(2)}, u32[]{:S(2)}) %collective-permute-start.50) | collective-permute-done | bytes 98336 | tf_op jit(solution)/shard_map/ppermute | solution.py:412
  76.5 0.0 collective-permute-start.54
  76.5 2.0 %collective-permute-done.51.refs_2_ = bf16[128,384]{1,0:T(8,128)(2,1)S(1)} collective-permute-done((bf16[128,384]{1,0:T(8,128)(2,1)S(1)}, bf16[128,384]{1,0:T(8,128)(2,1)S(1)}, u32[]{:S(2)}, u32[]{:S(2)}) %collective-permute-start.51) | collective-permute-done | bytes 98336 | tf_op jit(solution)/shard_map/ppermute | solution.py:412
  78.5 2.5 %collective-permute-start.55 = (bf16[128,384]{1,0:T(8,128)(2,1)S(1)}, bf16[128,384]{1,0:T(8,128)(2,1)S(1)}, u32[]{:S(2)}, u32[]{:S(2)}) collective-permute-start(bf16[128,384]{1,0:T(8,128)(2,1)S(1)} %collective-permute-done.51.refs_2_), channel_id=1, source_target_pairs={{0,1},{1,0},{2,3},{3,2},{4,5},{5,4},{6,7},{7,6},{8,9},{9,8},{10,11... | collective-permute-start | bytes 294920 | tf_op jit(solution)/shard_map/ppermute | solution.py:415
  81.0 1.8 %collective-permute-done.52.refs_3_ = bf16[128,384]{1,0:T(8,128)(2,1)S(1)} collective-permute-done((bf16[128,384]{1,0:T(8,128)(2,1)S(1)}, bf16[128,384]{1,0:T(8,128)(2,1)S(1)}, u32[]{:S(2)}, u32[]{:S(2)}) %collective-permute-start.52) | collective-permute-done | bytes 98336 | tf_op jit(solution)/shard_map/ppermute | solution.py:412
  82.8 0.8 collective-permute-start.56
  83.5 0.0 collective-permute-done.53.refs_4_
  83.5 0.0 collective-permute-done.54.refs_5_
  83.5 0.0 collective-permute-done.55.refs_6_
  83.5 0.9 %collective-permute-done.56.refs_7_ = bf16[128,384]{1,0:T(8,128)(2,1)S(1)} collective-permute-done((bf16[128,384]{1,0:T(8,128)(2,1)S(1)}, bf16[128,384]{1,0:T(8,128)(2,1)S(1)}, u32[]{:S(2)}, u32[]{:S(2)}) %collective-permute-start.56) | collective-permute-done | bytes 98336 | tf_op jit(solution)/shard_map/ppermute | solution.py:415
  84.5 1.3 %shard_map.93 = bf16[128,1536]{1,0:T(8,128)(2,1)} custom-call(s32[11]{0:T(128)S(1)} %concatenate.3._.s_ref, bf16[128,1536]{1,0:T(8,128)(2,1)S(1)} %bitcast.20, bf16[128,384]{1,0:T(8,128)(2,1)S(1)} %shard_map.92.refs_0_, bf16[128,384]{1,0:T(8,128)(2,1)S(1)} %collective-permute-done.50.refs_1_, bf16[128,384]{1,0:T(8,128)(2,1)S(1)} %collective-permute-done.51.refs_2_, ...), custom_call_target="tpu_custom_call" | custom-call | tf_op jit(solution)/shard_map/pallas_call | solution.py:24
  (5 shorter events, 0.0 us)
Async XLA Ops:
  0.0 24.9 %collective-permute-start.40 = (bf16[2,128,3072]{2,1,0:T(8,128)(2,1)}, bf16[2,128,3072]{2,1,0:T(8,128)(2,1)}, u32[]{:S(2)}, u32[]{:S(2)}) collective-permute-start(bf16[2,128,3072]{2,1,0:T(8,128)(2,1)} %bitcast.21), channel_id=1, source_target_pairs={{0,1},{1,0},{2,3},{3,2},{4,5},{5,4},{6,7},{7,6},{8,9},{9,8},{10,11... | collective-permute-start | bytes 4718600 | tf_op jit(solution)/shard_map/ppermute | solution.py:415
  2.0 19.6 %collective-permute-start.43 = (bf16[768,512]{1,0:T(8,128)(2,1)S(1)}, bf16[768,512]{1,0:T(8,128)(2,1)S(1)}, u32[]{:S(2)}, u32[]{:S(2)}) collective-permute-start(bf16[768,512]{1,0:T(8,128)(2,1)S(1)} %shard_map.82.refs_0_), channel_id=1, source_target_pairs={{0,8},{8,0},{16,24},{24,16},{1,9},{9,1},{17,25},{25,17},{2,10},{10... | collective-permute-start | bytes 2359304 | tf_op jit(solution)/shard_map/ppermute | solution.py:408
  3.2 19.0 %collective-permute-start.44 = (bf16[768,512]{1,0:T(8,128)(2,1)S(1)}, bf16[768,512]{1,0:T(8,128)(2,1)}, u32[]{:S(2)}, u32[]{:S(2)}) collective-permute-start(bf16[768,512]{1,0:T(8,128)(2,1)S(1)} %shard_map.82.refs_0_), channel_id=1, source_target_pairs={{0,16},{8,24},{16,0},{24,8},{1,17},{9,25},{17,1},{25,9},{2,18},{10... | collective-permute-start | bytes 2359304 | tf_op jit(solution)/shard_map/ppermute | solution.py:408
  6.9 6.3 %copy-start.2 = (s32[1,2]{1,0:T(1,128)S(1)}, s32[1,2]{1,0:T(1,128)}, u32[]{:S(2)}) copy-start(s32[1,2]{1,0:T(1,128)} %param.30) | copy-start | bytes 28
  6.9 22.9 %collective-permute-start.41 = (bf16[768,256]{1,0:T(8,128)(2,1)S(1)}, bf16[768,256]{1,0:T(8,128)(2,1)}, u32[]{:S(2)}, u32[]{:S(2)}) collective-permute-start(bf16[768,256]{1,0:T(8,128)(2,1)S(1)} %shard_map.84.refs_0_), channel_id=1, source_target_pairs={{0,8},{8,0},{16,24},{24,16},{1,9},{9,1},{17,25},{25,17},{2,10},{10... | collective-permute-start | bytes 1179656 | tf_op jit(solution)/shard_map/ppermute | solution.py:408
  7.2 23.4 %collective-permute-start.42 = (bf16[768,256]{1,0:T(8,128)(2,1)S(1)}, bf16[768,256]{1,0:T(8,128)(2,1)}, u32[]{:S(2)}, u32[]{:S(2)}) collective-permute-start(bf16[768,256]{1,0:T(8,128)(2,1)S(1)} %shard_map.84.refs_0_), channel_id=1, source_target_pairs={{0,16},{8,24},{16,0},{24,8},{1,17},{9,25},{17,1},{25,9},{2,18},{10... | collective-permute-start | bytes 1179656 | tf_op jit(solution)/shard_map/ppermute | solution.py:408
  8.4 37.4 %all-to-all-start = ((bf16[4,2,2,128,384]{4,3,2,1,0:T(8,128)(2,1)}), bf16[4,2,2,128,384]{4,3,2,1,0:T(8,128)(2,1)S(1)}, u32[]{:S(2)}, u32[]{:S(2)}) async-start(bf16[4,2,2,128,384]{4,3,2,1,0:T(8,128)(2,1)} %shard_map.83.refs_0_), calls=%async_computation | async-start | bytes 3145728 | tf_op jit(solution)/shard_map/all_to_all | solution.py:488
  21.6 3.3 %copy-start.1 = (bf16[2,1,128,3072]{3,2,1,0:T(8,128)(2,1)S(1)}, bf16[2,1,128,3072]{3,2,1,0:T(8,128)(2,1)}, u32[]{:S(2)}) copy-start(bf16[2,1,128,3072]{3,2,1,0:T(8,128)(2,1)} %param.24) | copy-start | bytes 4718596
  23.9 15.0 %collective-permute-start.47 = (bf16[384,512]{1,0:T(8,128)(2,1)S(1)}, bf16[384,512]{1,0:T(8,128)(2,1)S(1)}, u32[]{:S(2)}, u32[]{:S(2)}) collective-permute-start(bf16[384,512]{1,0:T(8,128)(2,1)S(1)} %get-tuple-element.155.refs_2_), channel_id=1, source_target_pairs={{0,16},{8,24},{16,0},{24,8},{1,17},{9,25},{17,1},{25,9},{2,18},{10... | collective-permute-start | bytes 1179656 | tf_op jit(solution)/shard_map/ppermute | solution.py:408
  24.2 14.7 %collective-permute-start.48 = (bf16[384,512]{1,0:T(8,128)(2,1)S(1)}, bf16[384,512]{1,0:T(8,128)(2,1)S(1)}, u32[]{:S(2)}, u32[]{:S(2)}) collective-permute-start(bf16[384,512]{1,0:T(8,128)(2,1)S(1)} %get-tuple-element.162), channel_id=1, source_target_pairs={{0,8},{8,0},{16,24},{24,16},{1,9},{9,1},{17,25},{25,17},{2,10},{10... | collective-permute-start | bytes 1179656 | tf_op jit(solution)/shard_map/ppermute | solution.py:408
  32.2 10.9 %collective-permute-start.45 = (bf16[384,256]{1,0:T(8,128)(2,1)S(1)}, bf16[384,256]{1,0:T(8,128)(2,1)S(1)}, u32[]{:S(2)}, u32[]{:S(2)}) collective-permute-start(bf16[384,256]{1,0:T(8,128)(2,1)S(1)} %get-tuple-element.157.refs_2_), channel_id=1, source_target_pairs={{0,16},{8,24},{16,0},{24,8},{1,17},{9,25},{17,1},{25,9},{2,18},{10... | collective-permute-start | bytes 589832 | tf_op jit(solution)/shard_map/ppermute | solution.py:408
  32.5 10.7 %collective-permute-start.46 = (bf16[384,256]{1,0:T(8,128)(2,1)S(1)}, bf16[384,256]{1,0:T(8,128)(2,1)S(1)}, u32[]{:S(2)}, u32[]{:S(2)}) collective-permute-start(bf16[384,256]{1,0:T(8,128)(2,1)S(1)} %get-tuple-element.160), channel_id=1, source_target_pairs={{0,8},{8,0},{16,24},{24,16},{1,9},{9,1},{17,25},{25,17},{2,10},{10... | collective-permute-start | bytes 589832 | tf_op jit(solution)/shard_map/ppermute | solution.py:408
  45.8 15.9 %collective-permute-start.49 = (bf16[4,2,2,128,384]{4,3,2,1,0:T(8,128)(2,1)S(1)}, bf16[4,2,2,128,384]{4,3,2,1,0:T(8,128)(2,1)S(1)}, u32[]{:S(2)}, u32[]{:S(2)}) collective-permute-start(bf16[4,2,2,128,384]{4,3,2,1,0:T(8,128)(2,1)S(1)} %shard_map.91.refs_2_), channel_id=1, source_target_pairs={{0,1},{1,0},{2,3},{3,2},{4,5},{5,4},{6,7},{7,6},{8,9},{9,8},{10,11... | collective-permute-start | bytes 4718600 | tf_op jit(solution)/shard_map/ppermute | solution.py:415
  48.8 8.3 %collective-permute-start.34 = (bf16[256,384]{1,0:T(8,128)(2,1)}, bf16[256,384]{1,0:T(8,128)(2,1)}, u32[]{:S(2)}, u32[]{:S(2)}) collective-permute-start(bf16[256,384]{1,0:T(8,128)(2,1)} %get-tuple-element.122), channel_id=1, source_target_pairs={{4,2},{5,6},{0,3},{1,7},{12,10},{13,14},{8,11},{9,15},{20,18},{21,... | collective-permute-start | bytes 589832 | tf_op jit(solution)/shard_map/cond/branch_10_fun/ppermute | solution.py:418
  50.1 8.3 %collective-permute-start.35 = (bf16[256,384]{1,0:T(8,128)(2,1)}, bf16[256,384]{1,0:T(8,128)(2,1)}, u32[]{:S(2)}, u32[]{:S(2)}) collective-permute-start(bf16[256,384]{1,0:T(8,128)(2,1)} %get-tuple-element.123), channel_id=1, source_target_pairs={{0,2},{1,6},{4,3},{5,7},{8,10},{9,14},{12,11},{13,15},{16,18},{17,... | collective-permute-start | bytes 589832 | tf_op jit(solution)/shard_map/cond/branch_10_fun/ppermute | solution.py:418
  51.4 8.6 %collective-permute-start.32 = (bf16[256,384]{1,0:T(8,128)(2,1)S(1)}, bf16[256,384]{1,0:T(8,128)(2,1)S(1)}, u32[]{:S(2)}, u32[]{:S(2)}) collective-permute-start(bf16[256,384]{1,0:T(8,128)(2,1)S(1)} %get-tuple-element.120), channel_id=1, source_target_pairs={{4,0},{5,4},{0,1},{1,5},{12,8},{13,12},{8,9},{9,13},{20,16},{21,20... | collective-permute-start | bytes 589832 | tf_op jit(solution)/shard_map/cond/branch_10_fun/ppermute | solution.py:418
  52.1 8.0 %collective-permute-start.33 = (bf16[256,384]{1,0:T(8,128)(2,1)}, bf16[256,384]{1,0:T(8,128)(2,1)}, u32[]{:S(2)}, u32[]{:S(2)}) collective-permute-start(bf16[256,384]{1,0:T(8,128)(2,1)} %get-tuple-element.121), channel_id=1, source_target_pairs={{0,0},{1,4},{4,1},{5,5},{8,8},{9,12},{12,9},{13,13},{16,16},{17,20... | collective-permute-start | bytes 589832 | tf_op jit(solution)/shard_map/cond/branch_10_fun/ppermute | solution.py:418
  61.7 22.8 %copy-start = (bf16[1,128,1536]{2,1,0:T(8,128)(2,1)S(1)}, bf16[1,128,1536]{2,1,0:T(8,128)(2,1)}, u32[]{:S(2)}) copy-start(bf16[1,128,1536]{2,1,0:T(8,128)(2,1)} %param.27) | copy-start | bytes 1179652
  65.0 11.5 %collective-permute-start.50 = (bf16[128,384]{1,0:T(8,128)(2,1)S(1)}, bf16[128,384]{1,0:T(8,128)(2,1)S(1)}, u32[]{:S(2)}, u32[]{:S(2)}) collective-permute-start(bf16[128,384]{1,0:T(8,128)(2,1)S(1)} %shard_map.92.refs_0_), channel_id=1, source_target_pairs={{0,2},{1,3},{2,0},{3,1},{4,6},{5,7},{6,4},{7,5},{8,10},{9,11},{10,... | collective-permute-start | bytes 294920 | tf_op jit(solution)/shard_map/ppermute | solution.py:412
  72.8 5.6 %collective-permute-start.51 = (bf16[128,384]{1,0:T(8,128)(2,1)S(1)}, bf16[128,384]{1,0:T(8,128)(2,1)S(1)}, u32[]{:S(2)}, u32[]{:S(2)}) collective-permute-start(bf16[128,384]{1,0:T(8,128)(2,1)S(1)} %shard_map.92.refs_0_), channel_id=1, source_target_pairs={{0,4},{1,5},{2,6},{3,7},{4,0},{5,1},{6,2},{7,3},{8,12},{9,13},{10,... | collective-permute-start | bytes 294920 | tf_op jit(solution)/shard_map/ppermute | solution.py:412
  72.8 9.9 %collective-permute-start.52 = (bf16[128,384]{1,0:T(8,128)(2,1)S(1)}, bf16[128,384]{1,0:T(8,128)(2,1)S(1)}, u32[]{:S(2)}, u32[]{:S(2)}) collective-permute-start(bf16[128,384]{1,0:T(8,128)(2,1)S(1)} %shard_map.92.refs_0_), channel_id=1, source_target_pairs={{0,6},{1,7},{2,4},{3,5},{4,2},{5,3},{6,0},{7,1},{8,14},{9,15},{10,... | collective-permute-start | bytes 294920 | tf_op jit(solution)/shard_map/ppermute | solution.py:412
  74.1 9.4 %collective-permute-start.53 = (bf16[128,384]{1,0:T(8,128)(2,1)S(1)}, bf16[128,384]{1,0:T(8,128)(2,1)S(1)}, u32[]{:S(2)}, u32[]{:S(2)}) collective-permute-start(bf16[128,384]{1,0:T(8,128)(2,1)S(1)} %shard_map.92.refs_0_), channel_id=1, source_target_pairs={{0,1},{1,0},{2,3},{3,2},{4,5},{5,4},{6,7},{7,6},{8,9},{9,8},{10,11... | collective-permute-start | bytes 294920 | tf_op jit(solution)/shard_map/ppermute | solution.py:415
  76.5 7.0 %collective-permute-start.54 = (bf16[128,384]{1,0:T(8,128)(2,1)S(1)}, bf16[128,384]{1,0:T(8,128)(2,1)S(1)}, u32[]{:S(2)}, u32[]{:S(2)}) collective-permute-start(bf16[128,384]{1,0:T(8,128)(2,1)S(1)} %collective-permute-done.50.refs_1_), channel_id=1, source_target_pairs={{0,1},{1,0},{2,3},{3,2},{4,5},{5,4},{6,7},{7,6},{8,9},{9,8},{10,11... | collective-permute-start | bytes 294920 | tf_op jit(solution)/shard_map/ppermute | solution.py:415
  78.5 5.1 %collective-permute-start.55 = (bf16[128,384]{1,0:T(8,128)(2,1)S(1)}, bf16[128,384]{1,0:T(8,128)(2,1)S(1)}, u32[]{:S(2)}, u32[]{:S(2)}) collective-permute-start(bf16[128,384]{1,0:T(8,128)(2,1)S(1)} %collective-permute-done.51.refs_2_), channel_id=1, source_target_pairs={{0,1},{1,0},{2,3},{3,2},{4,5},{5,4},{6,7},{7,6},{8,9},{9,8},{10,11... | collective-permute-start | bytes 294920 | tf_op jit(solution)/shard_map/ppermute | solution.py:415
  82.8 1.7 %collective-permute-start.56 = (bf16[128,384]{1,0:T(8,128)(2,1)S(1)}, bf16[128,384]{1,0:T(8,128)(2,1)S(1)}, u32[]{:S(2)}, u32[]{:S(2)}) collective-permute-start(bf16[128,384]{1,0:T(8,128)(2,1)S(1)} %collective-permute-done.52.refs_3_), channel_id=1, source_target_pairs={{0,1},{1,0},{2,3},{3,2},{4,5},{5,4},{6,7},{7,6},{8,9},{9,8},{10,11... | collective-permute-start | bytes 294920 | tf_op jit(solution)/shard_map/ppermute | solution.py:415

commit v6 on v5

--- a/solution.py
+++ b/solution.py
@@ -117,11 +117,11 @@
     )
 
 
-def halves(flags, by_x, by_y, events=()):
+def halves(flags, guide, by_x, by_y, events=()):
     rows, width = by_x.shape
     half = rows // 2
 
-    def kernel(_, x_ref, y_ref, *refs):
+    def kernel(_, __, x_ref, y_ref, *refs):
         first, last, sem = refs[-3:]
         run_all(
             [
@@ -133,7 +133,7 @@
     return call(
         kernel,
         [jax.ShapeDtypeStruct((half, width), BF)] * 2,
-        [flags],
+        [flags, guide],
         [by_x, by_y, *events],
         [pltpu.SemaphoreType.DMA((2,))],
         out_spec=VMEM_SPEC,
@@ -459,7 +459,7 @@
         return [own, over_image(own, 1), over_image(own, 2)]
 
     def far(k, *events):
-        first, last = halves(flags, weights[k][1], weights[k][2], events)
+        first, last = halves(flags, guide, weights[k][1], weights[k][2], events)
         return [over_image(first, 2), over_image(last, 1)], first
 
     def begin(k, *events):

time: 86.5 us -> 82.1 us (0.949)
  the two profiles are of different devices: /device:TPU:13 before, /device:TPU:0 now
where the time goes in v6:
time: 82.1 us; the launch traced here: 80.7 us
  starting transfers between devices  28.8 us (35%)
  Pallas kernels  21.7 us (26%)
  waiting for transfers between devices  21 us (26%)
  between operations  6.64 us (8%)
  local copies, waits for them, and re-layouts  2.54 us (3%)
    pallas_call x12, Pallas kernels, call(): pl.pallas_call(kernel, out_shape=out_shape, in_specs=[SMEM_SPEC] * len(sc...  21.7 us
    ppermute x8, starting transfers between devices, over_image(): return lax.ppermute(x, 'image', [(i, i ^ m) for i in range(images)])  9.43 us
    ppermute x3, starting transfers between devices, over_z(): lax.ppermute(x, 'token', [(t, (t // span ^ m) * span + t % span) for t in...  9.23 us
    ppermute x3, waiting for transfers between devices, over_z(): lax.ppermute(x, 'token', [(t, (t // span ^ m) * span + t % span) for t in...  6.03 us
    all_to_all x1, starting transfers between devices, body(): gathered = lax.all_to_all(blocks, 'token', 0, 0, axis_index_groups=z_groups)  5.33 us
    ppermute x8, waiting for transfers between devices, over_image(): return lax.ppermute(x, 'image', [(i, i ^ m) for i in range(images)])  5.22 us
    all_to_all x1, waiting for transfers between devices, body(): gathered = lax.all_to_all(blocks, 'token', 0, 0, axis_index_groups=z_groups)  5.03 us
    ppermute x2, waiting for transfers between devices, send(): return lax.ppermute(x, 'token', pairs)  3.82 us
  transfers between devices with their start and end apart: 20, of which 9 were waited for; matrix products, arithmetic and copies ran while one was open for 3% of the time, Pallas kernels for 21%

profile of v6, /device:TPU:0, one launch (start us, length us, event | category | flops | bytes accessed | tf_op | source)
XLA Modules:
  0.0 80.7 jit_solution(11541940352691187306)
XLA Ops:
  0.0 0.5 collective-permute-start.40
  0.5 1.3 %shard_map.82.refs_0_ = bf16[768,512]{1,0:T(8,128)(2,1)S(1)} custom-call(s32[1]{0:T(128)} %bitcast.9.core_ref, bf16[768,1536]{1,0:T(8,128)(2,1)} %w_ref.7), custom_call_target="tpu_custom_call" | custom-call | tf_op jit(solution)/shard_map/pallas_call | solution.py:24
  1.7 2.6 %collective-permute-start.43 = (bf16[768,512]{1,0:T(8,128)(2,1)S(1)}, bf16[768,512]{1,0:T(8,128)(2,1)S(1)}, u32[]{:S(2)}, u32[]{:S(2)}) collective-permute-start(bf16[768,512]{1,0:T(8,128)(2,1)S(1)} %shard_map.82.refs_0_), channel_id=1, source_target_pairs={{0,8},{8,0},{16,24},{24,16},{1,9},{9,1},{17,25},{25,17},{2,10},{10... | collective-permute-start | bytes 2359304 | tf_op jit(solution)/shard_map/ppermute | solution.py:408
  4.3 1.5 %collective-permute-start.44 = (bf16[768,512]{1,0:T(8,128)(2,1)S(1)}, bf16[768,512]{1,0:T(8,128)(2,1)}, u32[]{:S(2)}, u32[]{:S(2)}) collective-permute-start(bf16[768,512]{1,0:T(8,128)(2,1)S(1)} %shard_map.82.refs_0_), channel_id=1, source_target_pairs={{0,16},{8,24},{16,0},{24,8},{1,17},{9,25},{17,1},{25,9},{2,18},{10... | collective-permute-start | bytes 2359304 | tf_op jit(solution)/shard_map/ppermute | solution.py:408
  5.8 2.3 %shard_map.83.refs_0_ = bf16[4,2,2,128,384]{4,3,2,1,0:T(8,128)(2,1)} custom-call(bf16[2,128,1536]{2,1,0:T(8,128)(2,1)} %bitcast.24, bf16[2,128,1536]{2,1,0:T(8,128)(2,1)} %bitcast.25, bf16[768,512]{1,0:T(8,128)(2,1)S(1)} %shard_map.82.refs_0_), custom_call_target="tpu_custom_call" | custom-call | tf_op jit(solution)/shard_map/pallas_call | solution.py:24
  8.1 1.1 %shard_map.84.refs_0_ = bf16[768,256]{1,0:T(8,128)(2,1)S(1)} custom-call(s32[1]{0:T(128)} %bitcast.9.core_ref, bf16[768,1536]{1,0:T(8,128)(2,1)} %w_ref.7, bf16[4,2,2,128,384]{4,3,2,1,0:T(8,128)(2,1)} %shard_map.83.refs_0_), custom_call_target="tpu_custom_call" | custom-call | tf_op jit(solution)/shard_map/pallas_call | solution.py:24
  9.2 0.0 copy-start.2
  9.2 0.6 collective-permute-start.41
  9.8 0.1 collective-permute-start.42
  9.9 5.3 %all-to-all-start = ((bf16[4,2,2,128,384]{4,3,2,1,0:T(8,128)(2,1)}), bf16[4,2,2,128,384]{4,3,2,1,0:T(8,128)(2,1)S(1)}, u32[]{:S(2)}, u32[]{:S(2)}) async-start(bf16[4,2,2,128,384]{4,3,2,1,0:T(8,128)(2,1)} %shard_map.83.refs_0_), calls=%async_computation | async-start | bytes 3145728 | tf_op jit(solution)/shard_map/all_to_all | solution.py:488
  15.2 0.0 copy-done.2
  15.2 0.6 fusion.1
  22.3 0.6 fusion.2
  22.9 1.3 %concatenate.3._.s_ref = s32[11]{0:T(128)S(1)} concatenate(s32[1]{0:T(128)} %bitcast, s32[1]{0:T(128)} %bitcast.1, s32[1]{0:T(128)} %bitcast.2, s32[1]{0:T(128)} %get-tuple-element.178, s32[1]{0:T(128)} %get-tuple-element.177, s32[2]{0:T(128)S(1)} %get-tuple-element.175, s32[1]{0:T(128)} %bitcast.6, s32[1]{0:T(128)} %bitcast.8, s32[1]{0:T(128)} %bitcast.9.core_ref, s32[1]{0:T(128)} %bitcast.10), dimensions={0} | concatenate | bytes 88 | tf_op jit(solution)/shard_map/concatenate | solution.py:451
  24.2 0.0 copy-start.1
  24.3 0.0 collective-permute-done.43.x_ref.refs_0_
  24.3 0.5 collective-permute-done.44.y_ref.refs_1_
  24.8 1.7 %shard_map.85 = (bf16[384,512]{1,0:T(8,128)(2,1)S(1)}, bf16[384,512]{1,0:T(8,128)(2,1)S(1)}) custom-call(s32[11]{0:T(128)S(1)} %concatenate.3._.s_ref, f32[1]{0:T(128)S(6)} %copy.43.__.g_ref, bf16[768,512]{1,0:T(8,128)(2,1)S(1)} %collective-permute-done.43.x_ref.refs_0_, bf16[768,512]{1,0:T(8,128)(2,1)} %collective-permute-done.44.y_ref.refs_1_, ...), custom_call_target="tpu_custom_call" | custom-call | tf_op jit(solution)/shard_map/pallas_call | solution.py:24
  26.5 1.6 %collective-permute-start.47 = (bf16[384,512]{1,0:T(8,128)(2,1)S(1)}, bf16[384,512]{1,0:T(8,128)(2,1)S(1)}, u32[]{:S(2)}, u32[]{:S(2)}) collective-permute-start(bf16[384,512]{1,0:T(8,128)(2,1)S(1)} %get-tuple-element.155.refs_2_), channel_id=1, source_target_pairs={{0,16},{8,24},{16,0},{24,8},{1,17},{9,25},{17,1},{25,9},{2,18},{10... | collective-permute-start | bytes 1179656 | tf_op jit(solution)/shard_map/ppermute | solution.py:408
  28.1 1.0 %collective-permute-start.48 = (bf16[384,512]{1,0:T(8,128)(2,1)S(1)}, bf16[384,512]{1,0:T(8,128)(2,1)S(1)}, u32[]{:S(2)}, u32[]{:S(2)}) collective-permute-start(bf16[384,512]{1,0:T(8,128)(2,1)S(1)} %get-tuple-element.162), channel_id=1, source_target_pairs={{0,8},{8,0},{16,24},{24,16},{1,9},{9,1},{17,25},{25,17},{2,10},{10... | collective-permute-start | bytes 1179656 | tf_op jit(solution)/shard_map/ppermute | solution.py:408
  29.1 0.0 collective-permute-done.40.other_ref
  29.1 0.0 copy-done.1
  29.1 3.6 %shard_map.86 = (f32[2,256,512]{2,1,0:T(8,128)S(1)}, bf16[2,256,768]{2,1,0:T(8,128)(2,1)S(1)}) custom-call(s32[11]{0:T(128)S(1)} %concatenate.3._.s_ref, bf16[2,128,3072]{2,1,0:T(8,128)(2,1)S(1)} %bitcast.22, bf16[2,128,3072]{2,1,0:T(8,128)(2,1)} %collective-permute-done.40.other_ref, bf16[768,1536]{1,0:T(8,128)(2,1)} %w_ref.7, ...), custom_call_target="tpu_custom_call" | custom-call | flops 24999999488 | tf_op jit(solution)/shard_map/pallas_call | solution.py:24
  32.7 0.0 collective-permute-done.41.x_ref.refs_0_
  32.8 0.4 collective-permute-done.42.y_ref.refs_1_
  33.2 1.6 %shard_map.87 = (bf16[384,256]{1,0:T(8,128)(2,1)S(1)}, bf16[384,256]{1,0:T(8,128)(2,1)S(1)}) custom-call(s32[11]{0:T(128)S(1)} %concatenate.3._.s_ref, f32[1]{0:T(128)S(6)} %copy.43.__.g_ref, bf16[768,256]{1,0:T(8,128)(2,1)} %collective-permute-done.41.x_ref.refs_0_, bf16[768,256]{1,0:T(8,128)(2,1)} %collective-permute-done.42.y_ref.refs_1_, ...), custom_call_target="tpu_custom_call" | custom-call | tf_op jit(solution)/shard_map/pallas_call | solution.py:24
  34.8 1.6 %collective-permute-start.45 = (bf16[384,256]{1,0:T(8,128)(2,1)S(1)}, bf16[384,256]{1,0:T(8,128)(2,1)S(1)}, u32[]{:S(2)}, u32[]{:S(2)}) collective-permute-start(bf16[384,256]{1,0:T(8,128)(2,1)S(1)} %get-tuple-element.157.refs_2_), channel_id=1, source_target_pairs={{0,16},{8,24},{16,0},{24,8},{1,17},{9,25},{17,1},{25,9},{2,18},{10... | collective-permute-start | bytes 589832 | tf_op jit(solution)/shard_map/ppermute | solution.py:408
  36.4 0.5 collective-permute-start.46
  36.9 2.9 %shard_map.88 = (f32[2,256,256]{2,1,0:T(8,128)S(1)}, bf16[2,256,768]{2,1,0:T(8,128)(2,1)S(1)}) custom-call(s32[11]{0:T(128)S(1)} %concatenate.3._.s_ref, bf16[2,128,3072]{2,1,0:T(8,128)(2,1)S(1)} %bitcast.23, bf16[2,128,3072]{2,1,0:T(8,128)(2,1)} %collective-permute-done.40.other_ref, bf16[768,1536]{1,0:T(8,128)(2,1)} %w_ref.7, ...), custom_call_target="tpu_custom_call" | custom-call | flops 24999999488 | tf_op jit(solution)/shard_map/pallas_call | solution.py:24
  39.8 1.7 %collective-permute-done.47.refs_0_ = bf16[384,512]{1,0:T(8,128)(2,1)S(1)} collective-permute-done((bf16[384,512]{1,0:T(8,128)(2,1)S(1)}, bf16[384,512]{1,0:T(8,128)(2,1)S(1)}, u32[]{:S(2)}, u32[]{:S(2)}) %collective-permute-start.47) | collective-permute-done | bytes 393248 | tf_op jit(solution)/shard_map/ppermute | solution.py:408
  41.5 0.0 collective-permute-done.48.refs_1_
  41.5 1.0 %shard_map.89 = (bf16[256,256]{1,0:T(8,128)(2,1)S(1)}, bf16[256,256]{1,0:T(8,128)(2,1)S(1)}, bf16[256,256]{1,0:T(8,128)(2,1)S(1)}, bf16[256,256]{1,0:T(8,128)(2,1)S(1)}) custom-call(s32[11]{0:T(128)S(1)} %concatenate.3._.s_ref, f32[2,256,512]{2,1,0:T(8,128)S(1)} %get-tuple-element.161.t_ref, bf16[2,256,768]{2,1,0:T(8,128)(2,1)S(1)} %get-tuple-element.156.refs_0_.far_ref, ...), custom_call_target="tpu_custom_call" | custom-call | tf_op jit(solution)/shard_map/pallas_call | solution.py:24
  42.5 2.5 %collective-permute-done.45.refs_0_ = bf16[384,256]{1,0:T(8,128)(2,1)S(1)} collective-permute-done((bf16[384,256]{1,0:T(8,128)(2,1)S(1)}, bf16[384,256]{1,0:T(8,128)(2,1)S(1)}, u32[]{:S(2)}, u32[]{:S(2)}) %collective-permute-start.45) | collective-permute-done | bytes 196640 | tf_op jit(solution)/shard_map/ppermute | solution.py:408
  45.0 0.0 collective-permute-done.46.refs_1_
  45.0 1.6 %shard_map.90 = (bf16[256,384]{1,0:T(8,128)(2,1)S(1)}, bf16[256,384]{1,0:T(8,128)(2,1)}, bf16[256,384]{1,0:T(8,128)(2,1)}, bf16[256,384]{1,0:T(8,128)(2,1)}) custom-call(s32[11]{0:T(128)S(1)} %concatenate.3._.s_ref, f32[2,256,256]{2,1,0:T(8,128)S(1)} %get-tuple-element.158.t_ref, bf16[2,256,768]{2,1,0:T(8,128)(2,1)S(1)} %get-tuple-element.159.refs_2_.far_ref, ...), custom_call_target="tpu_custom_call" | custom-call | tf_op jit(solution)/shard_map/pallas_call | solution.py:24
  46.7 5.0 %all-to-all-done.refs_0_ = bf16[4,2,2,128,384]{4,3,2,1,0:T(8,128)(2,1)S(1)} async-done(((bf16[4,2,2,128,384]{4,3,2,1,0:T(8,128)(2,1)}), bf16[4,2,2,128,384]{4,3,2,1,0:T(8,128)(2,1)S(1)}, u32[]{:S(2)}, u32[]{:S(2)}) %all-to-all-start) | async-done | bytes 1572896 | tf_op jit(solution)/shard_map/all_to_all | solution.py:488
  51.7 0.0 collective-permute-start.49
  51.7 7.1 %conditional.1 = (bf16[256,384]{1,0:T(8,128)(2,1)}, bf16[256,384]{1,0:T(8,128)(2,1)}) conditional(s32[]{:T(128)} %clamp.3, (s32[]{:T(128)}, bf16[256,384]{1,0:T(8,128)(2,1)S(1)}, bf16[256,384]{1,0:T(8,128)(2,1)}, bf16[256,384]{1,0:T(8,128)(2,1)}, bf16[256,384]{1,0:T(8,128)(2,1)}) %tuple.69, ...), branch_computations={%region_0.1_spmd, %region_1.2_spmd, %region_2.3_spmd, %region_3.4_... | conditional | flops 196609 | bytes 4325563 | solution.py:517
  51.7 1.3 %collective-permute-start.4 = (bf16[256,384]{1,0:T(8,128)(2,1)S(1)}, bf16[256,384]{1,0:T(8,128)(2,1)}, u32[]{:S(2)}, u32[]{:S(2)}) collective-permute-start(bf16[256,384]{1,0:T(8,128)(2,1)S(1)} %get-tuple-element.102), channel_id=1, source_target_pairs={{0,0},{1,4},{6,1},{7,5},{8,8},{9,12},{14,9},{15,13},{16,16},{17,20... | collective-permute-start | bytes 589832 | tf_op jit(solution)/shard_map/cond/branch_3_fun/ppermute | solution.py:418
  53.0 2.0 %collective-permute-start.5 = (bf16[256,384]{1,0:T(8,128)(2,1)}, bf16[256,384]{1,0:T(8,128)(2,1)}, u32[]{:S(2)}, u32[]{:S(2)}) collective-permute-start(bf16[256,384]{1,0:T(8,128)(2,1)} %get-tuple-element.103), channel_id=1, source_target_pairs={{0,2},{1,6},{6,3},{7,7},{8,10},{9,14},{14,11},{15,15},{16,18},{17,... | collective-permute-start | bytes 589832 | tf_op jit(solution)/shard_map/cond/branch_3_fun/ppermute | solution.py:418
  55.0 0.0 collective-permute-done.4
  55.0 3.8 %collective-permute-done.5 = bf16[256,384]{1,0:T(8,128)(2,1)} collective-permute-done((bf16[256,384]{1,0:T(8,128)(2,1)}, bf16[256,384]{1,0:T(8,128)(2,1)}, u32[]{:S(2)}, u32[]{:S(2)}) %collective-permute-start.5) | collective-permute-done | bytes 196640 | tf_op jit(solution)/shard_map/cond/branch_3_fun/ppermute | solution.py:418
  58.8 0.0 collective-permute-done.49.refs_3_
  58.8 0.0 copy-start
  58.8 3.3 %shard_map.92.refs_0_ = bf16[128,384]{1,0:T(8,128)(2,1)S(1)} custom-call(s32[11]{0:T(128)S(1)} %concatenate.3._.s_ref, f32[1]{0:T(128)S(6)} %copy.43.__.g_ref, bf16[256,384]{1,0:T(8,128)(2,1)} %get-tuple-element.171.refs_0_, bf16[256,384]{1,0:T(8,128)(2,1)} %get-tuple-element.172.refs_1_, bf16[4,2,2,128,384]{4,3,2,1,0:T(8,128)(2,1)S(1)} %shard_map.91.refs_2_, ...), custom_call_target="tpu_custom_call" | custom-call | tf_op jit(solution)/shard_map/pallas_call | solution.py:24
  62.2 2.5 %collective-permute-start.50 = (bf16[128,384]{1,0:T(8,128)(2,1)S(1)}, bf16[128,384]{1,0:T(8,128)(2,1)S(1)}, u32[]{:S(2)}, u32[]{:S(2)}) collective-permute-start(bf16[128,384]{1,0:T(8,128)(2,1)S(1)} %shard_map.92.refs_0_), channel_id=1, source_target_pairs={{0,2},{1,3},{2,0},{3,1},{4,6},{5,7},{6,4},{7,5},{8,10},{9,11},{10,... | collective-permute-start | bytes 294920 | tf_op jit(solution)/shard_map/ppermute | solution.py:412
  64.7 6.7 %collective-permute-start.51 = (bf16[128,384]{1,0:T(8,128)(2,1)S(1)}, bf16[128,384]{1,0:T(8,128)(2,1)S(1)}, u32[]{:S(2)}, u32[]{:S(2)}) collective-permute-start(bf16[128,384]{1,0:T(8,128)(2,1)S(1)} %shard_map.92.refs_0_), channel_id=1, source_target_pairs={{0,4},{1,5},{2,6},{3,7},{4,0},{5,1},{6,2},{7,3},{8,12},{9,13},{10,... | collective-permute-start | bytes 294920 | tf_op jit(solution)/shard_map/ppermute | solution.py:412
  71.4 0.0 collective-permute-start.52
  71.4 0.0 collective-permute-start.53
  71.4 0.0 collective-permute-done.50.refs_1_
  71.4 0.5 collective-permute-start.54
  71.9 6.0 %collective-permute-done.51.refs_2_ = bf16[128,384]{1,0:T(8,128)(2,1)S(1)} collective-permute-done((bf16[128,384]{1,0:T(8,128)(2,1)S(1)}, bf16[128,384]{1,0:T(8,128)(2,1)S(1)}, u32[]{:S(2)}, u32[]{:S(2)}) %collective-permute-start.51) | collective-permute-done | bytes 98336 | tf_op jit(solution)/shard_map/ppermute | solution.py:412
  77.9 0.0 collective-permute-start.55
  77.9 0.0 collective-permute-done.52.refs_3_
  77.9 0.5 collective-permute-start.56
  78.5 0.0 collective-permute-done.53.refs_4_
  78.5 0.0 collective-permute-done.54.refs_5_
  78.5 0.8 collective-permute-done.55.refs_6_
  79.2 0.2 collective-permute-done.56.refs_7_
  79.4 0.0 copy-done
  79.4 1.3 %shard_map.93 = bf16[128,1536]{1,0:T(8,128)(2,1)} custom-call(s32[11]{0:T(128)S(1)} %concatenate.3._.s_ref, bf16[128,1536]{1,0:T(8,128)(2,1)S(1)} %bitcast.20, bf16[128,384]{1,0:T(8,128)(2,1)S(1)} %shard_map.92.refs_0_, bf16[128,384]{1,0:T(8,128)(2,1)S(1)} %collective-permute-done.50.refs_1_, bf16[128,384]{1,0:T(8,128)(2,1)S(1)} %collective-permute-done.51.refs_2_, ...), custom_call_target="tpu_custom_call" | custom-call | tf_op jit(solution)/shard_map/pallas_call | solution.py:24
  (2 shorter events, 0.0 us)
Async XLA Ops:
  0.0 29.1 %collective-permute-start.40 = (bf16[2,128,3072]{2,1,0:T(8,128)(2,1)}, bf16[2,128,3072]{2,1,0:T(8,128)(2,1)}, u32[]{:S(2)}, u32[]{:S(2)}) collective-permute-start(bf16[2,128,3072]{2,1,0:T(8,128)(2,1)} %bitcast.21), channel_id=1, source_target_pairs={{0,1},{1,0},{2,3},{3,2},{4,5},{5,4},{6,7},{7,6},{8,9},{9,8},{10,11... | collective-permute-start | bytes 4718600 | tf_op jit(solution)/shard_map/ppermute | solution.py:415
  1.7 22.5 %collective-permute-start.43 = (bf16[768,512]{1,0:T(8,128)(2,1)S(1)}, bf16[768,512]{1,0:T(8,128)(2,1)S(1)}, u32[]{:S(2)}, u32[]{:S(2)}) collective-permute-start(bf16[768,512]{1,0:T(8,128)(2,1)S(1)} %shard_map.82.refs_0_), channel_id=1, source_target_pairs={{0,8},{8,0},{16,24},{24,16},{1,9},{9,1},{17,25},{25,17},{2,10},{10... | collective-permute-start | bytes 2359304 | tf_op jit(solution)/shard_map/ppermute | solution.py:408
  4.3 20.5 %collective-permute-start.44 = (bf16[768,512]{1,0:T(8,128)(2,1)S(1)}, bf16[768,512]{1,0:T(8,128)(2,1)}, u32[]{:S(2)}, u32[]{:S(2)}) collective-permute-start(bf16[768,512]{1,0:T(8,128)(2,1)S(1)} %shard_map.82.refs_0_), channel_id=1, source_target_pairs={{0,16},{8,24},{16,0},{24,8},{1,17},{9,25},{17,1},{25,9},{2,18},{10... | collective-permute-start | bytes 2359304 | tf_op jit(solution)/shard_map/ppermute | solution.py:408
  9.2 6.0 %copy-start.2 = (s32[1,2]{1,0:T(1,128)S(1)}, s32[1,2]{1,0:T(1,128)}, u32[]{:S(2)}) copy-start(s32[1,2]{1,0:T(1,128)} %param.30) | copy-start | bytes 28
  9.2 23.5 %collective-permute-start.41 = (bf16[768,256]{1,0:T(8,128)(2,1)S(1)}, bf16[768,256]{1,0:T(8,128)(2,1)}, u32[]{:S(2)}, u32[]{:S(2)}) collective-permute-start(bf16[768,256]{1,0:T(8,128)(2,1)S(1)} %shard_map.84.refs_0_), channel_id=1, source_target_pairs={{0,8},{8,0},{16,24},{24,16},{1,9},{9,1},{17,25},{25,17},{2,10},{10... | collective-permute-start | bytes 1179656 | tf_op jit(solution)/shard_map/ppermute | solution.py:408
  9.8 23.4 %collective-permute-start.42 = (bf16[768,256]{1,0:T(8,128)(2,1)S(1)}, bf16[768,256]{1,0:T(8,128)(2,1)}, u32[]{:S(2)}, u32[]{:S(2)}) collective-permute-start(bf16[768,256]{1,0:T(8,128)(2,1)S(1)} %shard_map.84.refs_0_), channel_id=1, source_target_pairs={{0,16},{8,24},{16,0},{24,8},{1,17},{9,25},{17,1},{25,9},{2,18},{10... | collective-permute-start | bytes 1179656 | tf_op jit(solution)/shard_map/ppermute | solution.py:408
  9.9 41.8 %all-to-all-start = ((bf16[4,2,2,128,384]{4,3,2,1,0:T(8,128)(2,1)}), bf16[4,2,2,128,384]{4,3,2,1,0:T(8,128)(2,1)S(1)}, u32[]{:S(2)}, u32[]{:S(2)}) async-start(bf16[4,2,2,128,384]{4,3,2,1,0:T(8,128)(2,1)} %shard_map.83.refs_0_), calls=%async_computation | async-start | bytes 3145728 | tf_op jit(solution)/shard_map/all_to_all | solution.py:488
  24.2 4.9 %copy-start.1 = (bf16[2,1,128,3072]{3,2,1,0:T(8,128)(2,1)S(1)}, bf16[2,1,128,3072]{3,2,1,0:T(8,128)(2,1)}, u32[]{:S(2)}) copy-start(bf16[2,1,128,3072]{3,2,1,0:T(8,128)(2,1)} %param.24) | copy-start | bytes 4718596
  26.5 15.0 %collective-permute-start.47 = (bf16[384,512]{1,0:T(8,128)(2,1)S(1)}, bf16[384,512]{1,0:T(8,128)(2,1)S(1)}, u32[]{:S(2)}, u32[]{:S(2)}) collective-permute-start(bf16[384,512]{1,0:T(8,128)(2,1)S(1)} %get-tuple-element.155.refs_2_), channel_id=1, source_target_pairs={{0,16},{8,24},{16,0},{24,8},{1,17},{9,25},{17,1},{25,9},{2,18},{10... | collective-permute-start | bytes 1179656 | tf_op jit(solution)/shard_map/ppermute | solution.py:408
  28.1 13.4 %collective-permute-start.48 = (bf16[384,512]{1,0:T(8,128)(2,1)S(1)}, bf16[384,512]{1,0:T(8,128)(2,1)S(1)}, u32[]{:S(2)}, u32[]{:S(2)}) collective-permute-start(bf16[384,512]{1,0:T(8,128)(2,1)S(1)} %get-tuple-element.162), channel_id=1, source_target_pairs={{0,8},{8,0},{16,24},{24,16},{1,9},{9,1},{17,25},{25,17},{2,10},{10... | collective-permute-start | bytes 1179656 | tf_op jit(solution)/shard_map/ppermute | solution.py:408
  34.8 10.2 %collective-permute-start.45 = (bf16[384,256]{1,0:T(8,128)(2,1)S(1)}, bf16[384,256]{1,0:T(8,128)(2,1)S(1)}, u32[]{:S(2)}, u32[]{:S(2)}) collective-permute-start(bf16[384,256]{1,0:T(8,128)(2,1)S(1)} %get-tuple-element.157.refs_2_), channel_id=1, source_target_pairs={{0,16},{8,24},{16,0},{24,8},{1,17},{9,25},{17,1},{25,9},{2,18},{10... | collective-permute-start | bytes 589832 | tf_op jit(solution)/shard_map/ppermute | solution.py:408
  36.4 8.7 %collective-permute-start.46 = (bf16[384,256]{1,0:T(8,128)(2,1)S(1)}, bf16[384,256]{1,0:T(8,128)(2,1)S(1)}, u32[]{:S(2)}, u32[]{:S(2)}) collective-permute-start(bf16[384,256]{1,0:T(8,128)(2,1)S(1)} %get-tuple-element.160), channel_id=1, source_target_pairs={{0,8},{8,0},{16,24},{24,16},{1,9},{9,1},{17,25},{25,17},{2,10},{10... | collective-permute-start | bytes 589832 | tf_op jit(solution)/shard_map/ppermute | solution.py:408
  51.7 7.1 %collective-permute-start.49 = (bf16[4,2,2,128,384]{4,3,2,1,0:T(8,128)(2,1)S(1)}, bf16[4,2,2,128,384]{4,3,2,1,0:T(8,128)(2,1)S(1)}, u32[]{:S(2)}, u32[]{:S(2)}) collective-permute-start(bf16[4,2,2,128,384]{4,3,2,1,0:T(8,128)(2,1)S(1)} %shard_map.91.refs_2_), channel_id=1, source_target_pairs={{0,1},{1,0},{2,3},{3,2},{4,5},{5,4},{6,7},{7,6},{8,9},{9,8},{10,11... | collective-permute-start | bytes 4718600 | tf_op jit(solution)/shard_map/ppermute | solution.py:415
  51.7 3.3 %collective-permute-start.4 = (bf16[256,384]{1,0:T(8,128)(2,1)S(1)}, bf16[256,384]{1,0:T(8,128)(2,1)}, u32[]{:S(2)}, u32[]{:S(2)}) collective-permute-start(bf16[256,384]{1,0:T(8,128)(2,1)S(1)} %get-tuple-element.102), channel_id=1, source_target_pairs={{0,0},{1,4},{6,1},{7,5},{8,8},{9,12},{14,9},{15,13},{16,16},{17,20... | collective-permute-start | bytes 589832 | tf_op jit(solution)/shard_map/cond/branch_3_fun/ppermute | solution.py:418
  53.0 5.8 %collective-permute-start.5 = (bf16[256,384]{1,0:T(8,128)(2,1)}, bf16[256,384]{1,0:T(8,128)(2,1)}, u32[]{:S(2)}, u32[]{:S(2)}) collective-permute-start(bf16[256,384]{1,0:T(8,128)(2,1)} %get-tuple-element.103), channel_id=1, source_target_pairs={{0,2},{1,6},{6,3},{7,7},{8,10},{9,14},{14,11},{15,15},{16,18},{17,... | collective-permute-start | bytes 589832 | tf_op jit(solution)/shard_map/cond/branch_3_fun/ppermute | solution.py:418
  58.8 20.6 %copy-start = (bf16[1,128,1536]{2,1,0:T(8,128)(2,1)S(1)}, bf16[1,128,1536]{2,1,0:T(8,128)(2,1)}, u32[]{:S(2)}) copy-start(bf16[1,128,1536]{2,1,0:T(8,128)(2,1)} %param.27) | copy-start | bytes 1179652
  62.2 9.2 %collective-permute-start.50 = (bf16[128,384]{1,0:T(8,128)(2,1)S(1)}, bf16[128,384]{1,0:T(8,128)(2,1)S(1)}, u32[]{:S(2)}, u32[]{:S(2)}) collective-permute-start(bf16[128,384]{1,0:T(8,128)(2,1)S(1)} %shard_map.92.refs_0_), channel_id=1, source_target_pairs={{0,2},{1,3},{2,0},{3,1},{4,6},{5,7},{6,4},{7,5},{8,10},{9,11},{10,... | collective-permute-start | bytes 294920 | tf_op jit(solution)/shard_map/ppermute | solution.py:412
  64.7 13.2 %collective-permute-start.51 = (bf16[128,384]{1,0:T(8,128)(2,1)S(1)}, bf16[128,384]{1,0:T(8,128)(2,1)S(1)}, u32[]{:S(2)}, u32[]{:S(2)}) collective-permute-start(bf16[128,384]{1,0:T(8,128)(2,1)S(1)} %shard_map.92.refs_0_), channel_id=1, source_target_pairs={{0,4},{1,5},{2,6},{3,7},{4,0},{5,1},{6,2},{7,3},{8,12},{9,13},{10,... | collective-permute-start | bytes 294920 | tf_op jit(solution)/shard_map/ppermute | solution.py:412
  71.4 6.5 %collective-permute-start.52 = (bf16[128,384]{1,0:T(8,128)(2,1)S(1)}, bf16[128,384]{1,0:T(8,128)(2,1)S(1)}, u32[]{:S(2)}, u32[]{:S(2)}) collective-permute-start(bf16[128,384]{1,0:T(8,128)(2,1)S(1)} %shard_map.92.refs_0_), channel_id=1, source_target_pairs={{0,6},{1,7},{2,4},{3,5},{4,2},{5,3},{6,0},{7,1},{8,14},{9,15},{10,... | collective-permute-start | bytes 294920 | tf_op jit(solution)/shard_map/ppermute | solution.py:412
  71.4 7.1 %collective-permute-start.53 = (bf16[128,384]{1,0:T(8,128)(2,1)S(1)}, bf16[128,384]{1,0:T(8,128)(2,1)S(1)}, u32[]{:S(2)}, u32[]{:S(2)}) collective-permute-start(bf16[128,384]{1,0:T(8,128)(2,1)S(1)} %shard_map.92.refs_0_), channel_id=1, source_target_pairs={{0,1},{1,0},{2,3},{3,2},{4,5},{5,4},{6,7},{7,6},{8,9},{9,8},{10,11... | collective-permute-start | bytes 294920 | tf_op jit(solution)/shard_map/ppermute | solution.py:415
  71.4 7.0 %collective-permute-start.54 = (bf16[128,384]{1,0:T(8,128)(2,1)S(1)}, bf16[128,384]{1,0:T(8,128)(2,1)S(1)}, u32[]{:S(2)}, u32[]{:S(2)}) collective-permute-start(bf16[128,384]{1,0:T(8,128)(2,1)S(1)} %collective-permute-done.50.refs_1_), channel_id=1, source_target_pairs={{0,1},{1,0},{2,3},{3,2},{4,5},{5,4},{6,7},{7,6},{8,9},{9,8},{10,11... | collective-permute-start | bytes 294920 | tf_op jit(solution)/shard_map/ppermute | solution.py:415
  77.9 1.3 %collective-permute-start.55 = (bf16[128,384]{1,0:T(8,128)(2,1)S(1)}, bf16[128,384]{1,0:T(8,128)(2,1)S(1)}, u32[]{:S(2)}, u32[]{:S(2)}) collective-permute-start(bf16[128,384]{1,0:T(8,128)(2,1)S(1)} %collective-permute-done.51.refs_2_), channel_id=1, source_target_pairs={{0,1},{1,0},{2,3},{3,2},{4,5},{5,4},{6,7},{7,6},{8,9},{9,8},{10,11... | collective-permute-start | bytes 294920 | tf_op jit(solution)/shard_map/ppermute | solution.py:415
  77.9 1.5 %collective-permute-start.56 = (bf16[128,384]{1,0:T(8,128)(2,1)S(1)}, bf16[128,384]{1,0:T(8,128)(2,1)S(1)}, u32[]{:S(2)}, u32[]{:S(2)}) collective-permute-start(bf16[128,384]{1,0:T(8,128)(2,1)S(1)} %collective-permute-done.52.refs_3_), channel_id=1, source_target_pairs={{0,1},{1,0},{2,3},{3,2},{4,5},{5,4},{6,7},{7,6},{8,9},{9,8},{10,11... | collective-permute-start | bytes 294920 | tf_op jit(solution)/shard_map/ppermute | solution.py:415
